TPU v7x, 32 devices: a whole 2x2x4 slice. The times are simulated.
32 devices in a mesh: tok: 4 (over y, x), wa: 8 (over z, core).
Axes of the slice: x: 2, y: 2, z: 4, core: 2. Of those that a mesh axis runs over, the one named last changes fastest.
Arguments:
- prompt_in: bfloat16 [8, 1024, 1024], P('wa', 'tok'), may hold values from -6 to 6
- cont_in: bfloat16 [8, 4, 256, 1024], P('wa', 'tok'), may hold values from -6 to 6
- first_gain: bfloat16 [2, 1024], P(None, 'wa'), may hold values from 0.25 to 1.75
- first_shift: bfloat16 [2, 1024], P(None, 'wa'), may hold values from -1.5 to 1.5
- qkv_weight: bfloat16 [2, 1024, 3072], P(None, 'wa'), may hold values from -0.1875 to 0.1875
- qv_bias: bfloat16 [2, 2048], P(None, 'wa'), may hold values from -1.5 to 1.5
- mix_weight: bfloat16 [2, 1024, 1024], P(None, 'wa'), may hold values from -2 to 2
- mix_bias: bfloat16 [2, 1024], P(None, 'wa'), may hold values from -1.5 to 1.5
- second_gain: bfloat16 [2, 1024], P(None, 'wa'), may hold values from 0.25 to 1.75
- second_shift: bfloat16 [2, 1024], P(None, 'wa'), may hold values from -1.5 to 1.5
- expand_weight: bfloat16 [2, 1024, 4096], P(None, 'wa'), may hold values from -0.1875 to 0.1875
- expand_bias: bfloat16 [2, 4096], P(None, 'wa'), may hold values from -1.5 to 1.5
- reduce_weight: bfloat16 [2, 4096, 1024], P(None, 'wa'), may hold values from -0.09375 to 0.09375
- reduce_bias: bfloat16 [2, 1024], P(None, 'wa'), may hold values from -1.5 to 1.5
- owners: int32 [8, 4], P('wa'), may hold values from 0 to 3, each once within a row
- prompt_cot: bfloat16 [8, 1024, 1024], P('wa', 'tok'), may hold values from -6 to 6
- cont_cot: bfloat16 [8, 4, 256, 1024], P('wa', 'tok'), may hold values from -6 to 6
Outputs:
- prompt_out: float32 [8, 1024, 1024], P('wa', 'tok')
- cont_out: float32 [8, 4, 256, 1024], P('wa', 'tok')
- prompt_grad: float32 [8, 1024, 1024], P('wa', 'tok')
- cont_grad: float32 [8, 4, 256, 1024], P('wa', 'tok')
- grad_first_gain: float32 [2, 1024], P(None, 'wa')
- grad_first_shift: float32 [2, 1024], P(None, 'wa')
- grad_qkv_weight: float32 [2, 1024, 3072], P(None, 'wa')
- grad_qv_bias: float32 [2, 2048], P(None, 'wa')
- grad_mix_weight: float32 [2, 1024, 1024], P(None, 'wa')
- grad_mix_bias: float32 [2, 1024], P(None, 'wa')
- grad_second_gain: float32 [2, 1024], P(None, 'wa')
- grad_second_shift: float32 [2, 1024], P(None, 'wa')
- grad_expand_weight: float32 [2, 1024, 4096], P(None, 'wa')
- grad_expand_bias: float32 [2, 4096], P(None, 'wa')
- grad_reduce_weight: float32 [2, 4096, 1024], P(None, 'wa')
- grad_reduce_bias: float32 [2, 1024], P(None, 'wa')
Inputs may be any that keep to these rules, and one draw needn't show every extreme that they name: Row w of owners is a permutation of 0 to 3: device t along tok holds block owners[w, t] of prompt w.
All inputs are finite; a program needn't handle non-finite values.
Results may differ from a plain program's by a relative error of at most 0.015.
Values may be sent and summed in bfloat16 or wider, within the bound.
No kernel may reach another device: no remote copies, remote signals or barrier semaphores. Data moves between devices by JAX's collectives and lax.ppermute only.
A program may use at most 320 MiB of HBM per device.

v0:
```python
import jax
import jax.numpy as jnp
from jax import lax
from jax.sharding import PartitionSpec as P

HEAD = 64
LAYERS = 2


epsilon = 1e-05
negative = -1e30


def normalize(stream, gain, shift):
    average = jnp.mean(stream, -1, keepdims=True)
    centred = stream - average
    variance = jnp.mean(centred * centred, -1, keepdims=True)
    return centred * lax.rsqrt(variance + epsilon) * gain + shift


def inner_rows(left, right):
    return lax.dot_general(
        left, right, (((0,), (0,)), ((), ())), preferred_element_type=jnp.float32
    )


def times_transposed(left, right):
    return lax.dot_general(
        left, right, (((1,), (1,)), ((), ())), preferred_element_type=jnp.float32
    )


def split_heads(matrix):
    return matrix.reshape(matrix.shape[0], -1, HEAD).transpose(1, 0, 2)


def merge_heads(stacked):
    return stacked.transpose(1, 0, 2).reshape(stacked.shape[1], -1)


def head_scores(head_queries, head_keys, allowed):
    scores = jnp.einsum(
        "qd,kd->qk", head_queries, head_keys, preferred_element_type=jnp.float32
    ) * HEAD ** (-0.5)
    return jnp.where(allowed, scores, negative)


def attend_forward(queries, key_rows, value_rows, allowed):

    def one_head(operands):
        head_queries, head_keys, head_values = operands
        scores = head_scores(head_queries, head_keys, allowed)
        highest = jnp.max(scores, -1, keepdims=True)
        expanded = jnp.exp(scores - highest)
        totals = jnp.sum(expanded, -1, keepdims=True)
        weights = (expanded / totals).astype(jnp.bfloat16)
        result = jnp.dot(weights, head_values, preferred_element_type=jnp.float32)
        return (result, (highest + jnp.log(totals))[:, 0])

    results, logsum = lax.map(
        one_head, (split_heads(queries), split_heads(key_rows), split_heads(value_rows))
    )
    return (merge_heads(results).astype(jnp.bfloat16), logsum)


def attend_backward(queries, key_rows, value_rows, logsum, grad_attended, allowed):

    def one_head(operands):
        head_queries, head_keys, head_values, head_logsum, head_grad = operands
        scores = head_scores(head_queries, head_keys, allowed)
        weights = jnp.exp(scores - head_logsum[:, None])
        grad_values = jnp.einsum(
            "qk,qd->kd", weights.astype(jnp.bfloat16), head_grad, preferred_element_type=jnp.float32
        )
        grad_weights = jnp.einsum(
            "qd,kd->qk", head_grad, head_values, preferred_element_type=jnp.float32
        )
        inner_sum = jnp.sum(weights * grad_weights, -1, keepdims=True)
        grad_scores = (weights * (grad_weights - inner_sum)).astype(jnp.bfloat16)
        grad_queries = jnp.einsum(
            "qk,kd->qd", grad_scores, head_keys, preferred_element_type=jnp.float32
        ) * HEAD ** (-0.5)
        grad_keys = jnp.einsum(
            "qk,qd->kd", grad_scores, head_queries, preferred_element_type=jnp.float32
        ) * HEAD ** (-0.5)
        return (grad_queries, grad_keys, grad_values)

    grad_queries, grad_keys, grad_values = lax.map(
        one_head,
        (
            split_heads(queries),
            split_heads(key_rows),
            split_heads(value_rows),
            logsum,
            split_heads(grad_attended),
        ),
    )
    return (merge_heads(grad_queries), merge_heads(grad_keys), merge_heads(grad_values))


def fetch_layer(shards, layer_index):
    (
        first_gain,
        first_shift,
        qkv_weight,
        qv_bias,
        mix_weight,
        mix_bias,
        second_gain,
        second_shift,
        expand_weight,
        expand_bias,
        reduce_weight,
        reduce_bias,
    ) = [piece[layer_index] for piece in shards]
    return (
        lax.all_gather(first_gain, "wa", axis=0, tiled=True),
        lax.all_gather(first_shift, "wa", axis=0, tiled=True),
        lax.all_gather(qkv_weight, "wa", axis=0, tiled=True),
        lax.all_gather(qv_bias, "wa", axis=0, tiled=True),
        lax.all_gather(mix_weight, "wa", axis=0, tiled=True),
        lax.all_gather(mix_bias, "wa", axis=0, tiled=True),
        lax.all_gather(second_gain, "wa", axis=0, tiled=True),
        lax.all_gather(second_shift, "wa", axis=0, tiled=True),
        lax.all_gather(expand_weight, "wa", axis=0, tiled=True),
        lax.all_gather(expand_bias, "wa", axis=0, tiled=True),
        lax.all_gather(reduce_weight, "wa", axis=0, tiled=True),
        lax.all_gather(reduce_bias, "wa", axis=0, tiled=True),
    )


def shard_layer(grads):
    (
        first_gain,
        first_shift,
        qkv_weight,
        qv_bias,
        mix_weight,
        mix_bias,
        second_gain,
        second_shift,
        expand_weight,
        expand_bias,
        reduce_weight,
        reduce_bias,
    ) = grads
    parts = (
        lax.psum_scatter(
            first_gain.astype(jnp.bfloat16), "wa", scatter_dimension=0, tiled=True
        ).astype(jnp.float32),
        lax.psum_scatter(
            first_shift.astype(jnp.bfloat16), "wa", scatter_dimension=0, tiled=True
        ).astype(jnp.float32),
        lax.psum_scatter(
            qkv_weight.astype(jnp.bfloat16), "wa", scatter_dimension=0, tiled=True
        ).astype(jnp.float32),
        lax.psum_scatter(
            qv_bias.astype(jnp.bfloat16), "wa", scatter_dimension=0, tiled=True
        ).astype(jnp.float32),
        lax.psum_scatter(
            mix_weight.astype(jnp.bfloat16), "wa", scatter_dimension=0, tiled=True
        ).astype(jnp.float32),
        lax.psum_scatter(
            mix_bias.astype(jnp.bfloat16), "wa", scatter_dimension=0, tiled=True
        ).astype(jnp.float32),
        lax.psum_scatter(
            second_gain.astype(jnp.bfloat16), "wa", scatter_dimension=0, tiled=True
        ).astype(jnp.float32),
        lax.psum_scatter(
            second_shift.astype(jnp.bfloat16), "wa", scatter_dimension=0, tiled=True
        ).astype(jnp.float32),
        lax.psum_scatter(
            expand_weight.astype(jnp.bfloat16), "wa", scatter_dimension=0, tiled=True
        ).astype(jnp.float32),
        lax.psum_scatter(
            expand_bias.astype(jnp.bfloat16), "wa", scatter_dimension=0, tiled=True
        ).astype(jnp.float32),
        lax.psum_scatter(
            reduce_weight.astype(jnp.bfloat16), "wa", scatter_dimension=0, tiled=True
        ).astype(jnp.float32),
        lax.psum_scatter(
            reduce_bias.astype(jnp.bfloat16), "wa", scatter_dimension=0, tiled=True
        ).astype(jnp.float32),
    )
    (
        first_gain,
        first_shift,
        qkv_weight,
        qv_bias,
        mix_weight,
        mix_bias,
        second_gain,
        second_shift,
        expand_weight,
        expand_bias,
        reduce_weight,
        reduce_bias,
    ) = parts
    return (
        lax.psum(first_gain.astype(jnp.bfloat16), "tok").astype(jnp.float32),
        lax.psum(first_shift.astype(jnp.bfloat16), "tok").astype(jnp.float32),
        lax.psum(qkv_weight.astype(jnp.bfloat16), "tok").astype(jnp.float32),
        lax.psum(qv_bias.astype(jnp.bfloat16), "tok").astype(jnp.float32),
        lax.psum(mix_weight.astype(jnp.bfloat16), "tok").astype(jnp.float32),
        lax.psum(mix_bias.astype(jnp.bfloat16), "tok").astype(jnp.float32),
        lax.psum(second_gain.astype(jnp.bfloat16), "tok").astype(jnp.float32),
        lax.psum(second_shift.astype(jnp.bfloat16), "tok").astype(jnp.float32),
        lax.psum(expand_weight.astype(jnp.bfloat16), "tok").astype(jnp.float32),
        lax.psum(expand_bias.astype(jnp.bfloat16), "tok").astype(jnp.float32),
        lax.psum(reduce_weight.astype(jnp.bfloat16), "tok").astype(jnp.float32),
        lax.psum(reduce_bias.astype(jnp.bfloat16), "tok").astype(jnp.float32),
    )


def layer_forward(params, stream, prompt_rows, allowed):
    (
        first_gain,
        first_shift,
        qkv_weight,
        qv_bias,
        mix_weight,
        mix_bias,
        second_gain,
        second_shift,
        expand_weight,
        expand_bias,
        reduce_weight,
        reduce_bias,
    ) = params
    width = stream.shape[1]
    normed = normalize(
        stream, first_gain.astype(jnp.float32), first_shift.astype(jnp.float32)
    ).astype(jnp.bfloat16)
    mixed = jnp.dot(normed, qkv_weight, preferred_element_type=jnp.float32)
    biases = qv_bias.astype(jnp.float32)
    queries = (mixed[:, :width] + biases[:width]).astype(jnp.bfloat16)
    key_rows = mixed[:, width : 2 * width].astype(jnp.bfloat16)
    value_rows = (mixed[:, 2 * width :] + biases[width:]).astype(jnp.bfloat16)
    prompt_keys, prompt_values = (
        lax.all_gather(key_rows[:prompt_rows], "tok", axis=0, tiled=True),
        lax.all_gather(value_rows[:prompt_rows], "tok", axis=0, tiled=True),
    )
    all_keys = jnp.concatenate([prompt_keys, key_rows[prompt_rows:]], 0)
    all_values = jnp.concatenate([prompt_values, value_rows[prompt_rows:]], 0)
    attended, logsum = attend_forward(queries, all_keys, all_values, allowed)
    middle = stream + (
        jnp.dot(attended, mix_weight, preferred_element_type=jnp.float32)
        + mix_bias.astype(jnp.float32)
    )
    second = normalize(
        middle, second_gain.astype(jnp.float32), second_shift.astype(jnp.float32)
    ).astype(jnp.bfloat16)
    hidden = jnp.dot(
        second, expand_weight, preferred_element_type=jnp.float32
    ) + expand_bias.astype(jnp.float32)
    active = jax.nn.gelu(hidden, approximate=True).astype(jnp.bfloat16)
    result = middle + (
        jnp.dot(active, reduce_weight, preferred_element_type=jnp.float32)
        + reduce_bias.astype(jnp.float32)
    )
    return (
        result,
        (
            stream,
            normed,
            queries,
            all_keys,
            all_values,
            logsum,
            attended,
            middle,
            second,
            hidden,
            active,
        ),
    )


def layer_backward(params, kept_values, grad_stream, prompt_rows, allowed):
    (
        first_gain,
        first_shift,
        qkv_weight,
        qv_bias,
        mix_weight,
        mix_bias,
        second_gain,
        second_shift,
        expand_weight,
        expand_bias,
        reduce_weight,
        reduce_bias,
    ) = params
    (
        stream,
        normed,
        queries,
        all_keys,
        all_values,
        logsum,
        attended,
        middle,
        second,
        hidden,
        active,
    ) = kept_values
    prompt_total = all_keys.shape[0] - (stream.shape[0] - prompt_rows)
    grad_branch = grad_stream.astype(jnp.bfloat16)
    grad_reduce_bias = jnp.sum(grad_branch, 0, dtype=jnp.float32)
    grad_reduce = inner_rows(active, grad_branch)
    grad_active = times_transposed(grad_branch, reduce_weight)
    unused_value, gelu_pull = jax.vjp(
        lambda entries: jax.nn.gelu(entries, approximate=True), hidden
    )
    grad_hidden = gelu_pull(grad_active)[0].astype(jnp.bfloat16)
    grad_expand_bias = jnp.sum(grad_hidden, 0, dtype=jnp.float32)
    grad_expand = inner_rows(second, grad_hidden)
    grad_second = times_transposed(grad_hidden, expand_weight)
    unused_second, second_pull = jax.vjp(
        normalize, middle, second_gain.astype(jnp.float32), second_shift.astype(jnp.float32)
    )
    grad_middle, grad_second_gain, grad_second_shift = second_pull(grad_second)
    grad_middle = grad_middle + grad_stream
    grad_mix_out = grad_middle.astype(jnp.bfloat16)
    grad_mix_bias = jnp.sum(grad_mix_out, 0, dtype=jnp.float32)
    grad_mix = inner_rows(attended, grad_mix_out)
    grad_attended = times_transposed(grad_mix_out, mix_weight).astype(jnp.bfloat16)
    grad_queries, grad_keys, grad_values = attend_backward(
        queries, all_keys, all_values, logsum, grad_attended, allowed
    )
    own_keys, own_values = (
        lax.psum_scatter(
            grad_keys[:prompt_total].astype(jnp.bfloat16), "tok", scatter_dimension=0, tiled=True
        ).astype(jnp.float32),
        lax.psum_scatter(
            grad_values[:prompt_total].astype(jnp.bfloat16), "tok", scatter_dimension=0, tiled=True
        ).astype(jnp.float32),
    )
    grad_query_rows = grad_queries.astype(jnp.bfloat16)
    grad_key_rows = jnp.concatenate([own_keys, grad_keys[prompt_total:]], 0).astype(jnp.bfloat16)
    grad_value_rows = jnp.concatenate([own_values, grad_values[prompt_total:]], 0).astype(
        jnp.bfloat16
    )
    grad_mixed = jnp.concatenate([grad_query_rows, grad_key_rows, grad_value_rows], 1)
    grad_qv_bias = jnp.concatenate(
        [
            jnp.sum(grad_query_rows, 0, dtype=jnp.float32),
            jnp.sum(grad_value_rows, 0, dtype=jnp.float32),
        ],
        0,
    )
    grad_qkv = inner_rows(normed, grad_mixed)
    grad_normed = times_transposed(grad_mixed, qkv_weight)
    unused_first, first_pull = jax.vjp(
        normalize, stream, first_gain.astype(jnp.float32), first_shift.astype(jnp.float32)
    )
    grad_input, grad_first_gain, grad_first_shift = first_pull(grad_normed)
    grad_input = grad_input + grad_middle
    grads = (
        grad_first_gain,
        grad_first_shift,
        grad_qkv,
        grad_qv_bias,
        grad_mix,
        grad_mix_bias,
        grad_second_gain,
        grad_second_shift,
        grad_expand,
        grad_expand_bias,
        grad_reduce,
        grad_reduce_bias,
    )
    return (grad_input, grads)


def local(
    prompt_in,
    cont_in,
    first_gain,
    first_shift,
    qkv_weight,
    qv_bias,
    mix_weight,
    mix_bias,
    second_gain,
    second_shift,
    expand_weight,
    expand_bias,
    reduce_weight,
    reduce_bias,
    owners,
    prompt_cot,
    cont_cot,
):
    shards = (
        first_gain,
        first_shift,
        qkv_weight,
        qv_bias,
        mix_weight,
        mix_bias,
        second_gain,
        second_shift,
        expand_weight,
        expand_bias,
        reduce_weight,
        reduce_bias,
    )
    prompt_rows = prompt_in.shape[1]
    cont_length = cont_in.shape[2]
    prompt_total = prompt_rows * lax.axis_size("tok")
    block_order = owners[0]
    own_block = lax.dynamic_index_in_dim(block_order, lax.axis_index("tok"), 0, keepdims=False)
    offsets = jnp.arange(prompt_rows, dtype=jnp.int32)
    later = prompt_total + jnp.arange(cont_length, dtype=jnp.int32)
    query_pos = jnp.concatenate([own_block * prompt_rows + offsets, later], 0)
    key_pos = jnp.concatenate(
        [(block_order[:, None] * prompt_rows + offsets[None, :]).reshape(-1), later], 0
    )
    allowed = key_pos[None, :] <= query_pos[:, None]
    stream = jnp.concatenate([prompt_in[0], cont_in[0, 0]], 0).astype(jnp.float32)
    fetched = []
    saved = []
    for layer_index in range(LAYERS):
        params = fetch_layer(shards, layer_index)
        stream, kept_values = layer_forward(params, stream, prompt_rows, allowed)
        fetched.append(params)
        saved.append(kept_values)
    grad_stream = jnp.concatenate([prompt_cot[0], cont_cot[0, 0]], 0).astype(jnp.float32)
    per_layer = [None] * LAYERS
    for layer_index in reversed(range(LAYERS)):
        params = fetch_layer(shards, layer_index)
        grad_stream, grads = layer_backward(
            params, saved[layer_index], grad_stream, prompt_rows, allowed
        )
        per_layer[layer_index] = shard_layer(grads)
    stacked = tuple(
        (
            jnp.stack([per_layer[index][member] for index in range(LAYERS)], 0)
            for member in range(12)
        )
    )
    outputs = (
        stream[:prompt_rows][None],
        stream[prompt_rows:][None, None],
        grad_stream[:prompt_rows][None],
        grad_stream[prompt_rows:][None, None],
    )
    return outputs + stacked


def solution(mesh):
    in_specs = (
        P("wa", "tok", None),
        P("wa", "tok", None, None),
        P(None, "wa"),
        P(None, "wa"),
        P(None, "wa", None),
        P(None, "wa"),
        P(None, "wa", None),
        P(None, "wa"),
        P(None, "wa"),
        P(None, "wa"),
        P(None, "wa", None),
        P(None, "wa"),
        P(None, "wa", None),
        P(None, "wa"),
        P("wa", None),
        P("wa", "tok", None),
        P("wa", "tok", None, None),
    )
    out_specs = (
        P("wa", "tok", None),
        P("wa", "tok", None, None),
        P("wa", "tok", None),
        P("wa", "tok", None, None),
        P(None, "wa"),
        P(None, "wa"),
        P(None, "wa", None),
        P(None, "wa"),
        P(None, "wa", None),
        P(None, "wa"),
        P(None, "wa"),
        P(None, "wa"),
        P(None, "wa", None),
        P(None, "wa"),
        P(None, "wa", None),
        P(None, "wa"),
    )
    return jax.shard_map(local, mesh=mesh, in_specs=in_specs, out_specs=out_specs, check_vma=False)
```

profile of v0, /device:TPU:0, one launch (start us, length us, event | category | flops | bytes accessed | tf_op | source)
XLA Modules:
  0.0 1999.3 jit_solution(3418452276314909424)
XLA Ops:
  10.1 13.4 all-gather
  32.3 11.4 all-gather.3
  44.9 33.0 %all-gather.45.cloned.1.call-done = bf16[1,1024,3072]{2,1,0:T(8,128)(2,1)} async-done(((bf16[1,128,3072]{2,1,0:T(8,128)(2,1)}), bf16[1,1024,3072]{2,1,0:T(8,128)(2,1)}) %all-gather.45.cloned.1.call-update) | async-done | bytes 6291472 | tf_op jit(solution)/shard_map/all_gather | solution.py:119
  99.5 8.9 all-gather.5
  108.4 9.8 all-gather.6
  118.2 8.9 all-gather.7
  127.2 12.7 all-gather.9
  149.3 9.8 all-gather.12
  168.0 10.1 all-gather.15
  202.9 73.5 %while.56 = (s32[]{:T(128)}, bf16[16,512,64]{1,2,0:T(8,128)(2,1)}, f32[16,512]{1,0:T(8,128)S(1)}, bf16[16,512,64]{2,1,0:T(8,128)(2,1)}, bf16[16,1280,64]{2,1,0:T...) while((s32[]{:T(128)}, bf16[16,512,64]{1,2,0:T(8,128)(2,1)}, ...), condition=%wide.region_5.6_spmd.clone, body=%wide.region_2.5_spmd.clone.sunk | while | flops 173669888 | bytes 8811625 | solution.py:60
  280.3 11.8 fusion.120
  292.1 64.3 %all-gather.51.cloned.1.call-done = bf16[1,4096,1024]{2,1,0:T(8,128)(2,1)} async-done(((bf16[1,512,1024]{2,1,0:T(8,128)(2,1)}), bf16[1,4096,1024]{2,1,0:T(8,128)(2,1)}) %all-gather.51.cloned.1.call-update) | async-done | bytes 8388624 | tf_op jit(solution)/shard_map/all_gather | solution.py:127
  356.4 10.8 fusion.213
  368.9 53.0 %all-gather.53.cloned.1.call-done = bf16[1,1024,3072]{2,1,0:T(8,128)(2,1)} async-done(((bf16[1,128,3072]{2,1,0:T(8,128)(2,1)}), bf16[1,1024,3072]{2,1,0:T(8,128)(2,1)}) %all-gather.53.cloned.1.call-update) | async-done | bytes 6291472 | tf_op jit(solution)/shard_map/all_gather | solution.py:119
  436.3 9.0 all-gather.17
  445.3 9.6 all-gather.18
  455.0 9.0 all-gather.19
  464.0 12.7 all-gather.21
  489.6 14.3 all-gather.41.cloned.1.call-done
  515.5 73.5 %while.57 = (s32[]{:T(128)}, bf16[16,512,64]{1,2,0:T(8,128)(2,1)}, f32[16,512]{1,0:T(8,128)S(1)}, bf16[16,512,64]{2,1,0:T(8,128)(2,1)}, bf16[16,1280,64]{2,1,0:T...) while((s32[]{:T(128)}, bf16[16,512,64]{1,2,0:T(8,128)(2,1)}, ...), condition=%wide.region_13.14_spmd.clone, body=%wide.region_10.13_spmd.clone.sunk | while | flops 173669888 | bytes 8811625 | solution.py:60
  593.5 24.8 %all-gather.57.cloned.1.call-done = bf16[1,1024,4096]{2,1,0:T(8,128)(2,1)} async-done(((bf16[1,128,4096]{2,1,0:T(8,128)(2,1)}), bf16[1,1024,4096]{2,1,0:T(8,128)(2,1)}) %all-gather.57.cloned.1.call-update) | async-done | bytes 8388624 | tf_op jit(solution)/shard_map/all_gather | solution.py:125
  618.2 10.5 fusion.112
  628.8 72.1 %all-gather.59.cloned.1.call-done = bf16[1,4096,1024]{2,1,0:T(8,128)(2,1)} async-done(((bf16[1,512,1024]{2,1,0:T(8,128)(2,1)}), bf16[1,4096,1024]{2,1,0:T(8,128)(2,1)}) %all-gather.59.cloned.1.call-update) | async-done | bytes 8388624 | tf_op jit(solution)/shard_map/all_gather | solution.py:127
  700.9 14.3 fusion.216
  734.1 157.8 %while.58 = (s32[]{:T(128)}, bf16[16,512,64]{1,2,0:T(8,128)(2,1)}, bf16[16,1280,64]{1,2,0:T(8,128)(2,1)}, bf16[16,1280,64]{1,2,0:T(8,128)(2,1)}, bf16[16,512,64]...) while((s32[]{:T(128)}, bf16[16,512,64]{1,2,0:T(8,128)(2,1)}, ...), condition=%wide.region_20.21_spmd.clone, body=%wide.region_18.20_spmd.clone.sunk | while | flops 426098176 | bytes 21846136 | solution.py:88
  902.8 26.2 %reduce-scatter.13.cloned.1.call-done = bf16[256,1024]{0,1:T(8,128)(2,1)} async-done(((bf16[1024,1024]{0,1:T(8,128)(2,1)}), bf16[256,1024]{0,1:T(8,128)(2,1)}) %reduce-scatter.13.cloned.1.call-update) | async-done | bytes 524304 | tf_op jit(solution)/shard_map/reduce_scatter | solution.py:332
  928.9 38.3 %reduce-scatter.15.cloned.1.call-done = bf16[256,1024]{0,1:T(8,128)(2,1)} async-done(((bf16[1024,1024]{0,1:T(8,128)(2,1)}), bf16[256,1024]{0,1:T(8,128)(2,1)}) %reduce-scatter.15.cloned.1.call-update) | async-done | bytes 524304 | tf_op jit(solution)/shard_map/reduce_scatter | solution.py:335
  967.3 9.2 multiply_reduce_fusion.4
  978.3 17.3 fusion.217
  1016.1 169.3 %while.59 = (s32[]{:T(128)}, bf16[16,512,64]{1,2,0:T(8,128)(2,1)}, bf16[16,1280,64]{1,2,0:T(8,128)(2,1)}, bf16[16,1280,64]{1,2,0:T(8,128)(2,1)}, bf16[16,512,64]...) while((s32[]{:T(128)}, bf16[16,512,64]{1,2,0:T(8,128)(2,1)}, ...), condition=%wide.region_29.30_spmd.clone, body=%wide.region_27.29_spmd.clone.sunk | while | flops 426098176 | bytes 21846136 | solution.py:88
  1200.3 11.0 convolution_convert_fusion.2
  1212.0 8.9 convolution_convert_fusion.4
  1221.6 13.2 convolution_convert_fusion
  1235.1 13.8 convolution_convert_fusion.1
  1249.6 9.2 convolution_convert_fusion.3
  1274.1 12.1 all-gather.23
  1286.2 14.0 reduce-scatter.27.cloned.1.call-done
  1300.2 36.8 %reduce-scatter.25.cloned.1.call-done = bf16[128,1024]{1,0:T(8,128)(2,1)} async-done(((bf16[1024,1024]{1,0:T(8,128)(2,1)}), bf16[128,1024]{1,0:T(8,128)(2,1)}) %reduce-scatter.25.cloned.1.call-update) | async-done | bytes 262160 | tf_op jit(solution)/shard_map/reduce_scatter | solution.py:160
  1337.0 90.6 %reduce-scatter.31.cloned.1.call-done = bf16[128,4096]{1,0:T(8,128)(2,1)} async-done(((bf16[1024,4096]{1,0:T(8,128)(2,1)}), bf16[128,4096]{1,0:T(8,128)(2,1)}) %reduce-scatter.31.cloned.1.call-update) | async-done | bytes 1048592 | tf_op jit(solution)/shard_map/reduce_scatter | solution.py:172
  1427.6 70.4 %reduce-scatter.23.cloned.1.call-done = bf16[128,3072]{1,0:T(8,128)(2,1)} async-done(((bf16[1024,3072]{1,0:T(8,128)(2,1)}), bf16[128,3072]{1,0:T(8,128)(2,1)}) %reduce-scatter.23.cloned.1.call-update) | async-done | bytes 786448 | tf_op jit(solution)/shard_map/reduce_scatter | solution.py:154
  1498.0 90.3 %reduce-scatter.35.cloned.1.call-done = bf16[512,1024]{1,0:T(8,128)(2,1)} async-done(((bf16[4096,1024]{1,0:T(8,128)(2,1)}), bf16[512,1024]{1,0:T(8,128)(2,1)}) %reduce-scatter.35.cloned.1.call-update) | async-done | bytes 1048592 | tf_op jit(solution)/shard_map/reduce_scatter | solution.py:178
  1588.3 90.3 %reduce-scatter.33.cloned.1.call-done = bf16[512,1024]{1,0:T(8,128)(2,1)} async-done(((bf16[4096,1024]{1,0:T(8,128)(2,1)}), bf16[512,1024]{1,0:T(8,128)(2,1)}) %reduce-scatter.33.cloned.1.call-update) | async-done | bytes 1048592 | tf_op jit(solution)/shard_map/reduce_scatter | solution.py:178
  1678.6 90.3 %reduce-scatter.29.cloned.1.call-done = bf16[128,4096]{1,0:T(8,128)(2,1)} async-done(((bf16[1024,4096]{1,0:T(8,128)(2,1)}), bf16[128,4096]{1,0:T(8,128)(2,1)}) %reduce-scatter.29.cloned.1.call-update) | async-done | bytes 1048592 | tf_op jit(solution)/shard_map/reduce_scatter | solution.py:172
  1768.9 70.3 %reduce-scatter.21.cloned.1.call-done = bf16[128,3072]{1,0:T(8,128)(2,1)} async-done(((bf16[1024,3072]{1,0:T(8,128)(2,1)}), bf16[128,3072]{1,0:T(8,128)(2,1)}) %reduce-scatter.21.cloned.1.call-update) | async-done | bytes 786448 | tf_op jit(solution)/shard_map/reduce_scatter | solution.py:154
  1840.8 12.6 add_add_fusion.7
  1870.2 26.4 %all-reduce.16 = (bf16[1024]{0:T(1024)(128)(2,1)S(1)}, bf16[1024]{0:T(1024)(128)(2,1)S(1)}, bf16[1024]{0:T(1024)(128)(2,1)S(1)}, bf16[1024]{0:T(1024)(128)(2,1)S...) all-reduce(bf16[1024]{0:T(1024)(128)(2,1)S(1)} %copy-done.74, ...), channel_id=31, replica_groups=mesh['tok'=4,'wa'=8] {'wa'}, use_global_device_ids=true, to_apply=%region_38.39.clone | all-reduce | flops 24576 | bytes 98304
  1897.9 16.4 all-reduce.17
  1924.1 59.3 %all-reduce.21.cloned.1.call-done = (bf16[1,128,3072]{2,1,0:T(8,128)(2,1)}, bf16[1,128,3072]{2,1,0:T(8,128)(2,1)}, bf16[1,128,1024]{2,1,0:T(8,128)(2,1)}, bf16[1...) async-done(((bf16[1,128,3072]{2,1,0:T(8,128)(2,1)}, ...) | async-done | bytes 6291472 | tf_op jit(solution)/shard_map/psum | solution.py:202
  (798 shorter events, 719.5 us)
Async XLA Ops:
  7.2 25.0 %copy-start.71 = (bf16[2,256]{1,0:T(2,128)(2,1)S(1)}, bf16[2,256]{1,0:T(2,128)(2,1)}, u32[]{:S(2)}) copy-start(bf16[2,256]{1,0:T(2,128)(2,1)} %param.30) | copy-start | bytes 3076
  7.2 36.4 %copy-start.7 = (bf16[1,256,1024]{2,1,0:T(8,128)(2,1)S(1)}, bf16[1,256,1024]{2,1,0:T(8,128)(2,1)}, u32[]{:S(2)}) copy-start(bf16[1,256,1024]{2,1,0:T(8,128)(2,1)} %param.25) | copy-start | bytes 1572868
  7.2 36.4 %copy-start.5 = (bf16[1,1,256,1024]{3,2,1,0:T(8,128)(2,1)S(1)}, bf16[1,1,256,1024]{3,2,1,0:T(8,128)(2,1)}, u32[]{:S(2)}) copy-start(bf16[1,1,256,1024]{3,2,1,0:T(8,128)(2,1)} %param.26) | copy-start | bytes 1572868
  7.2 70.6 %all-gather.45.cloned.1.call-start = ((), (), s32[]{:S(2)}) async-start(), calls=%async_computation.28 | async-start | bytes 7077888 | tf_op jit(solution)/shard_map/all_gather | solution.py:119
  10.0 170.4 %all-gather.39.cloned.1.call-start = ((), (), s32[]{:S(2)}) async-start(), calls=%async_computation.13 | async-start | bytes 2621440 | tf_op jit(solution)/shard_map/all_gather | solution.py:241
  23.5 62.4 %copy-start.36 = (f32[1,1024]{1,0:T(1,128)}, f32[1,1024]{1,0:T(1,128)S(1)}, u32[]{:S(2)}) copy-start(f32[1,1024]{1,0:T(1,128)S(1)} %convert_element_type.415) | copy-start | bytes 12292
  32.2 53.6 %copy-start.63 = (f32[1,1024]{1,0:T(1,128)}, f32[1,1024]{1,0:T(1,128)S(1)}, u32[]{:S(2)}) copy-start(f32[1,1024]{1,0:T(1,128)S(1)} %convert_element_type.416) | copy-start | bytes 12292
  43.9 42.0 %copy-start.38 = (f32[512]{0:T(512)}, f32[512]{0:T(512)S(1)}, u32[]{:S(2)}) copy-start(f32[512]{0:T(512)S(1)} %broadcast_multiply_fusion.3) | copy-start | bytes 6148
  44.8 41.0 %copy-start.48 = (f32[512]{0:T(512)}, f32[512]{0:T(512)S(1)}, u32[]{:S(2)}) copy-start(f32[512]{0:T(512)S(1)} %fusion.173) | copy-start | bytes 6148
  87.6 103.5 %all-gather.37.cloned.1.call-start = ((), (), s32[]{:S(2)}) async-start(), calls=%async_computation.12 | async-start | bytes 2621440 | tf_op jit(solution)/shard_map/all_gather | solution.py:240
  89.9 186.5 %all-gather.47.cloned.1.call-start = ((), (), s32[]{:S(2)}) async-start(), calls=%async_computation.29 | async-start | bytes 2359296 | tf_op jit(solution)/shard_map/all_gather | solution.py:121
  90.8 189.4 %all-gather.49.cloned.1.call-start = ((), (), s32[]{:S(2)}) async-start(), calls=%async_computation.30 | async-start | bytes 9437184 | tf_op jit(solution)/shard_map/all_gather | solution.py:125
  94.0 24.2 %copy-start.82 = (bf16[2,128]{1,0:T(2,128)(2,1)S(1)}, bf16[2,128]{1,0:T(2,128)(2,1)}, u32[]{:S(2)}) copy-start(bf16[2,128]{1,0:T(2,128)(2,1)} %param.34) | copy-start | bytes 1540
  94.0 33.1 %copy-start.59 = (bf16[2,512]{1,0:T(2,128)(2,1)S(1)}, bf16[2,512]{1,0:T(2,128)(2,1)}, u32[]{:S(2)}) copy-start(bf16[2,512]{1,0:T(2,128)(2,1)} %param.36) | copy-start | bytes 6148
  94.1 45.9 %copy-start.83 = (bf16[2,128]{1,0:T(2,128)(2,1)S(1)}, bf16[2,128]{1,0:T(2,128)(2,1)}, u32[]{:S(2)}) copy-start(bf16[2,128]{1,0:T(2,128)(2,1)} %param.38) | copy-start | bytes 1540
  94.1 262.3 %all-gather.51.cloned.1.call-start = ((), (), s32[]{:S(2)}) async-start(), calls=%async_computation.31 | async-start | bytes 9437184 | tf_op jit(solution)/shard_map/all_gather | solution.py:127
  97.3 324.6 %all-gather.53.cloned.1.call-start = ((), (), s32[]{:S(2)}) async-start(), calls=%async_computation.32 | async-start | bytes 7077888 | tf_op jit(solution)/shard_map/all_gather | solution.py:119
  98.1 381.0 %all-gather.43.cloned.1.call-start = ((), (), s32[]{:S(2)}) async-start(), calls=%async_computation.15 | async-start | bytes 2621440 | tf_op jit(solution)/shard_map/all_gather | solution.py:241
  118.2 162.0 %copy-start.53 = (f32[1,1024]{1,0:T(1,128)}, f32[1,1024]{1,0:T(1,128)S(1)}, u32[]{:S(2)}) copy-start(f32[1,1024]{1,0:T(1,128)S(1)} %convert_element_type.419) | copy-start | bytes 12292
  127.1 153.1 %copy-start.65 = (f32[1,1024]{1,0:T(1,128)}, f32[1,1024]{1,0:T(1,128)S(1)}, u32[]{:S(2)}) copy-start(f32[1,1024]{1,0:T(1,128)S(1)} %convert_element_type.420) | copy-start | bytes 12292
  168.0 253.9 %copy-start.67 = (f32[1,1024]{1,0:T(1,128)}, f32[1,1024]{1,0:T(1,128)S(1)}, u32[]{:S(2)}) copy-start(f32[1,1024]{1,0:T(1,128)S(1)} %convert_element_type.424) | copy-start | bytes 12292
  279.8 76.5 %copy-start = (f32[512,1024]{1,0:T(8,128)}, f32[512,1024]{1,0:T(8,128)S(1)}, u32[]{:S(2)}) copy-start(f32[512,1024]{1,0:T(8,128)S(1)} %get-tuple-element.578) | copy-start | bytes 6291460
  432.0 71.9 %all-gather.41.cloned.1.call-start = ((), (), s32[]{:S(2)}) async-start(), calls=%async_computation.14 | async-start | bytes 2621440 | tf_op jit(solution)/shard_map/all_gather | solution.py:240
  434.3 154.7 %all-gather.55.cloned.1.call-start = ((), (), s32[]{:S(2)}) async-start(), calls=%async_computation.33 | async-start | bytes 2359296 | tf_op jit(solution)/shard_map/all_gather | solution.py:121
  434.9 183.3 %all-gather.57.cloned.1.call-start = ((), (), s32[]{:S(2)}) async-start(), calls=%async_computation.34 | async-start | bytes 9437184 | tf_op jit(solution)/shard_map/all_gather | solution.py:125
  435.7 265.2 %all-gather.59.cloned.1.call-start = ((), (), s32[]{:S(2)}) async-start(), calls=%async_computation.35 | async-start | bytes 9437184 | tf_op jit(solution)/shard_map/all_gather | solution.py:127
  436.2 492.7 %reduce-scatter.13.cloned.1.call-start = ((), (), s32[]{:S(2)}) async-start(), calls=%async_computation.16 | async-start | bytes 2621440 | tf_op jit(solution)/shard_map/reduce_scatter | solution.py:332
  464.0 154.3 %copy-start.69 = (f32[1,1024]{1,0:T(1,128)}, f32[1,1024]{1,0:T(1,128)S(1)}, u32[]{:S(2)}) copy-start(f32[1,1024]{1,0:T(1,128)S(1)} %convert_element_type.428) | copy-start | bytes 12292
  476.7 224.2 %copy-start.51 = (f32[1,4096]{1,0:T(1,128)}, f32[1,4096]{1,0:T(1,128)S(1)}, u32[]{:S(2)}) copy-start(f32[1,4096]{1,0:T(1,128)S(1)} %convert_element_type.429) | copy-start | bytes 49156
  483.6 20.3 %copy-start.19 = (bf16[256,1024]{1,0:T(8,128)(2,1)S(1)}, bf16[256,1024]{1,0:T(8,128)(2,1)}, u32[]{:S(2)}) copy-start(bf16[256,1024]{1,0:T(8,128)(2,1)} %get-tuple-element.532) | copy-start | bytes 1572868
  593.1 122.1 %copy-start.11 = (f32[512,1024]{1,0:T(8,128)}, f32[512,1024]{1,0:T(8,128)S(1)}, u32[]{:S(2)}) copy-start(f32[512,1024]{1,0:T(8,128)S(1)} %get-tuple-element.584) | copy-start | bytes 6291460
  618.2 82.7 %copy-start.14 = (bf16[1,256,1024]{2,1,0:T(8,128)(2,1)S(1)}, bf16[1,256,1024]{2,1,0:T(8,128)(2,1)}, u32[]{:S(2)}) copy-start(bf16[1,256,1024]{2,1,0:T(8,128)(2,1)} %param.40) | copy-start | bytes 1572868
  618.2 82.7 %copy-start.16 = (bf16[1,1,256,1024]{3,2,1,0:T(8,128)(2,1)S(1)}, bf16[1,1,256,1024]{3,2,1,0:T(8,128)(2,1)}, u32[]{:S(2)}) copy-start(bf16[1,1,256,1024]{3,2,1,0:T(8,128)(2,1)} %param.41) | copy-start | bytes 1572868
  895.1 72.2 %reduce-scatter.15.cloned.1.call-start = ((), (), s32[]{:S(2)}) async-start(), calls=%async_computation.17 | async-start | bytes 2621440 | tf_op jit(solution)/shard_map/reduce_scatter | solution.py:335
  898.3 363.2 %reduce-scatter.19.cloned.1.call-start = ((), (), s32[]{:S(2)}) async-start(), calls=%async_computation.19 | async-start | bytes 2621440 | tf_op jit(solution)/shard_map/reduce_scatter | solution.py:335
  978.2 26.2 %copy-start.4 = (f32[512,1024]{1,0:T(8,128)}, f32[512,1024]{1,0:T(8,128)S(1)}, u32[]{:S(2)}) copy-start(f32[512,1024]{1,0:T(8,128)S(1)} %get-tuple-element.508) | copy-start | bytes 6291460
  1188.6 73.6 %reduce-scatter.17.cloned.1.call-start = ((), (), s32[]{:S(2)}) async-start(), calls=%async_computation.18 | async-start | bytes 2621440 | tf_op jit(solution)/shard_map/reduce_scatter | solution.py:332
  1191.8 108.4 %reduce-scatter.27.cloned.1.call-start = ((), (), s32[]{:S(2)}) async-start(), calls=%async_computation.23 | async-start | bytes 2359296 | tf_op jit(solution)/shard_map/reduce_scatter | solution.py:160
  1196.0 140.9 %reduce-scatter.25.cloned.1.call-start = ((), (), s32[]{:S(2)}) async-start(), calls=%async_computation.22 | async-start | bytes 2359296 | tf_op jit(solution)/shard_map/reduce_scatter | solution.py:160
  1200.3 227.3 %reduce-scatter.31.cloned.1.call-start = ((), (), s32[]{:S(2)}) async-start(), calls=%async_computation.25 | async-start | bytes 9437184 | tf_op jit(solution)/shard_map/reduce_scatter | solution.py:172
  1211.3 286.6 %reduce-scatter.23.cloned.1.call-start = ((), (), s32[]{:S(2)}) async-start(), calls=%async_computation.21 | async-start | bytes 7077888 | tf_op jit(solution)/shard_map/reduce_scatter | solution.py:154
  1221.0 367.3 %reduce-scatter.35.cloned.1.call-start = ((), (), s32[]{:S(2)}) async-start(), calls=%async_computation.27 | async-start | bytes 9437184 | tf_op jit(solution)/shard_map/reduce_scatter | solution.py:178
  1234.8 443.7 %reduce-scatter.33.cloned.1.call-start = ((), (), s32[]{:S(2)}) async-start(), calls=%async_computation.26 | async-start | bytes 9437184 | tf_op jit(solution)/shard_map/reduce_scatter | solution.py:178
  1248.9 519.9 %reduce-scatter.29.cloned.1.call-start = ((), (), s32[]{:S(2)}) async-start(), calls=%async_computation.24 | async-start | bytes 9437184 | tf_op jit(solution)/shard_map/reduce_scatter | solution.py:172
  1258.8 580.4 %reduce-scatter.21.cloned.1.call-start = ((), (), s32[]{:S(2)}) async-start(), calls=%async_computation.20 | async-start | bytes 7077888 | tf_op jit(solution)/shard_map/reduce_scatter | solution.py:154
  1270.3 713.1 %all-reduce.21.cloned.1.call-start = ((), (), s32[]{:S(2)}) async-start(), calls=%async_computation.36 | async-start | bytes 12582912 | tf_op jit(solution)/shard_map/psum | solution.py:202
  1867.9 51.1 %copy-start.3 = (f32[512,1024]{1,0:T(8,128)S(1)}, f32[512,1024]{1,0:T(8,128)}, u32[]{:S(2)}) copy-start(f32[512,1024]{1,0:T(8,128)} %copy-done.2) | copy-start | bytes 6291460
  1867.9 51.1 %copy-start.47 = (f32[512]{0:T(512)S(1)}, f32[512]{0:T(512)}, u32[]{:S(2)}) copy-start(f32[512]{0:T(512)} %copy-done.46) | copy-start | bytes 6148
  (69 other events, 384.0 us)
Sparse Core Ops, SparseCore 0:
  10.3 67.5 all-gather.44
  87.7 33.9 all-gather.38
  124.1 35.2 all-gather.36
  160.9 29.1 all-gather.46
  192.1 81.5 all-gather.48
  275.7 80.5 all-gather.50
  358.6 63.2 all-gather.52
  432.1 33.9 all-gather.42
  468.6 35.2 all-gather.40
  505.3 29.0 all-gather.54
  536.7 81.5 all-gather.56
  620.3 80.5 all-gather.58
  895.2 33.7 reduce-scatter.12
  932.0 35.1 reduce-scatter.14
  1188.7 35.1 reduce-scatter.18
  1227.0 35.1 reduce-scatter.16
  1264.4 35.7 reduce-scatter.26
  1302.4 34.5 reduce-scatter.24
  1339.2 88.3 reduce-scatter.30
  1429.8 68.1 reduce-scatter.22
  1500.3 87.9 reduce-scatter.34
  1590.6 87.9 reduce-scatter.32
  1680.9 87.9 reduce-scatter.28
  1771.0 68.1 reduce-scatter.20
  1843.6 139.7 all-reduce.20
where the time goes:
time: 2010 us; the launch traced here: 2000 us
  waiting for transfers between devices  942 us (47%)
  matrix products  640 us (32%)
  blocking collectives  207 us (10%)
  local copies, waits for them, and re-layouts  119 us (6%)
  other arithmetic  71.1 us (4%)
    reduce_scatter x2, waiting for transfers between devices, shard_layer(): lax.psum_scatter(expand_weight.astype(jnp.bfloat16), 'wa', scatter_dimens...  181 us
    reduce_scatter x2, waiting for transfers between devices, shard_layer(): lax.psum_scatter(reduce_weight.astype(jnp.bfloat16), 'wa', scatter_dimens...  181 us
    reduce_scatter x2, waiting for transfers between devices, shard_layer(): lax.psum_scatter(qkv_weight.astype(jnp.bfloat16), 'wa', scatter_dimension...  141 us
    all_gather x2, waiting for transfers between devices, fetch_layer(): lax.all_gather(reduce_weight, 'wa', axis=0, tiled=True)  136 us
    dot_general x64, matrix products, head_scores(): jnp.einsum('qd,kd->qk', head_queries, head_keys, preferred_element_type=j...  118 us
    all_gather x2, waiting for transfers between devices, fetch_layer(): lax.all_gather(qkv_weight, 'wa', axis=0, tiled=True)  86 us
    dot_general x32, matrix products, one_head(): result = jnp.dot(weights, head_values, preferred_element_type=jnp.float32)  73.7 us
    dot_general x8, matrix products, inner_rows(): lax.dot_general(left, right, (((0,), (0,)), ((), ())), preferred_element_...  72.3 us
  transfers between devices with their start and end apart: 25, of which 18 were waited for; matrix products, arithmetic and copies ran while one was open for 19% of the time, Pallas kernels for 0%

commit v1 on v0

v1 whole, which is shorter than its diff:
```python
import functools

import jax
import jax.numpy as jnp
from jax import lax
from jax.experimental import pallas as pl
from jax.experimental.pallas import tpu as pltpu
from jax.sharding import PartitionSpec as P

HEAD = 64
PAIR = 2 * HEAD
LAYERS = 2
EPSILON = 1e-05
NEGATIVE = -1e30
CURVE = 0.7978845608028654
CUBIC = 0.044715
F32 = jnp.float32
BF16 = jnp.bfloat16

V_FG, V_FS, V_QKV, V_MB, V_SG, V_SS, V_RB, V_EB = 0, 1, 2, 5, 6, 7, 8, 9


def dot(left, right):
    return jnp.dot(left, right, preferred_element_type=F32)


def dot_nt(left, right):
    return lax.dot_general(left, right, (((1,), (1,)), ((), ())), preferred_element_type=F32)


def dot_tn(left, right):
    return lax.dot_general(left, right, (((0,), (0,)), ((), ())), preferred_element_type=F32)


def params(semantics=("arbitrary",), mib=56):
    return pltpu.CompilerParams(dimension_semantics=semantics, vmem_limit_bytes=mib * 2**20)


def cost(flops, nbytes, trans=0):
    return pl.CostEstimate(flops=int(flops), bytes_accessed=int(nbytes), transcendentals=int(trans))


def center(rows):
    centred = rows - jnp.mean(rows, -1, keepdims=True)
    inverse = lax.rsqrt(jnp.mean(centred * centred, -1, keepdims=True) + EPSILON)
    return centred * inverse, inverse


def norm_pull(rows, gain, grad):
    normal, inverse = center(rows)
    inner = grad * gain
    term = inverse * (
        inner
        - jnp.mean(inner, -1, keepdims=True)
        - normal * jnp.mean(inner * normal, -1, keepdims=True)
    )
    return term, jnp.sum(grad * normal, 0, keepdims=True), jnp.sum(grad, 0, keepdims=True)


def whole(shape):
    return pl.BlockSpec(shape, lambda *_: (0,) * len(shape))


def vector(width, place):
    return pl.BlockSpec((1, width), lambda *_: (0, place))


def qkv_kernel(x_ref, gain_ref, shift_ref, bias_ref, w_ref, out_ref, normed_ref):
    @pl.when(pl.program_id(0) == 0)
    def _():
        normal, _ = center(x_ref[...])
        normed_ref[...] = (normal * gain_ref[...] + shift_ref[...]).astype(BF16)

    out_ref[...] = (dot(normed_ref[...], w_ref[...]) + bias_ref[...]).astype(BF16)


def qkv_forward(stream, vec, weights, place):
    rows, width = stream.shape
    block = 512
    steps = 3 * width // block
    return pl.pallas_call(
        qkv_kernel,
        grid=(steps,),
        in_specs=[
            whole((rows, width)),
            vector(width, V_FG),
            vector(width, V_FS),
            pl.BlockSpec((1, block), lambda j: (0, V_QKV * width // block + j)),
            pl.BlockSpec((width, block), lambda j: (0, place // block + j)),
        ],
        out_specs=[pl.BlockSpec((rows, block), lambda j: (0, j)), whole((rows, width))],
        out_shape=[
            jax.ShapeDtypeStruct((rows, 3 * width), BF16),
            jax.ShapeDtypeStruct((rows, width), BF16),
        ],
        compiler_params=params(),
        cost_estimate=cost(6 * rows * width * width, 16 * 2**20),
        name="qkv_forward",
    )(stream, vec, vec, vec, weights)


def offsets(rows):
    return lax.broadcasted_iota(jnp.int32, (rows, rows), 0) - lax.broadcasted_iota(
        jnp.int32, (rows, rows), 1
    )


def head_lanes(block, half):
    lanes = lax.broadcasted_iota(jnp.int32, block.shape, 1) // HEAD
    return jnp.where(lanes == half, block, jnp.zeros_like(block))


def attend_kernel(pb, far, *refs):
    thr_ref, q_ref, k_ref, v_ref = refs[:4]
    far_refs = refs[4 : 4 + far]
    out_ref, lse_ref = refs[4 + far :]
    steps = offsets(pb)
    keys = [k_ref[:pb, :]] + [ref[0] for ref in far_refs]
    values = [v_ref[:pb, :]] + [ref[1] for ref in far_refs]
    total = None
    for half in range(2):
        q = head_lanes(q_ref[...], half) * jnp.asarray(HEAD**-0.5, BF16)
        lefts, rights = [], []
        for j, k in enumerate(keys):
            s = dot_nt(k, q)
            lefts.append(jnp.where(steps <= thr_ref[j], s[:, :pb], NEGATIVE))
            rights.append(s[:, pb:])
        own = jnp.where(steps <= 0, dot_nt(k_ref[pb:, :], q[pb:, :]), NEGATIVE)
        top_p = jnp.max(functools.reduce(jnp.maximum, lefts), 0, keepdims=True)
        top_c = jnp.max(functools.reduce(jnp.maximum, rights + [own]), 0, keepdims=True)
        sum_p = jnp.zeros((1, pb), F32)
        own = jnp.exp(own - top_c)
        sum_c = jnp.sum(own, 0, keepdims=True)
        acc_p = jnp.zeros((PAIR, pb), F32)
        acc_c = dot_tn(head_lanes(v_ref[pb:, :], half), own.astype(BF16))
        for j, v in enumerate(values):
            v = head_lanes(v, half)
            left = jnp.exp(lefts[j] - top_p)
            right = jnp.exp(rights[j] - top_c)
            sum_p += jnp.sum(left, 0, keepdims=True)
            sum_c += jnp.sum(right, 0, keepdims=True)
            acc_p += dot_tn(v, left.astype(BF16))
            acc_c += dot_tn(v, right.astype(BF16))
        lse_ref[half, :, :] = jnp.concatenate(
            [top_p + jnp.log(sum_p), top_c + jnp.log(sum_c)], 1
        )
        part = jnp.concatenate([acc_p / sum_p, acc_c / sum_c], 1)
        total = part if total is None else total + part
    out_ref[...] = total.T.astype(BF16)


def attend_forward(thr, qkv, far, part, parts):
    rows, width = qkv.shape[0], qkv.shape[1] // 3
    pb = rows // 2
    pairs = width // PAIR // parts
    place = lambda kind: pl.BlockSpec((rows, PAIR), lambda i: (0, (kind * parts + part) * pairs + i))
    block = pl.BlockSpec((2, pb, PAIR), lambda i: (0, 0, i))
    return pl.pallas_call(
        functools.partial(attend_kernel, pb, len(far)),
        grid=(pairs,),
        in_specs=[pl.BlockSpec(memory_space=pltpu.SMEM), place(0), place(1), place(2)]
        + [block] * len(far),
        out_specs=[
            pl.BlockSpec((rows, PAIR), lambda i: (0, i)),
            pl.BlockSpec((2, 1, rows), lambda i: (i, 0, 0)),
        ],
        out_shape=[
            jax.ShapeDtypeStruct((rows, width // parts), BF16),
            jax.ShapeDtypeStruct((2 * pairs, 1, rows), F32),
        ],
        compiler_params=params(),
        cost_estimate=cost(
            48 * rows * (len(far) + 2) * pb * width // parts,
            10 * 2**20 // parts,
            rows * (len(far) + 1) * pb * 16 // parts,
        ),
        name="attend_forward",
    )(thr, qkv, qkv, qkv, *far)


def attend_pull_kernel(pb, far, *refs):
    thr_ref, q_ref, k_ref, v_ref = refs[:4]
    far_refs = refs[4 : 4 + far]
    lse_ref, do_ref, o_ref = refs[4 + far : 7 + far]
    dq_ref, dcont_ref = refs[7 + far : 9 + far]
    dfar_refs = refs[9 + far :]
    steps = offsets(pb)
    scale = HEAD**-0.5
    keys = [k_ref[:pb, :]] + [ref[0] for ref in far_refs]
    values = [v_ref[:pb, :]] + [ref[1] for ref in far_refs]
    both = (do_ref[...].astype(F32) * o_ref[...].astype(F32)).T
    dq = jnp.zeros((PAIR, 2 * pb), F32)
    dks = [jnp.zeros((pb, PAIR), F32) for _ in keys]
    dvs = [jnp.zeros((pb, PAIR), F32) for _ in keys]
    dkc = jnp.zeros((pb, PAIR), F32)
    dvc = jnp.zeros((pb, PAIR), F32)
    dqc = jnp.zeros((PAIR, pb), F32)
    for half in range(2):
        q = head_lanes(q_ref[...], half) * jnp.asarray(scale, BF16)
        do = head_lanes(do_ref[...], half)
        lse = lse_ref[half, :, :]
        delta = jnp.sum(both[half * HEAD : (half + 1) * HEAD, :], 0, keepdims=True)
        for j, (k, v) in enumerate(zip(keys, values)):
            s = dot_nt(k, q)
            left = jnp.where(steps <= thr_ref[j], s[:, :pb], NEGATIVE)
            p = jnp.exp(jnp.concatenate([left, s[:, pb:]], 1) - lse)
            dp = dot_nt(v, do)
            ds = (p * (dp - delta)).astype(BF16)
            dvs[j] += dot(p.astype(BF16), do)
            dks[j] += dot(ds, q)
            dq += dot_tn(head_lanes(k, half), ds)
        kc, vc = k_ref[pb:, :], v_ref[pb:, :]
        s = jnp.where(steps <= 0, dot_nt(kc, q[pb:, :]), NEGATIVE)
        p = jnp.exp(s - lse[:, pb:])
        dp = dot_nt(vc, do[pb:, :])
        ds = (p * (dp - delta[:, pb:])).astype(BF16)
        dvc += dot(p.astype(BF16), do[pb:, :])
        dkc += dot(ds, q[pb:, :])
        dqc += dot_tn(head_lanes(kc, half), ds)
    for ref, dk, dv in zip(dfar_refs, dks, dvs):
        ref[0] = dk.astype(BF16)
        ref[1] = dv.astype(BF16)
    dcont_ref[0] = dkc.astype(BF16)
    dcont_ref[1] = dvc.astype(BF16)
    dq = jnp.concatenate([dq[:, :pb], dq[:, pb:] + dqc], 1)
    dq_ref[...] = (dq.T * scale).astype(BF16)


def attend_backward(thr, qkv, far, lse, do, attended, part, parts):
    rows, width = qkv.shape[0], qkv.shape[1] // 3
    pb = rows // 2
    pairs = width // PAIR // parts
    place = lambda kind: pl.BlockSpec((rows, PAIR), lambda i: (0, (kind * parts + part) * pairs + i))
    block = pl.BlockSpec((2, pb, PAIR), lambda i: (0, 0, i))
    column = pl.BlockSpec((rows, PAIR), lambda i: (0, i))
    pieces = len(far) + 2
    return pl.pallas_call(
        functools.partial(attend_pull_kernel, pb, len(far)),
        grid=(pairs,),
        in_specs=[pl.BlockSpec(memory_space=pltpu.SMEM), place(0), place(1), place(2)]
        + [block] * len(far)
        + [pl.BlockSpec((2, 1, rows), lambda i: (i, 0, 0)), place(0), column],
        out_specs=[column] + [block] * pieces,
        out_shape=[jax.ShapeDtypeStruct((rows, width // parts), BF16)]
        + [jax.ShapeDtypeStruct((2, pb, width // parts), BF16)] * pieces,
        compiler_params=params(),
        cost_estimate=cost(
            80 * rows * pieces * pb * width // parts,
            18 * 2**20 // parts,
            rows * pieces * pb * 16 // parts,
        ),
        name="attend_backward",
    )(thr, qkv, qkv, qkv, *far, lse, do, attended)


def gather_slabs(target, source):
    span, width = source.shape[0], target.shape[1]
    for a in range(target.shape[0] // span):
        target[a * span : (a + 1) * span, :] = source[:, a * width : (a + 1) * width]


def feed_kernel(
    parts, x_ref, *refs
):
    att_refs = refs[:parts]
    (wm_ref, mb_ref, gain_ref, shift_ref, eb_ref, rb_ref, we_ref, wr_ref,
     out_ref, middle_ref, second_ref, hidden_ref, wr_scr) = refs[parts:]

    @pl.when(pl.program_id(0) == 0)
    def _():
        middle = x_ref[...] + mb_ref[...]
        size = att_refs[0].shape[1]
        for part, ref in enumerate(att_refs):
            middle += dot(ref[...], wm_ref[part * size : (part + 1) * size, :])
        middle_ref[...] = middle
        normal, _ = center(middle)
        second_ref[...] = (normal * gain_ref[...] + shift_ref[...]).astype(BF16)
        out_ref[...] = middle + rb_ref[...]

    gather_slabs(wr_scr, wr_ref)
    hidden = dot(second_ref[...], we_ref[...]) + eb_ref[...]
    hidden_ref[...] = hidden.astype(BF16)
    active = 0.5 * hidden * (1.0 + jnp.tanh(CURVE * (hidden + CUBIC * hidden * hidden * hidden)))
    out_ref[...] += dot(active.astype(BF16), wr_scr[...])


def feed_forward(steps, stream, attended, vec, weights):
    rows, width = stream.shape
    ff = 4 * width
    block = ff // steps
    span = width // steps
    (wr, reduce_at), (we, expand_at), (wm, mix_at) = weights
    return pl.pallas_call(
        functools.partial(feed_kernel, len(attended)),
        grid=(steps,),
        in_specs=[whole((rows, width))]
        + [whole(piece.shape) for piece in attended]
        + [
            pl.BlockSpec((width, width), lambda j: (0, mix_at // width)),
            vector(width, V_MB),
            vector(width, V_SG),
            vector(width, V_SS),
            pl.BlockSpec((1, block), lambda j: (0, V_EB * width // block + j)),
            vector(width, V_RB),
            pl.BlockSpec((width, block), lambda j: (0, expand_at // block + j)),
            pl.BlockSpec((span, ff), lambda j: (j, reduce_at // ff)),
        ],
        out_specs=[
            whole((rows, width)),
            whole((rows, width)),
            whole((rows, width)),
            pl.BlockSpec((rows, block), lambda j: (0, j)),
        ],
        out_shape=[
            jax.ShapeDtypeStruct((rows, width), F32),
            jax.ShapeDtypeStruct((rows, width), F32),
            jax.ShapeDtypeStruct((rows, width), BF16),
            jax.ShapeDtypeStruct((rows, ff), BF16),
        ],
        scratch_shapes=[pltpu.VMEM((block, width), BF16)],
        compiler_params=params(),
        cost_estimate=cost(18 * rows * width * width, 30 * 2**20, rows * ff),
        name="feed_forward",
    )(stream, *attended, wm, vec, vec, vec, vec, vec, we, wr)


def put_rows(refs, grad, core):
    if len(refs) == 1:
        refs[0][...] = grad
        return
    mine, other = refs
    planes, span, block = mine.shape
    split = grad.reshape(planes, 2, span, block)
    first = core == 0
    mine[...] = jnp.where(first, split[:, 0], split[:, 1])
    other[...] = jnp.where(first, split[:, 1], split[:, 0])


def grad_outs(steps, width, columns, block, index, apart):
    if not apart:
        return [pl.BlockSpec((width, block), lambda j: (0, index(j)))], [
            jax.ShapeDtypeStruct((width, columns), BF16)
        ]
    shape = (steps // 2, width // steps)
    spec = pl.BlockSpec(shape + (block,), lambda j: (0, 0, index(j)))
    return [spec] * 2, [jax.ShapeDtypeStruct(shape + (columns,), BF16)] * 2


def feed_pull_kernel(steps, parts, outs, core_ref, gs_ref, *refs):
    att_refs = refs[:parts]
    hidden_ref, second_ref, middle_ref, gain_ref, we_ref, wr_ref, wm_ref = refs[parts : parts + 7]
    refs = refs[parts + 7 :]
    dwe_refs, dwr_refs = refs[:outs], refs[outs : 2 * outs]
    (gm_ref, gatt_ref, deb_ref, drb_ref, dsg_ref, dss_ref, dmb_ref,
     gb_scr, sec_scr, wr_scr, acc_scr, att_scr) = refs[2 * outs :]
    step = pl.program_id(0)
    core = core_ref[0]
    width = gs_ref.shape[1]
    block = wr_scr.shape[0]

    @pl.when(step == 0)
    def _():
        branch = gs_ref[...].astype(BF16)
        gb_scr[...] = branch
        drb_ref[...] = jnp.sum(branch.astype(F32), 0, keepdims=True)
        sec_scr[...] = second_ref[...].T
        acc_scr[...] = jnp.zeros_like(acc_scr)
        size = att_refs[0].shape[1]
        for part, ref in enumerate(att_refs):
            att_scr[part * size : (part + 1) * size, :] = ref[...].T

    @pl.when(step < steps)
    def _():
        gather_slabs(wr_scr, wr_ref)
        branch = gb_scr[...]
        grad_active = dot_nt(branch, wr_scr[...])
        v = hidden_ref[...].astype(F32)
        square = v * v
        t = jnp.tanh(CURVE * v * (1.0 + CUBIC * square))
        half = 0.5 + 0.5 * t
        slope = half + 0.5 * v * (1.0 - t * t) * (CURVE * (1.0 + 3 * CUBIC * square))
        grad_hidden = (grad_active * slope).astype(BF16)
        active = (v * half).astype(BF16)
        deb_ref[...] = jnp.sum(grad_hidden.astype(F32), 0, keepdims=True)
        wr_scr[...] = dot_tn(active, branch).astype(BF16)
        span = block * width // (4 * width)

        def put_slabs(target):
            for a in range(4):
                target(slice(a * width, (a + 1) * width), wr_scr[a * span : (a + 1) * span, :])

        if outs == 1:
            def one(columns, value):
                dwr_refs[0][:, columns] = value

            put_slabs(one)
        else:
            for place, ref in enumerate(dwr_refs):
                @pl.when(step % 2 == (core if place == 0 else 1 - core))
                def _(ref=ref):
                    def one(columns, value):
                        ref[0, :, columns] = value

                    put_slabs(one)

        put_rows(dwe_refs, dot(sec_scr[...], grad_hidden).astype(BF16), core)
        acc_scr[...] += dot_nt(grad_hidden, we_ref[...])

    @pl.when(step == steps)
    def _():
        term, dgain, dshift = norm_pull(middle_ref[...], gain_ref[...], acc_scr[...])
        dsg_ref[...] = dgain
        dss_ref[...] = dshift
        grad_middle = gs_ref[...] + term
        gm_ref[...] = grad_middle
        grad_mix = grad_middle.astype(BF16)
        gb_scr[...] = grad_mix
        dmb_ref[...] = jnp.sum(grad_mix.astype(F32), 0, keepdims=True)
        gatt_ref[...] = dot_nt(grad_mix, wm_ref[...]).astype(BF16)

    @pl.when(step >= steps)
    def _():
        start = pl.multiple_of((step - steps) * block, block)
        put_rows(dwe_refs, dot(att_scr[...], gb_scr[:, pl.ds(start, block)]).astype(BF16), core)


def feed_backward(steps, core, grad_stream, hidden, second, middle, attended, vec, weights, apart):
    rows, width = grad_stream.shape
    ff = 4 * width
    block = ff // steps
    span = width // steps
    (wr, reduce_at), (we, expand_at), (wm, mix_at) = weights
    row = whole((1, width))
    small = jax.ShapeDtypeStruct((1, width), F32)
    last = lambda j: jnp.minimum(j, steps - 1)
    dwe_specs, dwe_shapes = grad_outs(steps, width, ff + width, block, lambda j: j, apart)
    if apart:
        dwr_specs = [pl.BlockSpec((1, span, ff), lambda j: (last(j) // 2, 0, 0))] * 2
        dwr_shapes = [jax.ShapeDtypeStruct((steps // 2, span, ff), BF16)] * 2
    else:
        dwr_specs = [pl.BlockSpec((span, ff), lambda j: (last(j), 0))]
        dwr_shapes = [jax.ShapeDtypeStruct((width, ff), BF16)]
    outs = len(dwe_specs)
    return pl.pallas_call(
        functools.partial(feed_pull_kernel, steps, len(attended), outs),
        grid=(steps + width // block,),
        in_specs=[pl.BlockSpec(memory_space=pltpu.SMEM), whole((rows, width))]
        + [whole(piece.shape) for piece in attended]
        + [
            pl.BlockSpec((rows, block), lambda j: (0, last(j))),
            whole((rows, width)),
            whole((rows, width)),
            vector(width, V_SG),
            pl.BlockSpec((width, block), lambda j: (0, expand_at // block + last(j))),
            pl.BlockSpec((span, ff), lambda j: (last(j), reduce_at // ff)),
            pl.BlockSpec((width, width), lambda j: (0, mix_at // width)),
        ],
        out_specs=dwe_specs
        + dwr_specs
        + [
            whole((rows, width)),
            whole((rows, width)),
            pl.BlockSpec((1, block), lambda j: (0, last(j))),
            row,
            row,
            row,
            row,
        ],
        out_shape=dwe_shapes
        + dwr_shapes
        + [
            jax.ShapeDtypeStruct((rows, width), F32),
            jax.ShapeDtypeStruct((rows, width), BF16),
            jax.ShapeDtypeStruct((1, ff), F32),
            small,
            small,
            small,
            small,
        ],
        scratch_shapes=[
            pltpu.VMEM((rows, width), BF16),
            pltpu.VMEM((width, rows), BF16),
            pltpu.VMEM((block, width), BF16),
            pltpu.VMEM((rows, width), F32),
            pltpu.VMEM((width, rows), BF16),
        ],
        compiler_params=params(),
        cost_estimate=cost(36 * rows * width * width, 50 * 2**20, rows * ff),
        name="feed_backward",
    )(core, grad_stream, *attended, hidden, second, middle, vec, we, wr, wm)


def qkv_pull_kernel(parts, sums, outs, core_ref, *refs):
    dq_refs, refs = refs[:parts], refs[parts:]
    cont_refs, refs = refs[:parts], refs[parts:]
    sum_refs, refs = refs[: parts * sums], refs[parts * sums :]
    normed_ref, x_ref, gm_ref, gain_ref, w_ref = refs[:5]
    dw_refs = refs[5 : 5 + outs]
    out_ref, dbias_ref, dgain_ref, dshift_ref, norm_scr, acc_scr, g_scr = refs[5 + outs :]
    step = pl.program_id(0)

    @pl.when(step == 0)
    def _():
        norm_scr[...] = normed_ref[...].T
        acc_scr[...] = jnp.zeros_like(acc_scr)
        for part in range(parts):
            g_scr[part] = dq_refs[part][...]
            total = sum(ref[...].astype(F32) for ref in sum_refs[part * sums : (part + 1) * sums])
            for kind in range(2):
                both = jnp.concatenate([total[kind].astype(BF16), cont_refs[part][kind]], 0)
                g_scr[(1 + kind) * parts + part] = both

    grad = g_scr[step]
    dbias_ref[...] = jnp.sum(grad.astype(F32), 0, keepdims=True)
    put_rows(dw_refs, dot(norm_scr[...], grad).astype(BF16), core_ref[0])
    acc_scr[...] += dot_nt(grad, w_ref[...])

    @pl.when(step == pl.num_programs(0) - 1)
    def _():
        term, dgain, dshift = norm_pull(x_ref[...], gain_ref[...], acc_scr[...])
        dgain_ref[...] = dgain
        dshift_ref[...] = dshift
        out_ref[...] = gm_ref[...] + term


def qkv_backward(steps, core, dqs, conts, sums, normed, stream, grad_middle, vec, weights, apart):
    rows, width = stream.shape
    parts = len(dqs)
    block = width // parts
    wq, place = weights
    small = jax.ShapeDtypeStruct((1, width), F32)
    flat = [piece for part in sums for piece in part]
    dw_specs, dw_shapes = grad_outs(steps, width, 3 * width, block, lambda j: j, apart)
    return pl.pallas_call(
        functools.partial(qkv_pull_kernel, parts, len(sums[0]), len(dw_specs)),
        grid=(3 * parts,),
        in_specs=[pl.BlockSpec(memory_space=pltpu.SMEM)]
        + [whole(piece.shape) for piece in dqs + conts + flat]
        + [
            whole((rows, width)),
            whole((rows, width)),
            whole((rows, width)),
            vector(width, V_FG),
            pl.BlockSpec((width, block), lambda j: (0, place // block + j)),
        ],
        out_specs=dw_specs
        + [
            whole((rows, width)),
            pl.BlockSpec((1, block), lambda j: (0, j)),
            whole((1, width)),
            whole((1, width)),
        ],
        out_shape=dw_shapes
        + [
            jax.ShapeDtypeStruct((rows, width), F32),
            jax.ShapeDtypeStruct((1, 3 * width), F32),
            small,
            small,
        ],
        scratch_shapes=[
            pltpu.VMEM((width, rows), BF16),
            pltpu.VMEM((rows, width), F32),
            pltpu.VMEM((3 * parts, rows, block), BF16),
        ],
        compiler_params=params(),
        cost_estimate=cost(12 * rows * width * width, 24 * 2**20),
        name="qkv_backward",
    )(core, *dqs, *conts, *flat, normed, stream, grad_middle, vec, wq)


def trade(block, axis, bits):
    return lax.ppermute(block, axis, [(i, i ^ bits) for i in range(lax.axis_size(axis))])


def pick(block, place, axis):
    return lax.dynamic_index_in_dim(block, place, axis, keepdims=False)


def added(*blocks):
    return sum(block.astype(F32) for block in blocks).astype(BF16)


def reduce_blocks(mine, other):
    planes, span, columns = mine.shape
    n_tok = lax.axis_size("tok")
    me, plane = lax.axis_index("tok"), lax.axis_index("wa") // 2
    bits = n_tok.bit_length() - 1
    got = trade(other, "wa", 1)
    cut = columns // 2
    finished = []
    for side in range(2):
        order = list(range(bits)) if side == 0 else list(reversed(range(bits)))
        shape = (planes,) + (2,) * bits + (span // n_tok, cut)
        pieces = [block[:, :, side * cut : (side + 1) * cut].reshape(shape) for block in (mine, got)]
        left = list(reversed(range(bits)))
        for bit in order:
            axis = 1 + left.index(bit)
            left.remove(bit)
            place = (me >> bit) & 1
            send = added(*[pick(piece, 1 - place, axis) for piece in pieces])
            kept = [pick(piece, place, axis) for piece in pieces]
            pieces = kept + [trade(send, "tok", 1 << bit)]
        finished.append(added(*pieces))
    block = jnp.concatenate(finished, -1)
    return added(
        pick(block, plane, 0),
        *[trade(pick(block, plane ^ step, 0), "wa", 2 * step) for step in range(1, planes)]
    )


def my_rows(shard, parts, me):
    rows = shard.shape[0] // parts
    return lax.dynamic_slice_in_dim(shard, me * rows, rows, 0)


def my_slabs(shard, parts, me):
    width = shard.shape[1]
    stacked = shard.reshape(4, shard.shape[0] // 4, width)
    rows = stacked.shape[1] // parts
    mine = lax.dynamic_slice_in_dim(stacked, me * rows, rows, 1)
    return mine.transpose(1, 0, 2).reshape(rows, 4 * width)


def local(
    prompt_in, cont_in, first_gain, first_shift, qkv_weight, qv_bias, mix_weight, mix_bias,
    second_gain, second_shift, expand_weight, expand_bias, reduce_weight, reduce_bias, owners,
    prompt_cot, cont_cot,
):
    n_tok, n_wa = lax.axis_size("tok"), lax.axis_size("wa")
    me = lax.axis_index("tok")
    core = (lax.axis_index("wa") % 2).reshape(1)
    rows = prompt_in.shape[1]
    width = prompt_in.shape[2]
    span = width // n_wa
    parts = 2
    steps = list(range(1, n_tok))
    order = owners[0]
    by_step = jnp.stack([pick(order, me ^ step, 0) for step in [0] + steps])
    thr = (by_step[0] - by_step) * rows

    small = jnp.concatenate(
        [first_gain, first_shift, qv_bias, mix_bias, second_gain, second_shift, reduce_bias, expand_bias], 1
    )
    small = lax.all_gather(small, "wa", axis=0, tiled=False)

    def spread(layer):
        def piece(start, count):
            return small[:, layer, start * span : (start + count) * span].reshape(1, -1)

        pair = piece(2, 2)
        pieces = [
            piece(0, 1), piece(1, 1), pair[:, :width], jnp.zeros((1, width), BF16), pair[:, width:],
            piece(4, 1), piece(5, 1), piece(6, 1), piece(7, 1), piece(8, 4),
        ]
        return jnp.concatenate(pieces, 1).astype(F32)

    vecs = [spread(layer) for layer in range(LAYERS)]
    both = ("wa", "tok")

    def gather(blocks):
        return lax.all_gather(jnp.concatenate(blocks, 1), both, axis=0, tiled=True)

    def piece_of(weight, layer):
        return my_rows(weight[layer], n_tok, me)

    def late(layer):
        return [my_slabs(reduce_weight[layer], n_tok, me), piece_of(expand_weight, layer)]

    first = gather([piece_of(qkv_weight, 0)])
    rest = gather(late(0) + [piece_of(mix_weight, 0)])
    after = gather(late(1) + [piece_of(qkv_weight, 1), piece_of(mix_weight, 1)])
    weights = [
        ((first, 0), ((rest, 0), (rest, 4 * width), (rest, 8 * width))),
        ((after, 8 * width), ((after, 0), (after, 4 * width), (after, 11 * width))),
    ]

    stream = jnp.concatenate([prompt_in[0], cont_in[0, 0]], 0).astype(F32)
    kept = []
    size = width // parts
    for layer in range(LAYERS):
        wq, wf = weights[layer]
        qkv, normed = qkv_forward(stream, vecs[layer], *wq)
        fars, attended, lses = [], [], []
        for part in range(parts):
            block = jnp.stack(
                [
                    qkv[:rows, kind * width + part * size : kind * width + (part + 1) * size]
                    for kind in (1, 2)
                ]
            )
            fars.append([trade(block, "tok", step) for step in steps])
        for part in range(parts):
            one, lse = attend_forward(thr, qkv, fars[part], part, parts)
            attended.append(one)
            lses.append(lse)
        result, middle, second, hidden = feed_forward(n_wa, stream, attended, vecs[layer], wf)
        kept.append((stream, normed, qkv, fars, lses, attended, middle, second, hidden))
        stream = result

    grad_stream = jnp.concatenate([prompt_cot[0], cont_cot[0, 0]], 0).astype(F32)
    totals = [None] * LAYERS
    smalls = [None] * LAYERS
    for layer in reversed(range(LAYERS)):
        wq, wf = weights[layer]
        before, normed, qkv, fars, lses, attended, middle, second, hidden = kept[layer]
        apart = layer == 0
        grads = feed_backward(
            n_wa, core, grad_stream, hidden, second, middle, attended, vecs[layer], wf, apart
        )
        outs = 2 if apart else 1
        dwe, dwr = grads[:outs], grads[outs : 2 * outs]
        grad_middle, grad_att, deb, drb, dsg, dss, dmb = grads[2 * outs :]
        dqs, conts, sums = [], [], []
        for part in range(parts):
            dq, cont, own, *far = attend_backward(
                thr, qkv, fars[part], lses[part], grad_att, attended[part], part, parts
            )
            dqs.append(dq)
            conts.append(cont)
            sums.append([own] + [trade(block, "tok", step) for step, block in zip(steps, far)])
        dwq_mine, dwq_other, grad_stream, dqb, dfg, dfs = qkv_backward(
            n_wa, core, dqs, conts, sums, normed, before, grad_middle, vecs[layer], wq, True
        )
        if apart:
            done = [reduce_blocks(*dwr), reduce_blocks(*dwe)]
        else:
            done = [
                lax.psum_scatter(block[0], "wa", scatter_dimension=0, tiled=True) for block in (dwr, dwe)
            ]
        totals[layer] = done + [reduce_blocks(dwq_mine, dwq_other)]
        dqb = jnp.concatenate([dqb[:, :width], dqb[:, 2 * width :]], 1)
        smalls[layer] = [
            piece.reshape(n_wa, -1) for piece in (dfg, dfs, dqb, dmb, dsg, dss, deb, drb)
        ]

    small = jnp.stack([jnp.concatenate(pieces, 1) for pieces in smalls], 1)
    small = lax.psum(small, both)
    small = lax.dynamic_index_in_dim(small, lax.axis_index("wa"), 0, keepdims=False)

    def vec_out(start, count):
        return small[:, start * span : (start + count) * span]

    def complete(block):
        return lax.all_gather(block, "tok", axis=0, tiled=True)

    upper = lax.psum(jnp.concatenate(totals[1][:2], 1), "tok")
    lower = complete(jnp.concatenate(totals[0][:2] + totals[1][2:], 1))
    lower_qkv = complete(totals[0][2])
    wide = 9 * width
    pairs = [(lower[:, :wide], lower_qkv), (upper, lower[:, wide:])]

    def weight_out(source, start, count):
        return jnp.stack(
            [pair[source][:, start * width : (start + count) * width] for pair in pairs], 0
        ).astype(F32)

    reduce_out = weight_out(0, 0, 4).reshape(LAYERS, span, 4, width).transpose(0, 2, 1, 3)
    return (
        stream[:rows][None],
        stream[rows:][None, None],
        grad_stream[:rows][None],
        grad_stream[rows:][None, None],
        vec_out(0, 1),
        vec_out(1, 1),
        weight_out(1, 0, 3),
        vec_out(2, 2),
        weight_out(0, 8, 1),
        vec_out(4, 1),
        vec_out(5, 1),
        vec_out(6, 1),
        weight_out(0, 4, 4),
        vec_out(7, 4),
        reduce_out.reshape(LAYERS, 4 * span, width),
        vec_out(11, 1),
    )


def solution(mesh):
    in_specs = (
        P("wa", "tok", None),
        P("wa", "tok", None, None),
        P(None, "wa"),
        P(None, "wa"),
        P(None, "wa", None),
        P(None, "wa"),
        P(None, "wa", None),
        P(None, "wa"),
        P(None, "wa"),
        P(None, "wa"),
        P(None, "wa", None),
        P(None, "wa"),
        P(None, "wa", None),
        P(None, "wa"),
        P("wa", None),
        P("wa", "tok", None),
        P("wa", "tok", None, None),
    )
    out_specs = (
        P("wa", "tok", None),
        P("wa", "tok", None, None),
        P("wa", "tok", None),
        P("wa", "tok", None, None),
        P(None, "wa"),
        P(None, "wa"),
        P(None, "wa", None),
        P(None, "wa"),
        P(None, "wa", None),
        P(None, "wa"),
        P(None, "wa"),
        P(None, "wa"),
        P(None, "wa", None),
        P(None, "wa"),
        P(None, "wa", None),
        P(None, "wa"),
    )
    return jax.shard_map(local, mesh=mesh, in_specs=in_specs, out_specs=out_specs, check_vma=False)
```

time: 2010 us -> 1270 us (0.63)
  matrix products: 640 us -> 0 us
  Pallas kernels: 0 us -> 279 us
  blocking collectives: 207 us -> 32.1 us
  waiting for transfers between devices: 942 us -> 769 us
  starting transfers between devices: 1.41 us -> 68.4 us
  local copies, waits for them, and re-layouts: 119 us -> 54.2 us
  other arithmetic: 71.1 us -> 36.6 us
    dot_general x248 -> x0, matrix products: 640 us -> none  [the longest x64 118 us: head_scores(): jnp.einsum('qd,kd->qk', head_queries, head_keys, preferred_element_type=j...]
    reduce_scatter x12 -> x2, waiting for transfers between devices: 618 us -> 115 us  [local(): lax.psum_scatter(block[0], 'wa', scatter_dimension=0, tiled=True)]
    ppermute x0 -> x56, waiting for transfers between devices: none -> 315 us  [trade(): lax.ppermute(block, axis, [(i, i ^ bits) for i in range(lax.axis_size(axi...]
    pallas_call x0 -> x16, Pallas kernels: none -> 279 us  [the longest x2 75.9 us: feed_backward(): pl.pallas_call(functools.partial(feed_pull_kernel, steps, len(attended),...]
    all_gather x16 -> x2, blocking collectives: 164 us -> 32.1 us  [the longest x1 16.5 us: complete(): return lax.all_gather(block, 'tok', axis=0, tiled=True)]
    ppermute x0 -> x56, starting transfers between devices: none -> 67.7 us  [trade(): lax.ppermute(block, axis, [(i, i ^ bits) for i in range(lax.axis_size(axi...]
    reduce_sum x55 -> x0, other arithmetic: 33.5 us -> none  [the longest x32 16.6 us: one_head(): totals = jnp.sum(expanded, -1, keepdims=True)]
    unnamed x1 -> x0, blocking collectives: 26.4 us -> none
  transfers between devices with their start and end apart: 25 -> 64, of which waited for: 18 -> 40; matrix products, arithmetic and copies ran while one was open for 19% -> 5% of each run, Pallas kernels for 0% -> 8%
where the time goes in v1:
time: 1270 us; the launch traced here: 1250 us
  waiting for transfers between devices  769 us (61%)
  Pallas kernels  279 us (22%)
  starting transfers between devices  68.4 us (5%)
  local copies, waits for them, and re-layouts  54.2 us (4%)
  other arithmetic  36.6 us (3%)
  blocking collectives  32.1 us (3%)
  between operations  15.7 us (1%)
    ppermute x56, waiting for transfers between devices, trade(): lax.ppermute(block, axis, [(i, i ^ bits) for i in range(lax.axis_size(axi...  315 us
    all_gather x3, waiting for transfers between devices, gather(): return lax.all_gather(jnp.concatenate(blocks, 1), both, axis=0, tiled=True)  241 us
    reduce_scatter x2, waiting for transfers between devices, local(): lax.psum_scatter(block[0], 'wa', scatter_dimension=0, tiled=True)  115 us
    pallas_call x2, Pallas kernels, feed_backward(): pl.pallas_call(functools.partial(feed_pull_kernel, steps, len(attended),...  75.9 us
    psum x1, waiting for transfers between devices, local(): upper = lax.psum(jnp.concatenate(totals[1][:2], 1), 'tok')  70.2 us
    ppermute x56, starting transfers between devices, trade(): lax.ppermute(block, axis, [(i, i ^ bits) for i in range(lax.axis_size(axi...  67.7 us
    pallas_call x4, Pallas kernels, attend_backward(): pl.pallas_call(functools.partial(attend_pull_kernel, pb, len(far)), grid=...  66.1 us
    pallas_call x4, Pallas kernels, attend_forward(): pl.pallas_call(functools.partial(attend_kernel, pb, len(far)), grid=(pair...  43.7 us
  transfers between devices with their start and end apart: 64, of which 40 were waited for; matrix products, arithmetic and copies ran while one was open for 5% of the time, Pallas kernels for 8%

profile of v1, /device:TPU:0, one launch (start us, length us, event | category | flops | bytes accessed | tf_op | source)
XLA Modules:
  0.0 1254.7 jit_solution(3950871528888049609)
XLA Ops:
  16.2 15.7 %all-gather.2 = bf16[8,2,1536]{2,1,0:T(2,128)(2,1)S(1)} all-gather(bf16[1,2,1536]{2,1,0:T(2,128)(2,1)S(1)} %bitcast.430), channel_id=2, replica_groups=mesh['tok'=4,'wa'=8] {'wa'}, dimensions={0}, use_global_device_ids=true | all-gather | bytes 55296 | tf_op jit(solution)/shard_map/all_gather | solution.py:644
  34.4 49.5 %all-gather.14.cloned.1.call-done = bf16[1,1024,3072]{2,1,0:T(8,128)(2,1)} async-done(((bf16[1,32,3072]{2,1,0:T(8,128)(2,1)}), bf16[1,1024,3072]{2,1,0:T(8,128)(2,1)}) %all-gather.14.cloned.1.call-update) | async-done | bytes 6291472 | tf_op jit(solution)/shard_map/all_gather | solution.py:661
  83.9 9.3 qkv_forward.2
  105.4 7.5 collective-permute-done.refs_4_
  114.3 13.5 %collective-permute-done.2.refs_6_ = bf16[2,256,512]{2,1,0:T(8,128)(2,1)S(1)} collective-permute-done((bf16[2,256,512]{2,1,0:T(8,128)(2,1)S(1)}, bf16[2,256,512]{2,1,0:T(8,128)(2,1)S(1)}, u32[]{:S(2)}, u32[]{:S(2)}) %collective-permute-start.2) | collective-permute-done | bytes 524320 | tf_op jit(solution)/shard_map/ppermute | solution.py:572
  128.6 10.9 attend_forward.4
  139.5 9.9 collective-permute-done.3.refs_4_
  149.4 14.8 %collective-permute-done.5.refs_6_ = bf16[2,256,512]{2,1,0:T(8,128)(2,1)S(1)} collective-permute-done((bf16[2,256,512]{2,1,0:T(8,128)(2,1)S(1)}, bf16[2,256,512]{2,1,0:T(8,128)(2,1)S(1)}, u32[]{:S(2)}, u32[]{:S(2)}) %collective-permute-start.5) | collective-permute-done | bytes 524320 | tf_op jit(solution)/shard_map/ppermute | solution.py:572
  165.0 10.9 attend_forward.5
  175.9 54.5 %all-gather.8.cloned.1.call-done.refs_2_.refs_8_.refs_9_.refs_6_.refs_7_ = bf16[1024,9216]{1,0:T(8,128)(2,1)} async-done(((bf16[32,9216]{1,0:T(8,128)(2,1)}), bf16[1024,9216]{1,0:T(8,128)(2,1)}) %all-gather.8.cloned.1.call-update) | async-done | bytes 18874384 | tf_op jit(solution)/shard_map/all_gather | solution.py:661
  230.4 19.4 %feed_forward.2 = (f32[512,1024]{1,0:T(8,128)}, f32[512,1024]{1,0:T(8,128)}, bf16[512,1024]{1,0:T(8,128)(2,1)}, bf16[512,4096]{1,0:T(8,128)(2,1)}) custom-call(f32[512,1024]{1,0:T(8,128)} %maximum_convert_fusion.2.x_ref.refs_13_, bf16[512,512]{1,0:T(8,128)(2,1)} %get-tuple-element.93.refs_0_.refs_9_, bf16[512,512]{1,0:T(8,128)(2,1)} %get-tuple-element.94.refs_1_.refs_9_, ...), custom_call_target="tpu_custom_call" | custom-call | flops 9663676416 | bytes 31457280 | tf_op jit(solution)/shard_map/feed_forward/pallas_call | solution.py:293
  249.8 137.0 %all-gather.10.cloned.1.call-done.w_ref.refs_2_.refs_8_.refs_9_.refs_6_.refs_7_.refs_16_ = bf16[1024,12288]{1,0:T(8,128)(2,1)} async-done(((bf16[32,12288]{1,0:T(8,128)(2,1)}), bf16[1024,12288]{1,0:T(8,128)(2,1)}) %all-gather.10.cloned.1.call-update) | async-done | bytes 25165840 | tf_op jit(solution)/shard_map/all_gather | solution.py:661
  386.8 9.3 qkv_forward.3
  404.9 7.5 collective-permute-done.6.refs_4_
  413.9 11.2 collective-permute-done.7.refs_5_
  425.9 11.0 attend_forward.6
  437.0 9.6 collective-permute-done.10.refs_5_
  448.2 10.9 attend_forward.7
  459.1 19.1 %feed_forward.3 = (f32[512,1024]{1,0:T(8,128)}, f32[512,1024]{1,0:T(8,128)}, bf16[512,1024]{1,0:T(8,128)(2,1)}, bf16[512,4096]{1,0:T(8,128)(2,1)}) custom-call(f32[512,1024]{1,0:T(8,128)} %get-tuple-element.95.x_ref.refs_13_, bf16[512,512]{1,0:T(8,128)(2,1)} %get-tuple-element.97.refs_0_.refs_9_, bf16[512,512]{1,0:T(8,128)(2,1)} %get-tuple-element.98.refs_1_.refs_9_, ...), custom_call_target="tpu_custom_call" | custom-call | flops 9663676416 | bytes 31457280 | tf_op jit(solution)/shard_map/feed_forward/pallas_call | solution.py:293
  478.2 36.8 %feed_backward.2 = (bf16[1024,5120]{1,0:T(8,128)(2,1)}, bf16[1024,4096]{1,0:T(8,128)(2,1)}, f32[512,1024]{1,0:T(8,128)}, bf16[512,1024]{1,0:T(8,128)(2,1)}, f32[...) custom-call(s32[1]{0:T(128)} %bitcast.44.core_ref, ...), custom_call_target="tpu_custom_call" | custom-call | flops 19327352832 | bytes 52428800 | tf_op jit(solution)/shard_map/feed_backward/pallas_call | solution.py:444
  515.0 16.3 %attend_backward.4 = (bf16[512,512]{1,0:T(8,128)(2,1)}, bf16[2,256,512]{2,1,0:T(8,128)(2,1)}, bf16[2,256,512]{2,1,0:T(8,128)(2,1)}, bf16[2,256,512]{2,1,0:T(8,12...) custom-call(s32[4]{0:T(128)} %fusion.76.refs_0_, ...), custom_call_target="tpu_custom_call" | custom-call | flops 26843545600 | bytes 9437184 | tf_op jit(solution)/shard_map/attend_backward/pallas_call | solution.py:237
  534.9 16.6 %attend_backward.5 = (bf16[512,512]{1,0:T(8,128)(2,1)}, bf16[2,256,512]{2,1,0:T(8,128)(2,1)}, bf16[2,256,512]{2,1,0:T(8,128)(2,1)}, bf16[2,256,512]{2,1,0:T(8,12...) custom-call(s32[4]{0:T(128)} %fusion.76.refs_0_, ...), custom_call_target="tpu_custom_call" | custom-call | flops 26843545600 | bytes 9437184 | tf_op jit(solution)/shard_map/attend_backward/pallas_call | solution.py:237
  557.8 11.2 collective-permute-done.15.refs_9_
  569.0 9.0 collective-permute-done.16.refs_10_
  579.0 17.9 %qkv_backward.2 = (bf16[4,128,3072]{2,1,0:T(8,128)(2,1)}, bf16[4,128,3072]{2,1,0:T(8,128)(2,1)}, f32[512,1024]{1,0:T(8,128)}, f32[1,3072]{1,0:T(1,128)}, f32[1,1024]{1,0:T(1,128)}, /*index=5*/f32[1,1024]{1,0:T(1,128)}) custom-call(s32[1]{0:T(128)} %bitcast.44.core_ref, bf16[512,512]{1,0:T(8,128)(2,1)} %get-tuple-element.106.refs_0_, ...), custom_call_target="tpu_custom_call" | custom-call | flops 6442450944 | bytes 25165824 | tf_op jit(solution)/shard_map/qkv_backward/pallas_call | solution.py:534
  596.9 39.1 %feed_backward.3 = (bf16[4,128,5120]{2,1,0:T(8,128)(2,1)}, bf16[4,128,5120]{2,1,0:T(8,128)(2,1)}, bf16[4,128,4096]{2,1,0:T(8,128)(2,1)}, bf16[4,128,4096]{2,1,0:...) custom-call(s32[1]{0:T(128)} %bitcast.44.core_ref, ...), custom_call_target="tpu_custom_call" | custom-call | flops 19327352832 | bytes 52428800 | tf_op jit(solution)/shard_map/feed_backward/pallas_call | solution.py:444
  636.1 16.3 %attend_backward.6 = (bf16[512,512]{1,0:T(8,128)(2,1)}, bf16[2,256,512]{2,1,0:T(8,128)(2,1)}, bf16[2,256,512]{2,1,0:T(8,128)(2,1)}, bf16[2,256,512]{2,1,0:T(8,12...) custom-call(s32[4]{0:T(128)} %fusion.76.refs_0_, ...), custom_call_target="tpu_custom_call" | custom-call | flops 26843545600 | bytes 9437184 | tf_op jit(solution)/shard_map/attend_backward/pallas_call | solution.py:237
  656.0 16.8 %attend_backward.7 = (bf16[512,512]{1,0:T(8,128)(2,1)}, bf16[2,256,512]{2,1,0:T(8,128)(2,1)}, bf16[2,256,512]{2,1,0:T(8,128)(2,1)}, bf16[2,256,512]{2,1,0:T(8,12...) custom-call(s32[4]{0:T(128)} %fusion.76.refs_0_, ...), custom_call_target="tpu_custom_call" | custom-call | flops 26843545600 | bytes 9437184 | tf_op jit(solution)/shard_map/attend_backward/pallas_call | solution.py:237
  678.7 10.3 collective-permute-done.21.refs_9_
  689.0 9.5 collective-permute-done.22.refs_10_
  699.5 17.9 %qkv_backward.3 = (bf16[4,128,3072]{2,1,0:T(8,128)(2,1)}, bf16[4,128,3072]{2,1,0:T(8,128)(2,1)}, f32[512,1024]{1,0:T(8,128)}, f32[1,3072]{1,0:T(1,128)}, f32[1,1024]{1,0:T(1,128)}, /*index=5*/f32[1,1024]{1,0:T(1,128)}) custom-call(s32[1]{0:T(128)} %bitcast.44.core_ref, bf16[512,512]{1,0:T(8,128)(2,1)} %get-tuple-element.126.refs_0_, ...), custom_call_target="tpu_custom_call" | custom-call | flops 6442450944 | bytes 25165824 | tf_op jit(solution)/shard_map/qkv_backward/pallas_call | solution.py:534
  733.8 12.0 collective-permute-done.24
  762.5 15.2 %collective-permute-done.52 = bf16[4,32,1536]{2,1,0:T(8,128)(2,1)S(1)} collective-permute-done((bf16[4,32,1536]{2,1,0:T(8,128)(2,1)S(1)}, bf16[4,32,1536]{2,1,0:T(8,128)(2,1)S(1)}, u32[]{:S(2)}, u32[]{:S(2)}) %collective-permute-start.52) | collective-permute-done | bytes 393248 | tf_op jit(solution)/shard_map/ppermute | solution.py:572
  788.3 8.4 collective-permute-done.54
  802.4 11.5 collective-permute-done.33
  815.0 8.0 collective-permute-done.35
  826.2 8.0 collective-permute-done.34
  834.5 14.7 %collective-permute-done.36 = bf16[4,32,2048]{2,1,0:T(8,128)(2,1)S(1)} collective-permute-done((bf16[4,32,2048]{2,1,0:T(8,128)(2,1)S(1)}, bf16[4,32,2048]{2,1,0:T(8,128)(2,1)S(1)}, u32[]{:S(2)}, u32[]{:S(2)}) %collective-permute-start.36) | collective-permute-done | bytes 524320 | tf_op jit(solution)/shard_map/ppermute | solution.py:572
  864.3 9.9 collective-permute-done.42
  875.3 13.2 %collective-permute-done.44 = bf16[4,32,2560]{2,1,0:T(8,128)(2,1)S(1)} collective-permute-done((bf16[4,32,2560]{2,1,0:T(8,128)(2,1)S(1)}, bf16[4,32,2560]{2,1,0:T(8,128)(2,1)S(1)}, u32[]{:S(2)}, u32[]{:S(2)}) %collective-permute-start.44) | collective-permute-done | bytes 655392 | tf_op jit(solution)/shard_map/ppermute | solution.py:572
  895.5 9.2 collective-permute-done.47
  904.7 38.1 %collective-permute-done.46 = bf16[32,5120]{1,0:T(8,128)(2,1)S(1)} collective-permute-done((bf16[32,5120]{1,0:T(8,128)(2,1)S(1)}, bf16[32,5120]{1,0:T(8,128)(2,1)S(1)}, u32[]{:S(2)}, u32[]{:S(2)}) %collective-permute-start.46) | collective-permute-done | bytes 327712 | tf_op jit(solution)/shard_map/ppermute | solution.py:572
  954.8 11.3 collective-permute-done.27
  984.1 10.4 collective-permute-done.30
  994.7 115.1 %reduce-scatter.5.cloned.1.call-done = bf16[128,5120]{1,0:T(8,128)(2,1)} async-done(((bf16[1024,5120]{1,0:T(8,128)(2,1)}), bf16[128,5120]{1,0:T(8,128)(2,1)}) %reduce-scatter.5.cloned.1.call-update) | async-done | bytes 1310736 | tf_op jit(solution)/shard_map/reduce_scatter | solution.py:728
  1113.0 16.5 %all_gather.26 = bf16[128,3072]{1,0:T(8,128)(2,1)S(1)} all-gather(bf16[32,3072]{1,0:T(8,128)(2,1)S(1)} %fusion.43), channel_id=1, replica_groups=mesh['tok'=4,'wa'=8] {'tok'}, dimensions={0}, use_global_device_ids=true | all-gather | bytes 983040 | tf_op jit(solution)/shard_map/all_gather | solution.py:744
  1129.5 26.6 %all-gather.12.cloned.1.call-done = bf16[128,12288]{1,0:T(8,128)(2,1)} async-done(((bf16[32,12288]{1,0:T(8,128)(2,1)}), bf16[128,12288]{1,0:T(8,128)(2,1)}) %all-gather.12.cloned.1.call-update) | async-done | bytes 3145744 | tf_op jit(solution)/shard_map/all_gather | solution.py:744
  1163.7 70.2 %all-reduce.5.cloned.1.call-done = bf16[128,9216]{1,0:T(8,128)(2,1)} async-done(((bf16[128,9216]{1,0:T(8,128)(2,1)}), bf16[128,9216]{1,0:T(8,128)(2,1)}) %all-reduce.5.cloned.1.call-update) | async-done | bytes 2359312 | tf_op jit(solution)/shard_map/psum | solution.py:746
  (375 shorter events, 191.3 us)
Async XLA Ops:
  7.2 76.7 %all-gather.14.cloned.1.call-start = ((), (), s32[]{:S(2)}) async-start(), calls=%async_computation.9 | async-start | bytes 6488064 | tf_op jit(solution)/shard_map/all_gather | solution.py:661
  10.4 220.0 %all-gather.8.cloned.1.call-start = ((), (), s32[]{:S(2)}) async-start(), calls=%async_computation.2 | async-start | bytes 19464192 | tf_op jit(solution)/shard_map/all_gather | solution.py:661
  13.4 373.4 %all-gather.10.cloned.1.call-start = ((), (), s32[]{:S(2)}) async-start(), calls=%async_computation.3 | async-start | bytes 25952256 | tf_op jit(solution)/shard_map/all_gather | solution.py:661
  15.9 936.7 %all-reduce.3.cloned.1.call-start = ((), (), s32[]{:S(2)}) async-start(), calls=%async_computation.4 | async-start | bytes 196608 | tf_op jit(solution)/shard_map/psum | solution.py:737
  96.6 31.2 %collective-permute-start.2 = (bf16[2,256,512]{2,1,0:T(8,128)(2,1)S(1)}, bf16[2,256,512]{2,1,0:T(8,128)(2,1)S(1)}, u32[]{:S(2)}, u32[]{:S(2)}) collective-permute-start(bf16[2,256,512]{2,1,0:T(8,128)(2,1)S(1)} %pad_maximum_fusion.4), channel_id=1, source_target_pairs={{0,24},{8,16},{16,8},{24,0},{1,25},{9,17},{17,9},{25,1},{2,26},{10... | collective-permute-start | bytes 1572872 | tf_op jit(solution)/shard_map/ppermute | solution.py:572
  103.4 46.0 %collective-permute-start.3 = (bf16[2,256,512]{2,1,0:T(8,128)(2,1)S(1)}, bf16[2,256,512]{2,1,0:T(8,128)(2,1)S(1)}, u32[]{:S(2)}, u32[]{:S(2)}) collective-permute-start(bf16[2,256,512]{2,1,0:T(8,128)(2,1)S(1)} %pad_maximum_fusion.5), channel_id=1, source_target_pairs={{0,8},{8,0},{16,24},{24,16},{1,9},{9,1},{17,25},{25,17},{2,10},{10... | collective-permute-start | bytes 1572872 | tf_op jit(solution)/shard_map/ppermute | solution.py:572
  104.9 44.5 %collective-permute-start.4 = (bf16[2,256,512]{2,1,0:T(8,128)(2,1)S(1)}, bf16[2,256,512]{2,1,0:T(8,128)(2,1)S(1)}, u32[]{:S(2)}, u32[]{:S(2)}) collective-permute-start(bf16[2,256,512]{2,1,0:T(8,128)(2,1)S(1)} %pad_maximum_fusion.5), channel_id=1, source_target_pairs={{0,16},{8,24},{16,0},{24,8},{1,17},{9,25},{17,1},{25,9},{2,18},{10... | collective-permute-start | bytes 1572872 | tf_op jit(solution)/shard_map/ppermute | solution.py:572
  112.8 51.4 %collective-permute-start.5 = (bf16[2,256,512]{2,1,0:T(8,128)(2,1)S(1)}, bf16[2,256,512]{2,1,0:T(8,128)(2,1)S(1)}, u32[]{:S(2)}, u32[]{:S(2)}) collective-permute-start(bf16[2,256,512]{2,1,0:T(8,128)(2,1)S(1)} %pad_maximum_fusion.5), channel_id=1, source_target_pairs={{0,24},{8,16},{16,8},{24,0},{1,25},{9,17},{17,9},{25,1},{2,26},{10... | collective-permute-start | bytes 1572872 | tf_op jit(solution)/shard_map/ppermute | solution.py:572
  399.1 26.0 %collective-permute-start.7 = (bf16[2,256,512]{2,1,0:T(8,128)(2,1)S(1)}, bf16[2,256,512]{2,1,0:T(8,128)(2,1)S(1)}, u32[]{:S(2)}, u32[]{:S(2)}) collective-permute-start(bf16[2,256,512]{2,1,0:T(8,128)(2,1)S(1)} %pad_maximum_fusion.6), channel_id=1, source_target_pairs={{0,16},{8,24},{16,0},{24,8},{1,17},{9,25},{17,1},{25,9},{2,18},{10... | collective-permute-start | bytes 1572872 | tf_op jit(solution)/shard_map/ppermute | solution.py:572
  399.7 25.4 %collective-permute-start.8 = (bf16[2,256,512]{2,1,0:T(8,128)(2,1)S(1)}, bf16[2,256,512]{2,1,0:T(8,128)(2,1)}, u32[]{:S(2)}, u32[]{:S(2)}) collective-permute-start(bf16[2,256,512]{2,1,0:T(8,128)(2,1)S(1)} %pad_maximum_fusion.6), channel_id=1, source_target_pairs={{0,24},{8,16},{16,8},{24,0},{1,25},{9,17},{17,9},{25,1},{2,26},{10... | collective-permute-start | bytes 1572872 | tf_op jit(solution)/shard_map/ppermute | solution.py:572
  402.8 34.2 %collective-permute-start.9 = (bf16[2,256,512]{2,1,0:T(8,128)(2,1)S(1)}, bf16[2,256,512]{2,1,0:T(8,128)(2,1)S(1)}, u32[]{:S(2)}, u32[]{:S(2)}) collective-permute-start(bf16[2,256,512]{2,1,0:T(8,128)(2,1)S(1)} %pad_maximum_fusion.7), channel_id=1, source_target_pairs={{0,8},{8,0},{16,24},{24,16},{1,9},{9,1},{17,25},{25,17},{2,10},{10... | collective-permute-start | bytes 1572872 | tf_op jit(solution)/shard_map/ppermute | solution.py:572
  404.3 42.3 %collective-permute-start.10 = (bf16[2,256,512]{2,1,0:T(8,128)(2,1)S(1)}, bf16[2,256,512]{2,1,0:T(8,128)(2,1)S(1)}, u32[]{:S(2)}, u32[]{:S(2)}) collective-permute-start(bf16[2,256,512]{2,1,0:T(8,128)(2,1)S(1)} %pad_maximum_fusion.7), channel_id=1, source_target_pairs={{0,16},{8,24},{16,0},{24,8},{1,17},{9,25},{17,1},{25,9},{2,18},{10... | collective-permute-start | bytes 1572872 | tf_op jit(solution)/shard_map/ppermute | solution.py:572
  412.4 34.2 %collective-permute-start.11 = (bf16[2,256,512]{2,1,0:T(8,128)(2,1)S(1)}, bf16[2,256,512]{2,1,0:T(8,128)(2,1)S(1)}, u32[]{:S(2)}, u32[]{:S(2)}) collective-permute-start(bf16[2,256,512]{2,1,0:T(8,128)(2,1)S(1)} %pad_maximum_fusion.7), channel_id=1, source_target_pairs={{0,24},{8,16},{16,8},{24,0},{1,25},{9,17},{17,9},{25,1},{2,26},{10... | collective-permute-start | bytes 1572872 | tf_op jit(solution)/shard_map/ppermute | solution.py:572
  531.4 22.3 %collective-permute-start.12 = (bf16[2,256,512]{2,1,0:T(8,128)(2,1)}, bf16[2,256,512]{2,1,0:T(8,128)(2,1)S(1)}, u32[]{:S(2)}, u32[]{:S(2)}) collective-permute-start(bf16[2,256,512]{2,1,0:T(8,128)(2,1)} %get-tuple-element.112), channel_id=1, source_target_pairs={{0,8},{8,0},{16,24},{24,16},{1,9},{9,1},{17,25},{25,17},{2,10},{10... | collective-permute-start | bytes 1572872 | tf_op jit(solution)/shard_map/ppermute | solution.py:572
  532.0 24.3 %collective-permute-start.13 = (bf16[2,256,512]{2,1,0:T(8,128)(2,1)}, bf16[2,256,512]{2,1,0:T(8,128)(2,1)S(1)}, u32[]{:S(2)}, u32[]{:S(2)}) collective-permute-start(bf16[2,256,512]{2,1,0:T(8,128)(2,1)} %get-tuple-element.113), channel_id=1, source_target_pairs={{0,16},{8,24},{16,0},{24,8},{1,17},{9,25},{17,1},{25,9},{2,18},{10... | collective-permute-start | bytes 1572872 | tf_op jit(solution)/shard_map/ppermute | solution.py:572
  533.5 24.3 %collective-permute-start.14 = (bf16[2,256,512]{2,1,0:T(8,128)(2,1)}, bf16[2,256,512]{2,1,0:T(8,128)(2,1)S(1)}, u32[]{:S(2)}, u32[]{:S(2)}) collective-permute-start(bf16[2,256,512]{2,1,0:T(8,128)(2,1)} %get-tuple-element.114), channel_id=1, source_target_pairs={{0,24},{8,16},{16,8},{24,0},{1,25},{9,17},{17,9},{25,1},{2,26},{10... | collective-permute-start | bytes 1572872 | tf_op jit(solution)/shard_map/ppermute | solution.py:572
  552.2 25.8 %collective-permute-start.16 = (bf16[2,256,512]{2,1,0:T(8,128)(2,1)}, bf16[2,256,512]{2,1,0:T(8,128)(2,1)S(1)}, u32[]{:S(2)}, u32[]{:S(2)}) collective-permute-start(bf16[2,256,512]{2,1,0:T(8,128)(2,1)} %get-tuple-element.117), channel_id=1, source_target_pairs={{0,16},{8,24},{16,0},{24,8},{1,17},{9,25},{17,1},{25,9},{2,18},{10... | collective-permute-start | bytes 1572872 | tf_op jit(solution)/shard_map/ppermute | solution.py:572
  553.6 24.3 %collective-permute-start.17 = (bf16[2,256,512]{2,1,0:T(8,128)(2,1)}, bf16[2,256,512]{2,1,0:T(8,128)(2,1)S(1)}, u32[]{:S(2)}, u32[]{:S(2)}) collective-permute-start(bf16[2,256,512]{2,1,0:T(8,128)(2,1)} %get-tuple-element.118), channel_id=1, source_target_pairs={{0,24},{8,16},{16,8},{24,0},{1,25},{9,17},{17,9},{25,1},{2,26},{10... | collective-permute-start | bytes 1572872 | tf_op jit(solution)/shard_map/ppermute | solution.py:572
  652.4 23.4 %collective-permute-start.18 = (bf16[2,256,512]{2,1,0:T(8,128)(2,1)}, bf16[2,256,512]{2,1,0:T(8,128)(2,1)S(1)}, u32[]{:S(2)}, u32[]{:S(2)}) collective-permute-start(bf16[2,256,512]{2,1,0:T(8,128)(2,1)} %get-tuple-element.132), channel_id=1, source_target_pairs={{0,8},{8,0},{16,24},{24,16},{1,9},{9,1},{17,25},{25,17},{2,10},{10... | collective-permute-start | bytes 1572872 | tf_op jit(solution)/shard_map/ppermute | solution.py:572
  653.9 23.5 %collective-permute-start.19 = (bf16[2,256,512]{2,1,0:T(8,128)(2,1)}, bf16[2,256,512]{2,1,0:T(8,128)(2,1)S(1)}, u32[]{:S(2)}, u32[]{:S(2)}) collective-permute-start(bf16[2,256,512]{2,1,0:T(8,128)(2,1)} %get-tuple-element.133), channel_id=1, source_target_pairs={{0,16},{8,24},{16,0},{24,8},{1,17},{9,25},{17,1},{25,9},{2,18},{10... | collective-permute-start | bytes 1572872 | tf_op jit(solution)/shard_map/ppermute | solution.py:572
  654.5 24.2 %collective-permute-start.20 = (bf16[2,256,512]{2,1,0:T(8,128)(2,1)}, bf16[2,256,512]{2,1,0:T(8,128)(2,1)S(1)}, u32[]{:S(2)}, u32[]{:S(2)}) collective-permute-start(bf16[2,256,512]{2,1,0:T(8,128)(2,1)} %get-tuple-element.134), channel_id=1, source_target_pairs={{0,24},{8,16},{16,8},{24,0},{1,25},{9,17},{17,9},{25,1},{2,26},{10... | collective-permute-start | bytes 1572872 | tf_op jit(solution)/shard_map/ppermute | solution.py:572
  674.4 24.1 %collective-permute-start.22 = (bf16[2,256,512]{2,1,0:T(8,128)(2,1)}, bf16[2,256,512]{2,1,0:T(8,128)(2,1)S(1)}, u32[]{:S(2)}, u32[]{:S(2)}) collective-permute-start(bf16[2,256,512]{2,1,0:T(8,128)(2,1)} %get-tuple-element.137), channel_id=1, source_target_pairs={{0,16},{8,24},{16,0},{24,8},{1,17},{9,25},{17,1},{25,9},{2,18},{10... | collective-permute-start | bytes 1572872 | tf_op jit(solution)/shard_map/ppermute | solution.py:572
  675.8 22.7 %collective-permute-start.23 = (bf16[2,256,512]{2,1,0:T(8,128)(2,1)}, bf16[2,256,512]{2,1,0:T(8,128)(2,1)S(1)}, u32[]{:S(2)}, u32[]{:S(2)}) collective-permute-start(bf16[2,256,512]{2,1,0:T(8,128)(2,1)} %get-tuple-element.138), channel_id=1, source_target_pairs={{0,24},{8,16},{16,8},{24,0},{1,25},{9,17},{17,9},{25,1},{2,26},{10... | collective-permute-start | bytes 1572872 | tf_op jit(solution)/shard_map/ppermute | solution.py:572
  720.3 274.3 %reduce-scatter.3.cloned.1.call-start = ((), (), s32[]{:S(2)}) async-start(), calls=%async_computation.6 | async-start | bytes 9437184 | tf_op jit(solution)/shard_map/reduce_scatter | solution.py:728
  720.9 388.9 %reduce-scatter.5.cloned.1.call-start = ((), (), s32[]{:S(2)}) async-start(), calls=%async_computation.7 | async-start | bytes 11796480 | tf_op jit(solution)/shard_map/reduce_scatter | solution.py:728
  721.5 434.6 %all-gather.12.cloned.1.call-start = ((), (), s32[]{:S(2)}) async-start(), calls=%async_computation.5 | async-start | bytes 3932160 | tf_op jit(solution)/shard_map/all_gather | solution.py:744
  721.8 75.9 %collective-permute-start.40 = (bf16[4,128,5120]{2,1,0:T(8,128)(2,1)}, bf16[4,128,5120]{2,1,0:T(8,128)(2,1)}, u32[]{:S(2)}, u32[]{:S(2)}) collective-permute-start(bf16[4,128,5120]{2,1,0:T(8,128)(2,1)} %get-tuple-element.163), channel_id=1, source_target_pairs={{0,1},{1,0},{2,3},{3,2},{4,5},{5,4},{6,7},{7,6},{8,9},{9,8},{10,11... | collective-permute-start | bytes 15728648 | tf_op jit(solution)/shard_map/ppermute | solution.py:572
  722.3 31.7 %collective-permute-start.32 = (bf16[4,128,4096]{2,1,0:T(8,128)(2,1)}, bf16[4,128,4096]{2,1,0:T(8,128)(2,1)S(1)}, u32[]{:S(2)}, u32[]{:S(2)}) collective-permute-start(bf16[4,128,4096]{2,1,0:T(8,128)(2,1)} %get-tuple-element.161), channel_id=1, source_target_pairs={{0,1},{1,0},{2,3},{3,2},{4,5},{5,4},{6,7},{7,6},{8,9},{9,8},{10,11... | collective-permute-start | bytes 12582920 | tf_op jit(solution)/shard_map/ppermute | solution.py:572
  723.1 22.7 %collective-permute-start.24 = (bf16[4,128,3072]{2,1,0:T(8,128)(2,1)}, bf16[4,128,3072]{2,1,0:T(8,128)(2,1)}, u32[]{:S(2)}, u32[]{:S(2)}) collective-permute-start(bf16[4,128,3072]{2,1,0:T(8,128)(2,1)} %get-tuple-element.159), channel_id=1, source_target_pairs={{0,1},{1,0},{2,3},{3,2},{4,5},{5,4},{6,7},{7,6},{8,9},{9,8},{10,11... | collective-permute-start | bytes 9437192 | tf_op jit(solution)/shard_map/ppermute | solution.py:572
  731.3 20.0 %collective-permute-start.49 = (bf16[4,2,32,1536]{3,2,0,1:T(8,128)(2,1)S(1)}, bf16[4,2,32,1536]{3,2,0,1:T(8,128)(2,1)S(1)}, u32[]{:S(2)}, u32[]{:S(2)}) collective-permute-start(bf16[4,2,32,1536]{3,2,0,1:T(8,128)(2,1)S(1)} %fusion.18), channel_id=1, source_target_pairs={{0,8},{8,0},{16,24},{24,16},{1,9},{9,1},{17,25},{25,17},{2,10},{10... | collective-permute-start | bytes 2359304 | tf_op jit(solution)/shard_map/ppermute | solution.py:572
  732.2 20.0 %collective-permute-start.51 = (bf16[4,2,32,1536]{3,2,0,1:T(8,128)(2,1)S(1)}, bf16[4,2,32,1536]{3,2,0,1:T(8,128)(2,1)S(1)}, u32[]{:S(2)}, u32[]{:S(2)}) collective-permute-start(bf16[4,2,32,1536]{3,2,0,1:T(8,128)(2,1)S(1)} %fusion.19), channel_id=1, source_target_pairs={{0,16},{8,24},{16,0},{24,8},{1,17},{9,25},{17,1},{25,9},{2,18},{10... | collective-permute-start | bytes 2359304 | tf_op jit(solution)/shard_map/ppermute | solution.py:572
  749.3 201.2 %collective-permute-start.25 = (bf16[4,2,32,1536]{3,2,0,1:T(8,128)(2,1)}, bf16[4,2,32,1536]{3,2,0,1:T(8,128)(2,1)}, u32[]{:S(2)}, u32[]{:S(2)}) collective-permute-start(bf16[4,2,32,1536]{3,2,0,1:T(8,128)(2,1)} %fusion.16), channel_id=1, source_target_pairs={{0,8},{8,0},{16,24},{24,16},{1,9},{9,1},{17,25},{25,17},{2,10},{10... | collective-permute-start | bytes 2359304 | tf_op jit(solution)/shard_map/ppermute | solution.py:572
  752.4 25.2 %collective-permute-start.52 = (bf16[4,32,1536]{2,1,0:T(8,128)(2,1)S(1)}, bf16[4,32,1536]{2,1,0:T(8,128)(2,1)S(1)}, u32[]{:S(2)}, u32[]{:S(2)}) collective-permute-start(bf16[4,32,1536]{2,1,0:T(8,128)(2,1)S(1)} %fusion.20), channel_id=1, source_target_pairs={{0,8},{8,0},{16,24},{24,16},{1,9},{9,1},{17,25},{25,17},{2,10},{10... | collective-permute-start | bytes 1179656 | tf_op jit(solution)/shard_map/ppermute | solution.py:572
  787.8 26.2 %collective-permute-start.33 = (bf16[4,2,32,2048]{3,2,0,1:T(8,128)(2,1)S(1)}, bf16[4,2,32,2048]{3,2,0,1:T(8,128)(2,1)S(1)}, u32[]{:S(2)}, u32[]{:S(2)}) collective-permute-start(bf16[4,2,32,2048]{3,2,0,1:T(8,128)(2,1)S(1)} %fusion.8), channel_id=1, source_target_pairs={{0,8},{8,0},{16,24},{24,16},{1,9},{9,1},{17,25},{25,17},{2,10},{10... | collective-permute-start | bytes 3145736 | tf_op jit(solution)/shard_map/ppermute | solution.py:572
  796.7 26.3 %collective-permute-start.35 = (bf16[4,2,32,2048]{3,2,0,1:T(8,128)(2,1)S(1)}, bf16[4,2,32,2048]{3,2,0,1:T(8,128)(2,1)S(1)}, u32[]{:S(2)}, u32[]{:S(2)}) collective-permute-start(bf16[4,2,32,2048]{3,2,0,1:T(8,128)(2,1)S(1)} %fusion.9), channel_id=1, source_target_pairs={{0,16},{8,24},{16,0},{24,8},{1,17},{9,25},{17,1},{25,9},{2,18},{10... | collective-permute-start | bytes 3145736 | tf_op jit(solution)/shard_map/ppermute | solution.py:572
  801.0 48.6 %collective-permute-start.41 = (bf16[4,2,32,2560]{3,2,0,1:T(8,128)(2,1)S(1)}, bf16[4,2,32,2560]{3,2,0,1:T(8,128)(2,1)S(1)}, u32[]{:S(2)}, u32[]{:S(2)}) collective-permute-start(bf16[4,2,32,2560]{3,2,0,1:T(8,128)(2,1)S(1)} %fusion), channel_id=1, source_target_pairs={{0,8},{8,0},{16,24},{24,16},{1,9},{9,1},{17,25},{25,17},{2,10},{10... | collective-permute-start | bytes 3932168 | tf_op jit(solution)/shard_map/ppermute | solution.py:572
  814.2 19.9 %collective-permute-start.34 = (bf16[4,32,2048]{2,1,0:T(8,128)(2,1)S(1)}, bf16[4,32,2048]{2,1,0:T(8,128)(2,1)S(1)}, u32[]{:S(2)}, u32[]{:S(2)}) collective-permute-start(bf16[4,32,2048]{2,1,0:T(8,128)(2,1)S(1)} %fusion.13), channel_id=1, source_target_pairs={{0,16},{8,24},{16,0},{24,8},{1,17},{9,25},{17,1},{25,9},{2,18},{10... | collective-permute-start | bytes 1572872 | tf_op jit(solution)/shard_map/ppermute | solution.py:572
  823.2 26.0 %collective-permute-start.36 = (bf16[4,32,2048]{2,1,0:T(8,128)(2,1)S(1)}, bf16[4,32,2048]{2,1,0:T(8,128)(2,1)S(1)}, u32[]{:S(2)}, u32[]{:S(2)}) collective-permute-start(bf16[4,32,2048]{2,1,0:T(8,128)(2,1)S(1)} %fusion.10), channel_id=1, source_target_pairs={{0,8},{8,0},{16,24},{24,16},{1,9},{9,1},{17,25},{25,17},{2,10},{10... | collective-permute-start | bytes 1572872 | tf_op jit(solution)/shard_map/ppermute | solution.py:572
  824.4 38.1 %collective-permute-start.43 = (bf16[4,2,32,2560]{3,2,0,1:T(8,128)(2,1)S(1)}, bf16[4,2,32,2560]{3,2,0,1:T(8,128)(2,1)S(1)}, u32[]{:S(2)}, u32[]{:S(2)}) collective-permute-start(bf16[4,2,32,2560]{3,2,0,1:T(8,128)(2,1)S(1)} %fusion.1), channel_id=1, source_target_pairs={{0,16},{8,24},{16,0},{24,8},{1,17},{9,25},{17,1},{25,9},{2,18},{10... | collective-permute-start | bytes 3932168 | tf_op jit(solution)/shard_map/ppermute | solution.py:572
  849.8 24.3 %collective-permute-start.42 = (bf16[4,32,2560]{2,1,0:T(8,128)(2,1)S(1)}, bf16[4,32,2560]{2,1,0:T(8,128)(2,1)S(1)}, u32[]{:S(2)}, u32[]{:S(2)}) collective-permute-start(bf16[4,32,2560]{2,1,0:T(8,128)(2,1)S(1)} %fusion.5), channel_id=1, source_target_pairs={{0,16},{8,24},{16,0},{24,8},{1,17},{9,25},{17,1},{25,9},{2,18},{10... | collective-permute-start | bytes 1966088 | tf_op jit(solution)/shard_map/ppermute | solution.py:572
  850.6 42.1 %collective-permute-start.39 = (bf16[32,4096]{1,0:T(8,128)(2,1)S(1)}, bf16[32,4096]{1,0:T(8,128)(2,1)S(1)}, u32[]{:S(2)}, u32[]{:S(2)}) collective-permute-start(bf16[32,4096]{1,0:T(8,128)(2,1)S(1)} %get-tuple-element.211), channel_id=1, source_target_pairs={{0,6},{1,7},{2,4},{3,5},{4,2},{5,3},{6,0},{7,1},{8,14},{9,15},{10,... | collective-permute-start | bytes 786440 | tf_op jit(solution)/shard_map/ppermute | solution.py:572
  852.3 43.1 %collective-permute-start.38 = (bf16[32,4096]{1,0:T(8,128)(2,1)S(1)}, bf16[32,4096]{1,0:T(8,128)(2,1)S(1)}, u32[]{:S(2)}, u32[]{:S(2)}) collective-permute-start(bf16[32,4096]{1,0:T(8,128)(2,1)S(1)} %get-tuple-element.210), channel_id=1, source_target_pairs={{0,4},{1,5},{2,6},{3,7},{4,0},{5,1},{6,2},{7,3},{8,12},{9,13},{10,... | collective-permute-start | bytes 786440 | tf_op jit(solution)/shard_map/ppermute | solution.py:572
  862.5 32.9 %collective-permute-start.37 = (bf16[32,4096]{1,0:T(8,128)(2,1)S(1)}, bf16[32,4096]{1,0:T(8,128)(2,1)S(1)}, u32[]{:S(2)}, u32[]{:S(2)}) collective-permute-start(bf16[32,4096]{1,0:T(8,128)(2,1)S(1)} %get-tuple-element.209), channel_id=1, source_target_pairs={{0,2},{1,3},{2,0},{3,1},{4,6},{5,7},{6,4},{7,5},{8,10},{9,11},{10,... | collective-permute-start | bytes 786440 | tf_op jit(solution)/shard_map/ppermute | solution.py:572
  892.7 50.1 %collective-permute-start.46 = (bf16[32,5120]{1,0:T(8,128)(2,1)S(1)}, bf16[32,5120]{1,0:T(8,128)(2,1)S(1)}, u32[]{:S(2)}, u32[]{:S(2)}) collective-permute-start(bf16[32,5120]{1,0:T(8,128)(2,1)S(1)} %get-tuple-element.207), channel_id=1, source_target_pairs={{0,4},{1,5},{2,6},{3,7},{4,0},{5,1},{6,2},{7,3},{8,12},{9,13},{10,... | collective-permute-start | bytes 983048 | tf_op jit(solution)/shard_map/ppermute | solution.py:572
  895.4 47.4 %collective-permute-start.45 = (bf16[32,5120]{1,0:T(8,128)(2,1)S(1)}, bf16[32,5120]{1,0:T(8,128)(2,1)S(1)}, u32[]{:S(2)}, u32[]{:S(2)}) collective-permute-start(bf16[32,5120]{1,0:T(8,128)(2,1)S(1)} %get-tuple-element.206), channel_id=1, source_target_pairs={{0,2},{1,3},{2,0},{3,1},{4,6},{5,7},{6,4},{7,5},{8,10},{9,11},{10,... | collective-permute-start | bytes 983048 | tf_op jit(solution)/shard_map/ppermute | solution.py:572
  943.9 289.9 %all-reduce.5.cloned.1.call-start = ((), (), s32[]{:S(2)}) async-start(), calls=%async_computation.8 | async-start | bytes 4718592 | tf_op jit(solution)/shard_map/psum | solution.py:746
  945.3 20.8 %collective-permute-start.27 = (bf16[4,2,32,1536]{3,2,0,1:T(8,128)(2,1)}, bf16[4,2,32,1536]{3,2,0,1:T(8,128)(2,1)}, u32[]{:S(2)}, u32[]{:S(2)}) collective-permute-start(bf16[4,2,32,1536]{3,2,0,1:T(8,128)(2,1)} %fusion.17), channel_id=1, source_target_pairs={{0,16},{8,24},{16,0},{24,8},{1,17},{9,25},{17,1},{25,9},{2,18},{10... | collective-permute-start | bytes 2359304 | tf_op jit(solution)/shard_map/ppermute | solution.py:572
  951.8 19.4 %collective-permute-start.26 = (bf16[4,32,1536]{2,1,0:T(8,128)(2,1)S(1)}, bf16[4,32,1536]{2,1,0:T(8,128)(2,1)}, u32[]{:S(2)}, u32[]{:S(2)}) collective-permute-start(bf16[4,32,1536]{2,1,0:T(8,128)(2,1)S(1)} %fusion.29), channel_id=1, source_target_pairs={{0,16},{8,24},{16,0},{24,8},{1,17},{9,25},{17,1},{25,9},{2,18},{10... | collective-permute-start | bytes 1179656 | tf_op jit(solution)/shard_map/ppermute | solution.py:572
  (79 other events, 848.5 us)
Sparse Core Ops, SparseCore 0:
  11.5 72.4 all-gather.13
  87.4 142.9 all-gather.7
  233.9 152.8 all-gather.9
  720.4 135.9 all-reduce.2
  858.5 114.5 reduce-scatter.2
  975.3 134.4 reduce-scatter.4
  1112.2 43.8 all-gather.11
  1159.8 74.0 all-reduce.4

commit v2 on v1

--- a/solution.py
+++ b/solution.py
@@ -253,18 +253,15 @@
     )(thr, qkv, qkv, qkv, *far, lse, do, attended)
 
 
-def gather_slabs(target, source):
-    span, width = source.shape[0], target.shape[1]
-    for a in range(target.shape[0] // span):
-        target[a * span : (a + 1) * span, :] = source[:, a * width : (a + 1) * width]
-
-
-def feed_kernel(
-    parts, x_ref, *refs
-):
+SLABS = 4
+EARLY = 3
+
+
+def feed_kernel(parts, x_ref, *refs):
     att_refs = refs[:parts]
-    (wm_ref, mb_ref, gain_ref, shift_ref, eb_ref, rb_ref, we_ref, wr_ref,
-     out_ref, middle_ref, second_ref, hidden_ref, wr_scr) = refs[parts:]
+    (wm_ref, mb_ref, gain_ref, shift_ref, eb_ref, rb_ref, w_ref,
+     out_ref, middle_ref, second_ref, hidden_ref) = refs[parts:]
+    width = x_ref.shape[1]
 
     @pl.when(pl.program_id(0) == 0)
     def _():
@@ -277,22 +274,20 @@
         second_ref[...] = (normal * gain_ref[...] + shift_ref[...]).astype(BF16)
         out_ref[...] = middle + rb_ref[...]
 
-    gather_slabs(wr_scr, wr_ref)
-    hidden = dot(second_ref[...], we_ref[...]) + eb_ref[...]
-    hidden_ref[...] = hidden.astype(BF16)
-    active = 0.5 * hidden * (1.0 + jnp.tanh(CURVE * (hidden + CUBIC * hidden * hidden * hidden)))
-    out_ref[...] += dot(active.astype(BF16), wr_scr[...])
-
-
-def feed_forward(steps, stream, attended, vec, weights):
+    cut = width // 2
+    for start in range(0, width, cut):
+        hidden = dot(second_ref[...], w_ref[:, start : start + cut]) + eb_ref[:, start : start + cut]
+        hidden_ref[:, start : start + cut] = hidden.astype(BF16)
+        active = 0.5 * hidden * (1.0 + jnp.tanh(CURVE * hidden * (1.0 + CUBIC * hidden * hidden)))
+        out_ref[...] += dot(active.astype(BF16), w_ref[start : start + cut, width:])
+
+
+def feed_forward(stream, attended, vec, weights):
     rows, width = stream.shape
-    ff = 4 * width
-    block = ff // steps
-    span = width // steps
-    (wr, reduce_at), (we, expand_at), (wm, mix_at) = weights
+    array, at, mix_at = weights
     return pl.pallas_call(
         functools.partial(feed_kernel, len(attended)),
-        grid=(steps,),
+        grid=(SLABS,),
         in_specs=[whole((rows, width))]
         + [whole(piece.shape) for piece in attended]
         + [
@@ -300,28 +295,26 @@
             vector(width, V_MB),
             vector(width, V_SG),
             vector(width, V_SS),
-            pl.BlockSpec((1, block), lambda j: (0, V_EB * width // block + j)),
+            pl.BlockSpec((1, width), lambda j: (0, V_EB + j)),
             vector(width, V_RB),
-            pl.BlockSpec((width, block), lambda j: (0, expand_at // block + j)),
-            pl.BlockSpec((span, ff), lambda j: (j, reduce_at // ff)),
+            pl.BlockSpec((width, 2 * width), lambda j: (0, at // (2 * width) + j)),
         ],
         out_specs=[
             whole((rows, width)),
             whole((rows, width)),
             whole((rows, width)),
-            pl.BlockSpec((rows, block), lambda j: (0, j)),
+            pl.BlockSpec((rows, width), lambda j: (0, j)),
         ],
         out_shape=[
             jax.ShapeDtypeStruct((rows, width), F32),
             jax.ShapeDtypeStruct((rows, width), F32),
             jax.ShapeDtypeStruct((rows, width), BF16),
-            jax.ShapeDtypeStruct((rows, ff), BF16),
-        ],
-        scratch_shapes=[pltpu.VMEM((block, width), BF16)],
+            jax.ShapeDtypeStruct((rows, SLABS * width), BF16),
+        ],
         compiler_params=params(),
-        cost_estimate=cost(18 * rows * width * width, 30 * 2**20, rows * ff),
+        cost_estimate=cost(18 * rows * width * width, 30 * 2**20, rows * SLABS * width),
         name="feed_forward",
-    )(stream, *attended, wm, vec, vec, vec, vec, vec, we, wr)
+    )(stream, *attended, array, vec, vec, vec, vec, vec, array)
 
 
 def put_rows(refs, grad, core):
@@ -336,158 +329,142 @@
     other[...] = jnp.where(first, split[:, 1], split[:, 0])
 
 
-def grad_outs(steps, width, columns, block, index, apart):
+def grad_outs(holders, width, columns, block, apart):
     if not apart:
-        return [pl.BlockSpec((width, block), lambda j: (0, index(j)))], [
+        return [pl.BlockSpec((width, block), lambda j: (0, j))], [
             jax.ShapeDtypeStruct((width, columns), BF16)
         ]
-    shape = (steps // 2, width // steps)
-    spec = pl.BlockSpec(shape + (block,), lambda j: (0, 0, index(j)))
+    shape = (holders // 2, width // holders)
+    spec = pl.BlockSpec(shape + (block,), lambda j: (0, 0, j))
     return [spec] * 2, [jax.ShapeDtypeStruct(shape + (columns,), BF16)] * 2
 
 
-def feed_pull_kernel(steps, parts, outs, core_ref, gs_ref, *refs):
-    att_refs = refs[:parts]
-    hidden_ref, second_ref, middle_ref, gain_ref, we_ref, wr_ref, wm_ref = refs[parts : parts + 7]
-    refs = refs[parts + 7 :]
-    dwe_refs, dwr_refs = refs[:outs], refs[outs : 2 * outs]
-    (gm_ref, gatt_ref, deb_ref, drb_ref, dsg_ref, dss_ref, dmb_ref,
-     gb_scr, sec_scr, wr_scr, acc_scr, att_scr) = refs[2 * outs :]
+def feed_pull_kernel(final, slabs, parts, outs, core_ref, gs_ref, *refs):
+    att_refs, refs = refs[:parts], refs[parts:]
+    hidden_ref, second_ref, w_ref = refs[:3]
+    refs = refs[3:]
+    if final:
+        middle_ref, gain_ref, wm_ref, before_ref = refs[:4]
+        refs = refs[4:]
+    dw_refs, deb_ref, refs = refs[:outs], refs[outs], refs[outs + 1 :]
+    if final:
+        gm_ref, gatt_ref, dsg_ref, dss_ref, dmb_ref, acc_ref = refs[:6]
+    else:
+        acc_ref, drb_ref = refs[:2]
+    gb_scr, sec_scr, act_scr = refs[-3:]
     step = pl.program_id(0)
     core = core_ref[0]
     width = gs_ref.shape[1]
-    block = wr_scr.shape[0]
 
     @pl.when(step == 0)
     def _():
         branch = gs_ref[...].astype(BF16)
         gb_scr[...] = branch
-        drb_ref[...] = jnp.sum(branch.astype(F32), 0, keepdims=True)
         sec_scr[...] = second_ref[...].T
-        acc_scr[...] = jnp.zeros_like(acc_scr)
-        size = att_refs[0].shape[1]
-        for part, ref in enumerate(att_refs):
-            att_scr[part * size : (part + 1) * size, :] = ref[...].T
-
-    @pl.when(step < steps)
+        if final:
+            acc_ref[...] = before_ref[...]
+        else:
+            acc_ref[...] = jnp.zeros_like(acc_ref)
+            drb_ref[...] = jnp.sum(branch.astype(F32), 0, keepdims=True)
+
+    @pl.when((step % 2 == 0) & (step < 2 * slabs))
     def _():
-        gather_slabs(wr_scr, wr_ref)
-        branch = gb_scr[...]
-        grad_active = dot_nt(branch, wr_scr[...])
-        v = hidden_ref[...].astype(F32)
-        square = v * v
-        t = jnp.tanh(CURVE * v * (1.0 + CUBIC * square))
-        half = 0.5 + 0.5 * t
-        slope = half + 0.5 * v * (1.0 - t * t) * (CURVE * (1.0 + 3 * CUBIC * square))
-        grad_hidden = (grad_active * slope).astype(BF16)
-        active = (v * half).astype(BF16)
-        deb_ref[...] = jnp.sum(grad_hidden.astype(F32), 0, keepdims=True)
-        wr_scr[...] = dot_tn(active, branch).astype(BF16)
-        span = block * width // (4 * width)
-
-        def put_slabs(target):
-            for a in range(4):
-                target(slice(a * width, (a + 1) * width), wr_scr[a * span : (a + 1) * span, :])
-
-        if outs == 1:
-            def one(columns, value):
-                dwr_refs[0][:, columns] = value
-
-            put_slabs(one)
-        else:
-            for place, ref in enumerate(dwr_refs):
-                @pl.when(step % 2 == (core if place == 0 else 1 - core))
-                def _(ref=ref):
-                    def one(columns, value):
-                        ref[0, :, columns] = value
-
-                    put_slabs(one)
-
-        put_rows(dwe_refs, dot(sec_scr[...], grad_hidden).astype(BF16), core)
-        acc_scr[...] += dot_nt(grad_hidden, we_ref[...])
-
-    @pl.when(step == steps)
+        cut = width // 2
+        for start in range(0, width, cut):
+            columns = slice(start, start + cut)
+            grad_active = dot_nt(gb_scr[...], w_ref[columns, width:])
+            v = hidden_ref[:, columns].astype(F32)
+            square = v * v
+            t = jnp.tanh(CURVE * v * (1.0 + CUBIC * square))
+            half = 0.5 + 0.5 * t
+            slope = half + 0.5 * v * (1.0 - t * t) * (CURVE * (1.0 + 3 * CUBIC * square))
+            grad_hidden = (grad_active * slope).astype(BF16)
+            act_scr[:, columns] = (v * half).astype(BF16)
+            deb_ref[:, columns] = jnp.sum(grad_hidden.astype(F32), 0, keepdims=True)
+            acc_ref[...] += dot_nt(grad_hidden, w_ref[:, columns])
+            put_rows(
+                [ref.at[..., columns] for ref in dw_refs],
+                dot(sec_scr[...], grad_hidden).astype(BF16),
+                core,
+            )
+
+    @pl.when(step % 2 == 1)
     def _():
-        term, dgain, dshift = norm_pull(middle_ref[...], gain_ref[...], acc_scr[...])
+        put_rows(dw_refs, dot_tn(act_scr[...], gb_scr[...]).astype(BF16), core)
+
+    if not final:
+        return
+
+    @pl.when(step == 2 * slabs)
+    def _():
+        term, dgain, dshift = norm_pull(middle_ref[...], gain_ref[...], acc_ref[...])
         dsg_ref[...] = dgain
         dss_ref[...] = dshift
         grad_middle = gs_ref[...] + term
         gm_ref[...] = grad_middle
         grad_mix = grad_middle.astype(BF16)
-        gb_scr[...] = grad_mix
         dmb_ref[...] = jnp.sum(grad_mix.astype(F32), 0, keepdims=True)
         gatt_ref[...] = dot_nt(grad_mix, wm_ref[...]).astype(BF16)
-
-    @pl.when(step >= steps)
-    def _():
-        start = pl.multiple_of((step - steps) * block, block)
-        put_rows(dwe_refs, dot(att_scr[...], gb_scr[:, pl.ds(start, block)]).astype(BF16), core)
-
-
-def feed_backward(steps, core, grad_stream, hidden, second, middle, attended, vec, weights, apart):
+        size = att_refs[0].shape[1]
+        for part, ref in enumerate(att_refs):
+            sec_scr[part * size : (part + 1) * size, :] = ref[...].T
+        put_rows(dw_refs, dot(sec_scr[...], grad_mix).astype(BF16), core)
+
+
+def feed_backward(holders, core, grad_stream, hidden, second, vec, weights, apart, final=()):
     rows, width = grad_stream.shape
-    ff = 4 * width
-    block = ff // steps
-    span = width // steps
-    (wr, reduce_at), (we, expand_at), (wm, mix_at) = weights
+    array, at, mix_at = weights
+    half = SLABS - EARLY if final else EARLY
     row = whole((1, width))
     small = jax.ShapeDtypeStruct((1, width), F32)
-    last = lambda j: jnp.minimum(j, steps - 1)
-    dwe_specs, dwe_shapes = grad_outs(steps, width, ff + width, block, lambda j: j, apart)
-    if apart:
-        dwr_specs = [pl.BlockSpec((1, span, ff), lambda j: (last(j) // 2, 0, 0))] * 2
-        dwr_shapes = [jax.ShapeDtypeStruct((steps // 2, span, ff), BF16)] * 2
+    base = EARLY if final else 0
+    slab = lambda j: base + jnp.minimum(j // 2, half - 1)
+    blocks = 2 * half + 1 if final else 2 * half
+    dw_specs, dw_shapes = grad_outs(holders, width, blocks * width, width, apart)
+    square = whole((rows, width))
+    in_specs = [
+        pl.BlockSpec((rows, width), lambda j: (0, slab(j))),
+        square,
+        pl.BlockSpec((width, 2 * width), lambda j: (0, at // (2 * width) + slab(j))),
+    ]
+    operands = [hidden, second, array]
+    out_specs = dw_specs + [pl.BlockSpec((1, width), lambda j: (0, slab(j) - base))]
+    out_shape = dw_shapes + [jax.ShapeDtypeStruct((1, half * width), F32)]
+    total = jax.ShapeDtypeStruct((rows, width), F32)
+    scratch = [
+        pltpu.VMEM((rows, width), BF16),
+        pltpu.VMEM((width, rows), BF16),
+        pltpu.VMEM((rows, width), BF16),
+    ]
+    attended = []
+    if final:
+        middle, attended, so_far = final
+        in_specs += [
+            square,
+            vector(width, V_SG),
+            pl.BlockSpec((width, width), lambda j: (0, mix_at // width)),
+            square,
+        ]
+        operands += [middle, vec, array, so_far]
+        out_specs += [square, square, row, row, row]
+        out_shape += [total, jax.ShapeDtypeStruct((rows, width), BF16), small, small, small]
+        scratch = [pltpu.VMEM((rows, width), F32)] + scratch
     else:
-        dwr_specs = [pl.BlockSpec((span, ff), lambda j: (last(j), 0))]
-        dwr_shapes = [jax.ShapeDtypeStruct((width, ff), BF16)]
-    outs = len(dwe_specs)
+        out_specs += [square, row]
+        out_shape += [total, small]
     return pl.pallas_call(
-        functools.partial(feed_pull_kernel, steps, len(attended), outs),
-        grid=(steps + width // block,),
-        in_specs=[pl.BlockSpec(memory_space=pltpu.SMEM), whole((rows, width))]
+        functools.partial(feed_pull_kernel, bool(final), half, len(attended), len(dw_specs)),
+        grid=(blocks,),
+        in_specs=[pl.BlockSpec(memory_space=pltpu.SMEM), square]
         + [whole(piece.shape) for piece in attended]
-        + [
-            pl.BlockSpec((rows, block), lambda j: (0, last(j))),
-            whole((rows, width)),
-            whole((rows, width)),
-            vector(width, V_SG),
-            pl.BlockSpec((width, block), lambda j: (0, expand_at // block + last(j))),
-            pl.BlockSpec((span, ff), lambda j: (last(j), reduce_at // ff)),
-            pl.BlockSpec((width, width), lambda j: (0, mix_at // width)),
-        ],
-        out_specs=dwe_specs
-        + dwr_specs
-        + [
-            whole((rows, width)),
-            whole((rows, width)),
-            pl.BlockSpec((1, block), lambda j: (0, last(j))),
-            row,
-            row,
-            row,
-            row,
-        ],
-        out_shape=dwe_shapes
-        + dwr_shapes
-        + [
-            jax.ShapeDtypeStruct((rows, width), F32),
-            jax.ShapeDtypeStruct((rows, width), BF16),
-            jax.ShapeDtypeStruct((1, ff), F32),
-            small,
-            small,
-            small,
-            small,
-        ],
-        scratch_shapes=[
-            pltpu.VMEM((rows, width), BF16),
-            pltpu.VMEM((width, rows), BF16),
-            pltpu.VMEM((block, width), BF16),
-            pltpu.VMEM((rows, width), F32),
-            pltpu.VMEM((width, rows), BF16),
-        ],
+        + in_specs,
+        out_specs=out_specs,
+        out_shape=out_shape,
+        scratch_shapes=scratch,
         compiler_params=params(),
-        cost_estimate=cost(36 * rows * width * width, 50 * 2**20, rows * ff),
+        cost_estimate=cost(blocks * 4 * rows * width * width, blocks * 5 * 2**20, rows * half * width),
         name="feed_backward",
-    )(core, grad_stream, *attended, hidden, second, middle, vec, we, wr, wm)
+    )(core, grad_stream, *attended, *operands)
 
 
 def qkv_pull_kernel(parts, sums, outs, core_ref, *refs):
@@ -523,14 +500,14 @@
         out_ref[...] = gm_ref[...] + term
 
 
-def qkv_backward(steps, core, dqs, conts, sums, normed, stream, grad_middle, vec, weights, apart):
+def qkv_backward(holders, core, dqs, conts, sums, normed, stream, grad_middle, vec, weights):
     rows, width = stream.shape
     parts = len(dqs)
     block = width // parts
     wq, place = weights
     small = jax.ShapeDtypeStruct((1, width), F32)
     flat = [piece for part in sums for piece in part]
-    dw_specs, dw_shapes = grad_outs(steps, width, 3 * width, block, lambda j: j, apart)
+    dw_specs, dw_shapes = grad_outs(holders, width, 3 * width, block, True)
     return pl.pallas_call(
         functools.partial(qkv_pull_kernel, parts, len(sums[0]), len(dw_specs)),
         grid=(3 * parts,),
@@ -580,45 +557,302 @@
     return sum(block.astype(F32) for block in blocks).astype(BF16)
 
 
-def reduce_blocks(mine, other):
-    planes, span, columns = mine.shape
+def split_kernel(count, lows, bits_ref, *refs):
+    for side, low in enumerate(lows):
+        ins = refs[side * count : (side + 1) * count]
+        keep_ref, send_ref = refs[2 * count + 2 * side : 2 * count + 2 * side + 2]
+        bit = bits_ref[side]
+        for k in range(keep_ref.shape[1]):
+            base = (k >> low << (low + 1)) | (k & ((1 << low) - 1))
+            for ref, value in ((keep_ref, bit), (send_ref, 1 - bit)):
+                place = base + (value << low)
+                ref[:, k] = sum(one[:, place].astype(F32) for one in ins).astype(BF16)
+
+
+def split_sum(sides, bits, lows, starts, cut):
+    planes, holders, share, _ = sides[0][0].shape
+    piece = next(size for size in range(cut, 0, -128) if all(start % size == 0 for start in starts))
+    deep = max(1, planes // 2)
+    specs = [
+        pl.BlockSpec((deep, holders, share, piece), lambda i, j, start=start: (i, 0, 0, start // piece + j))
+        for blocks, start in zip(sides, starts)
+        for _ in blocks
+    ]
+    out = pl.BlockSpec((deep, holders // 2, share, piece), lambda i, j: (i, 0, 0, j))
+    return pl.pallas_call(
+        functools.partial(split_kernel, len(sides[0]), lows),
+        grid=(planes // deep, cut // piece),
+        in_specs=[pl.BlockSpec(memory_space=pltpu.SMEM)] + specs,
+        out_specs=[out] * 4,
+        out_shape=[jax.ShapeDtypeStruct((planes, holders // 2, share, cut), BF16)] * 4,
+        compiler_params=params(("arbitrary",) * 2),
+        cost_estimate=cost(planes * holders * share * cut * 4, 12 * planes * holders * share * cut),
+        name="split_sum",
+    )(jnp.stack(bits), *sides[0], *sides[1])
+
+
+def plane_kernel(plane_ref, *refs):
+    ins, outs = refs[:4], refs[4:]
+    cut = ins[0].shape[-1]
+    for step, ref in enumerate(outs):
+        place = jnp.bitwise_xor(plane_ref[0], step)
+        for side in range(2):
+            value = ins[2 * side][place, 0].astype(F32) + ins[2 * side + 1][place, 0].astype(F32)
+            ref[:, side * cut : (side + 1) * cut] = value.astype(BF16)
+
+
+def plane_rows(blocks, plane):
+    planes, _, share, cut = blocks[0].shape
+    return pl.pallas_call(
+        plane_kernel,
+        grid=(1,),
+        in_specs=[pl.BlockSpec(memory_space=pltpu.SMEM)] + [whole(block.shape) for block in blocks],
+        out_specs=[whole((share, 2 * cut))] * planes,
+        out_shape=[jax.ShapeDtypeStruct((share, 2 * cut), BF16)] * planes,
+        compiler_params=params(),
+        cost_estimate=cost(planes * share * cut * 4, planes * share * cut * 12),
+        name="plane_rows",
+    )(plane.reshape(1), *blocks)
+
+
+def reduce_stages(*pairs):
+    planes, span, columns = pairs[0][0].shape
     n_tok = lax.axis_size("tok")
     me, plane = lax.axis_index("tok"), lax.axis_index("wa") // 2
     bits = n_tok.bit_length() - 1
-    got = trade(other, "wa", 1)
-    cut = columns // 2
-    finished = []
-    for side in range(2):
-        order = list(range(bits)) if side == 0 else list(reversed(range(bits)))
-        shape = (planes,) + (2,) * bits + (span // n_tok, cut)
-        pieces = [block[:, :, side * cut : (side + 1) * cut].reshape(shape) for block in (mine, got)]
-        left = list(reversed(range(bits)))
-        for bit in order:
-            axis = 1 + left.index(bit)
-            left.remove(bit)
-            place = (me >> bit) & 1
-            send = added(*[pick(piece, 1 - place, axis) for piece in pieces])
-            kept = [pick(piece, place, axis) for piece in pieces]
-            pieces = kept + [trade(send, "tok", 1 << bit)]
-        finished.append(added(*pieces))
-    block = jnp.concatenate(finished, -1)
-    return added(
-        pick(block, plane, 0),
-        *[trade(pick(block, plane ^ step, 0), "wa", 2 * step) for step in range(1, planes)]
+    cut = columns * len(pairs) // 2
+    sides = [
+        [
+            block.reshape(planes, n_tok, span // n_tok, columns)
+            for block in (mine, trade(other, "wa", 1))
+        ]
+        for mine, other in pairs
+    ]
+    starts = [0, 0]
+    if len(pairs) == 1:
+        sides, starts = sides * 2, [0, cut]
+    orders = [list(range(bits)), list(reversed(range(bits)))]
+    left = [list(range(bits)), list(range(bits))]
+    for turn in range(bits):
+        lows = []
+        for order, rest in zip(orders, left):
+            lows.append(rest.index(order[turn]))
+            rest.remove(order[turn])
+        own = [(me >> order[turn]) & 1 for order in orders]
+        keep0, send0, keep1, send1 = split_sum(sides, own, lows, starts, cut)
+        starts = [0, 0]
+        sends = yield [send0, send1]
+        sides = [
+            [keep, trade(send, "tok", 1 << order[turn])]
+            for keep, send, order in zip((keep0, keep1), sends, orders)
+        ]
+    sends = plane_rows(sides[0] + sides[1], plane)
+    sends = yield sends
+    got = [trade(send, "wa", 2 * step) for step, send in enumerate(sends) if step]
+    return added(sends[0], *got)
+
+
+def assemble_kernel(planes, holders, places_ref, *refs):
+    own_ref, sibling_ref = refs[:2]
+    near_refs, far_refs = refs[2 : 2 + holders], refs[2 + holders : 2 + 2 * holders]
+    out_ref, sems = refs[-2:]
+    wa, me = places_ref[0], places_ref[1]
+    copies = []
+
+    def copy(source, target):
+        copies.append(pltpu.make_async_copy(source, target, sems.at[len(copies)]))
+        copies[-1].start()
+
+    copy(own_ref, out_ref.at[wa])
+    copy(sibling_ref, out_ref.at[jnp.bitwise_xor(wa, 1)])
+    for core, group in enumerate((near_refs, far_refs)):
+        for turn, ref in enumerate(group):
+            for step in range(1, planes):
+                place = out_ref.at[jnp.bitwise_xor(wa, 2 * step + core), jnp.bitwise_xor(me, turn)]
+                copy(ref.at[step - 1], place)
+    for one in copies:
+        one.wait()
+
+
+def assemble(own, sibling, near, far):
+    holders, share, columns = own.shape
+    planes = near[0].shape[0] + 1
+    anywhere = pl.BlockSpec(memory_space=pl.ANY)
+    places = jnp.stack([lax.axis_index("wa"), lax.axis_index("tok")])
+    whole_array = pl.pallas_call(
+        functools.partial(assemble_kernel, planes, holders),
+        in_specs=[pl.BlockSpec(memory_space=pltpu.SMEM)] + [anywhere] * (2 + 2 * holders),
+        out_specs=anywhere,
+        out_shape=jax.ShapeDtypeStruct((2 * planes, holders, share, columns), BF16),
+        scratch_shapes=[pltpu.SemaphoreType.DMA((2 + 2 * holders * (planes - 1),))],
+        compiler_params=pltpu.CompilerParams(vmem_limit_bytes=2**22),
+        cost_estimate=cost(0, 8 * planes * holders * share * columns),
+        name="assemble",
+    )(places, own, sibling, *near, *far)
+    return whole_array.reshape(-1, columns)
+
+
+class Gathering:
+    def __init__(self, shard):
+        n_tok = lax.axis_size("tok")
+        self.own = shard.reshape(n_tok, -1, shard.shape[1])
+        self.ready = pick(self.own, lax.axis_index("tok"), 0)
+        self.stage = 0
+
+    def go(self, ready):
+        planes, n_tok = lax.axis_size("wa") // 2, lax.axis_size("tok")
+        if self.stage == 0:
+            self.sibling = trade(self.own, "wa", 1)
+            self.ready = jnp.stack([trade(ready, "wa", 2 * step) for step in range(1, planes)])
+        elif self.stage == 1:
+            self.near = [ready] + [trade(ready, "tok", step) for step in range(1, n_tok)]
+            self.far = [trade(ready, "wa", 1)]
+            self.ready = self.near
+        elif self.stage == 2:
+            self.near = ready
+            self.far += [trade(block, "wa", 1) for block in ready[1:]]
+            self.ready = None
+        self.stage += 1
+
+    def finish(self):
+        while self.ready is not None:
+            self.go(self.ready)
+        return assemble(self.own, self.sibling, self.near, self.far)
+
+
+def pack_kernel(span, me_ref, expand_ref, reduce_ref, mix_ref, qkv_ref, *out_refs):
+    del me_ref
+    width = mix_ref.shape[2]
+    wide = (2 * SLABS + 1) * width
+    for layer, out_ref in enumerate(out_refs):
+        for a in range(SLABS):
+            start = 2 * a * width
+            for w in range(width // span):
+                place = (w * SLABS + a) * span
+                piece = expand_ref[layer, :, place : place + span]
+                out_ref[:, start + w * span : start + (w + 1) * span] = piece
+            out_ref[:, start + width : start + 2 * width] = reduce_ref[layer, a, 0]
+        out_ref[:, wide - width : wide] = mix_ref[layer]
+        if not layer:
+            out_ref[:, wide:] = qkv_ref[1]
+
+
+def pack(expand, reduce, mix, qkv):
+    n_tok, me = lax.axis_size("tok"), lax.axis_index("tok")
+    layers, span, width = mix.shape
+    share = span // n_tok
+    wide = (2 * SLABS + 1) * width
+    by_row = lambda size: pl.BlockSpec((layers, share, size), lambda i, me: (0, me[0], 0))
+    shapes = [(share, wide + 3 * width), (share, wide)]
+    return pl.pallas_call(
+        functools.partial(pack_kernel, span),
+        grid_spec=pltpu.PrefetchScalarGridSpec(
+            num_scalar_prefetch=1,
+            grid=(1,),
+            in_specs=[
+                by_row(SLABS * width),
+                pl.BlockSpec((layers, SLABS, 1, share, width), lambda i, me: (0, 0, me[0], 0, 0)),
+                by_row(width),
+                by_row(3 * width),
+            ],
+            out_specs=[pl.BlockSpec(shape, lambda i, me: (0, 0)) for shape in shapes],
+        ),
+        out_shape=[jax.ShapeDtypeStruct(shape, BF16) for shape in shapes],
+        compiler_params=params(),
+        cost_estimate=cost(0, 8 * share * wide),
+        name="pack",
+    )(
+        me.reshape(1), expand, reduce.reshape(layers, SLABS, n_tok, share, width), mix, qkv
     )
 
 
-def my_rows(shard, parts, me):
-    rows = shard.shape[0] // parts
-    return lax.dynamic_slice_in_dim(shard, me * rows, rows, 0)
-
-
-def my_slabs(shard, parts, me):
-    width = shard.shape[1]
-    stacked = shard.reshape(4, shard.shape[0] // 4, width)
-    rows = stacked.shape[1] // parts
-    mine = lax.dynamic_slice_in_dim(stacked, me * rows, rows, 1)
-    return mine.transpose(1, 0, 2).reshape(rows, 4 * width)
+class Reduction:
+    def __init__(self, *pairs):
+        self.walk = reduce_stages(*pairs)
+        self.result = None
+        self.ready = next(self.walk)
+
+    def go(self, values):
+        try:
+            self.ready = self.walk.send(values)
+        except StopIteration as stop:
+            self.ready = None
+            self.result = stop.value
+
+    def finish(self):
+        while self.ready is not None:
+            self.go(self.ready)
+        return self.result
+
+
+def together(value, reductions):
+    active = [item for item in reductions if item.ready is not None]
+    value, ready = lax.optimization_barrier((value, [item.ready for item in active]))
+    for item, values in zip(active, ready):
+        item.go(values)
+    return value
+
+
+def feed_out_kernel(pieces, me_ref, *refs):
+    mix_ref, expand_ref, reduce_ref = refs[-3:]
+    span, width = mix_ref.shape[1] * mix_ref.shape[2], mix_ref.shape[3]
+    for step, ref in enumerate(refs[:pieces]):
+        place = jnp.bitwise_xor(me_ref[0], step)
+        for a in range(SLABS):
+            for w in range(width // span):
+                there = 2 * a * width + w * span
+                value = ref[:, there : there + span].astype(F32)
+                expand_ref[0, place, :, (w * SLABS + a) * span : (w * SLABS + a + 1) * span] = value
+            there = (2 * a + 1) * width
+            reduce_ref[0, a, place] = ref[:, there : there + width].astype(F32)
+        mix_ref[0, place] = ref[:, 2 * SLABS * width :].astype(F32)
+
+
+def feed_out(pieces, width, me, layer, held):
+    n_tok = len(pieces)
+    share = pieces[0].shape[0]
+    shapes = [(n_tok, share, width), (n_tok, share, SLABS * width), (SLABS, n_tok, share, width)]
+    return pl.pallas_call(
+        functools.partial(feed_out_kernel, n_tok),
+        grid=(1,),
+        in_specs=[pl.BlockSpec(memory_space=pltpu.SMEM)]
+        + [whole((share, (2 * SLABS + 1) * width)) for _ in pieces]
+        + [pl.BlockSpec(memory_space=pl.ANY) for _ in held],
+        out_specs=[
+            pl.BlockSpec((1,) + shape, lambda i, rank=len(shape): (layer,) + (0,) * rank)
+            for shape in shapes
+        ],
+        out_shape=[jax.ShapeDtypeStruct((LAYERS,) + shape, F32) for shape in shapes],
+        input_output_aliases={1 + n_tok + k: k for k in range(len(held))},
+        compiler_params=params(),
+        cost_estimate=cost(9 * share * n_tok * width, 6 * 9 * share * n_tok * width),
+        name="feed_out",
+    )(me.reshape(1), *pieces, *held)
+
+
+def qkv_out_kernel(pieces, me_ref, *refs):
+    out_ref = refs[-1]
+    for step, ref in enumerate(refs[:pieces]):
+        out_ref[0, jnp.bitwise_xor(me_ref[0], step)] = ref[...].astype(F32)
+
+
+def qkv_out(pieces, columns, me, layer, held):
+    share = pieces[0].shape[0]
+    shape = (len(pieces), share, columns)
+    last = pieces[0].shape[1] // columns - 1
+    return pl.pallas_call(
+        functools.partial(qkv_out_kernel, len(pieces)),
+        grid=(1,),
+        in_specs=[pl.BlockSpec(memory_space=pltpu.SMEM)]
+        + [pl.BlockSpec((share, columns), lambda i: (0, last)) for _ in pieces]
+        + [pl.BlockSpec(memory_space=pl.ANY) for _ in held],
+        out_specs=pl.BlockSpec((1,) + shape, lambda i: (layer, 0, 0, 0)),
+        out_shape=jax.ShapeDtypeStruct((LAYERS,) + shape, F32),
+        input_output_aliases={1 + len(pieces) + k: k for k in range(len(held))},
+        compiler_params=params(),
+        cost_estimate=cost(share * columns, 24 * share * columns),
+        name="qkv_out",
+    )(me.reshape(1), *pieces, *held)
 
 
 def local(
@@ -648,35 +882,32 @@
             return small[:, layer, start * span : (start + count) * span].reshape(1, -1)
 
         pair = piece(2, 2)
+        units = small[:, layer, 8 * span : 12 * span].reshape(n_wa, SLABS, span)
         pieces = [
             piece(0, 1), piece(1, 1), pair[:, :width], jnp.zeros((1, width), BF16), pair[:, width:],
-            piece(4, 1), piece(5, 1), piece(6, 1), piece(7, 1), piece(8, 4),
+            piece(4, 1), piece(5, 1), piece(6, 1), piece(7, 1),
+            units.transpose(1, 0, 2).reshape(1, SLABS * width),
         ]
         return jnp.concatenate(pieces, 1).astype(F32)
 
     vecs = [spread(layer) for layer in range(LAYERS)]
     both = ("wa", "tok")
-
-    def gather(blocks):
-        return lax.all_gather(jnp.concatenate(blocks, 1), both, axis=0, tiled=True)
-
-    def piece_of(weight, layer):
-        return my_rows(weight[layer], n_tok, me)
-
-    def late(layer):
-        return [my_slabs(reduce_weight[layer], n_tok, me), piece_of(expand_weight, layer)]
-
-    first = gather([piece_of(qkv_weight, 0)])
-    rest = gather(late(0) + [piece_of(mix_weight, 0)])
-    after = gather(late(1) + [piece_of(qkv_weight, 1), piece_of(mix_weight, 1)])
-    weights = [
-        ((first, 0), ((rest, 0), (rest, 4 * width), (rest, 8 * width))),
-        ((after, 8 * width), ((after, 0), (after, 4 * width), (after, 11 * width))),
-    ]
+    share = span // n_tok
+
+    wide = (2 * SLABS + 1) * width
+    first = Gathering(qkv_weight[0])
+    rows_middle, rows_last = pack(expand_weight, reduce_weight, mix_weight, qkv_weight)
+    middle_array = lax.all_gather(rows_middle, both, axis=0, tiled=True)
+    last_array = lax.all_gather(rows_last, both, axis=0, tiled=True)
+    first = first.finish()
 
     stream = jnp.concatenate([prompt_in[0], cont_in[0, 0]], 0).astype(F32)
     kept = []
     size = width // parts
+    weights = [
+        ((first, 0), (middle_array, 0, wide - width)),
+        ((middle_array, wide), (last_array, 0, wide - width)),
+    ]
     for layer in range(LAYERS):
         wq, wf = weights[layer]
         qkv, normed = qkv_forward(stream, vecs[layer], *wq)
@@ -693,68 +924,94 @@
             one, lse = attend_forward(thr, qkv, fars[part], part, parts)
             attended.append(one)
             lses.append(lse)
-        result, middle, second, hidden = feed_forward(n_wa, stream, attended, vecs[layer], wf)
+        result, middle, second, hidden = feed_forward(stream, attended, vecs[layer], wf)
         kept.append((stream, normed, qkv, fars, lses, attended, middle, second, hidden))
         stream = result
 
     grad_stream = jnp.concatenate([prompt_cot[0], cont_cot[0, 0]], 0).astype(F32)
-    totals = [None] * LAYERS
     smalls = [None] * LAYERS
+    sync = lax.optimization_barrier
+
+    def spread_rows(block):
+        block = block.reshape(n_tok, share, block.shape[1])
+        return [pick(block, me ^ step, 0) for step in [0] + steps]
+
+    def from_each(blocks):
+        return [blocks[0]] + [trade(block, "tok", step) for step, block in zip(steps, blocks[1:])]
+
+    def to_each(block):
+        return from_each([block] * n_tok)
+
+    late, last, early = [None] * LAYERS, [None] * LAYERS, [None] * LAYERS
     for layer in reversed(range(LAYERS)):
         wq, wf = weights[layer]
-        before, normed, qkv, fars, lses, attended, middle, second, hidden = kept[layer]
-        apart = layer == 0
-        grads = feed_backward(
-            n_wa, core, grad_stream, hidden, second, middle, attended, vecs[layer], wf, apart
+        start, normed, qkv, fars, lses, attended, middle, second, hidden = kept[layer]
+        if not layer:
+            grad_stream = together(grad_stream, [late[1]])
+        common = (n_wa, core, grad_stream, hidden, second, vecs[layer], wf)
+        dw_early, deb_low, so_far, drb = feed_backward(*common, False)
+        early[layer] = lax.psum_scatter(dw_early, "wa", scatter_dimension=0, tiled=True)
+        if not layer:
+            so_far, spread = together((so_far, spread_rows(early[1])), [late[1], last[1]])
+            early[1] = added(*from_each(spread))
+        late_mine, late_other, deb_high, grad_middle, grad_att, dsg, dss, dmb = feed_backward(
+            *common, True, (middle, attended, so_far)
         )
-        outs = 2 if apart else 1
-        dwe, dwr = grads[:outs], grads[outs : 2 * outs]
-        grad_middle, grad_att, deb, drb, dsg, dss, dmb = grads[2 * outs :]
         dqs, conts, sums = [], [], []
         for part in range(parts):
+            if not layer:
+                grad_att = together(grad_att, [last[1]])
+            if layer or part:
+                late[layer] = late[layer] or Reduction((late_mine, late_other))
             dq, cont, own, *far = attend_backward(
                 thr, qkv, fars[part], lses[part], grad_att, attended[part], part, parts
             )
             dqs.append(dq)
             conts.append(cont)
             sums.append([own] + [trade(block, "tok", step) for step, block in zip(steps, far)])
+        conts[-1] = together(conts[-1], [late[layer]])
+        if not layer:
+            upper = jnp.concatenate([early[1], late[1].finish(), last[1].finish()], 1)
+            conts[-1], upper = sync((conts[-1], upper))
+            upper = to_each(upper)
         dwq_mine, dwq_other, grad_stream, dqb, dfg, dfs = qkv_backward(
-            n_wa, core, dqs, conts, sums, normed, before, grad_middle, vecs[layer], wq, True
+            n_wa, core, dqs, conts, sums, normed, start, grad_middle, vecs[layer], wq
         )
-        if apart:
-            done = [reduce_blocks(*dwr), reduce_blocks(*dwe)]
-        else:
-            done = [
-                lax.psum_scatter(block[0], "wa", scatter_dimension=0, tiled=True) for block in (dwr, dwe)
-            ]
-        totals[layer] = done + [reduce_blocks(dwq_mine, dwq_other)]
+        last[layer] = Reduction((dwq_mine, dwq_other))
         dqb = jnp.concatenate([dqb[:, :width], dqb[:, 2 * width :]], 1)
+        deb = jnp.concatenate([deb_low, deb_high], 1)
+        deb = deb.reshape(SLABS, n_wa, span).transpose(1, 0, 2)
         smalls[layer] = [
             piece.reshape(n_wa, -1) for piece in (dfg, dfs, dqb, dmb, dsg, dss, deb, drb)
         ]
 
     small = jnp.stack([jnp.concatenate(pieces, 1) for pieces in smalls], 1)
-    small = lax.psum(small, both)
-    small = lax.dynamic_index_in_dim(small, lax.axis_index("wa"), 0, keepdims=False)
+    bits = n_wa.bit_length() - 1
+    small = small.reshape((2,) * bits + small.shape[1:])
+    for bit in reversed(range(bits)):
+        place = (lax.axis_index("wa") >> bit) & 1
+        small = pick(small, place, 0) + trade(pick(small, 1 - place, 0), "wa", 1 << bit)
+    for step in [1 << bit for bit in range(n_tok.bit_length() - 1)]:
+        small = small + trade(small, "tok", step)
+
+    spread = together(spread_rows(early[0]), [late[0], last[0]])
+    early[0] = added(*from_each(spread))
+    early[0] = together(early[0], [late[0], last[0]])
+    lower = jnp.concatenate([early[0], late[0].finish()], 1)
+    upper, lower = together((upper, lower), [last[0]])
+    feeds = feed_out(upper, width, me, 1, [])
+    qkvs = qkv_out(upper, 3 * width, me, 1, [])
+    feeds = feed_out(to_each(lower), width, me, 0, feeds)
+    qkvs = qkv_out(to_each(last[0].finish()), 3 * width, me, 0, [qkvs])
+    mixes, expands, reduces = [
+        block.reshape(LAYERS, -1, width) if place != 1 else block.reshape(LAYERS, span, -1)
+        for place, block in enumerate(feeds)
+    ]
+    qkvs = qkvs.reshape(LAYERS, span, 3 * width)
 
     def vec_out(start, count):
         return small[:, start * span : (start + count) * span]
 
-    def complete(block):
-        return lax.all_gather(block, "tok", axis=0, tiled=True)
-
-    upper = lax.psum(jnp.concatenate(totals[1][:2], 1), "tok")
-    lower = complete(jnp.concatenate(totals[0][:2] + totals[1][2:], 1))
-    lower_qkv = complete(totals[0][2])
-    wide = 9 * width
-    pairs = [(lower[:, :wide], lower_qkv), (upper, lower[:, wide:])]
-
-    def weight_out(source, start, count):
-        return jnp.stack(
-            [pair[source][:, start * width : (start + count) * width] for pair in pairs], 0
-        ).astype(F32)
-
-    reduce_out = weight_out(0, 0, 4).reshape(LAYERS, span, 4, width).transpose(0, 2, 1, 3)
     return (
         stream[:rows][None],
         stream[rows:][None, None],
@@ -762,15 +1019,15 @@
         grad_stream[rows:][None, None],
         vec_out(0, 1),
         vec_out(1, 1),
-        weight_out(1, 0, 3),
+        qkvs,
         vec_out(2, 2),
-        weight_out(0, 8, 1),
+        mixes,
         vec_out(4, 1),
         vec_out(5, 1),
         vec_out(6, 1),
-        weight_out(0, 4, 4),
+        expands,
         vec_out(7, 4),
-        reduce_out.reshape(LAYERS, 4 * span, width),
+        reduces,
         vec_out(11, 1),
     )
 

time: 1270 us -> 949 us (0.75)
  waiting for transfers between devices: 769 us -> 391 us
  Pallas kernels: 279 us -> 358 us
  starting transfers between devices: 68.4 us -> 94.6 us
  other arithmetic: 36.6 us -> 13.1 us
  local copies, waits for them, and re-layouts: 54.2 us -> 31.6 us
    all_gather x4 -> x2, waiting for transfers between devices: 268 us -> 46.5 us  [the longest x1 37.6 us: local(): last_array = lax.all_gather(rows_last, both, axis=0, tiled=True)]
    reduce_scatter x2, waiting for transfers between devices: 115 us -> 0.02 us  [local(): lax.psum_scatter(dw_early, 'wa', scatter_dimension=0, tiled=True)]
    pallas_call x4 -> x24, Pallas kernels: 114 us -> 192 us  [the longest x4 97.6 us: feed_backward(): pl.pallas_call(functools.partial(feed_pull_kernel, bool(final), half, len...]
    psum x2 -> x0, waiting for transfers between devices: 70.2 us -> none  [the longest x1 70.2 us: local(): upper = lax.psum(jnp.concatenate(totals[1][:2], 1), 'tok')]
    ppermute x56 -> x87, waiting for transfers between devices: 315 us -> 344 us  [trade(): lax.ppermute(block, axis, [(i, i ^ bits) for i in range(lax.axis_size(axi...]
    ppermute x56 -> x87, starting transfers between devices: 67.7 us -> 94.5 us  [trade(): lax.ppermute(block, axis, [(i, i ^ bits) for i in range(lax.axis_size(axi...]
    all_gather x1, blocking collectives: 15.7 us -> 38.9 us  [local(): small = lax.all_gather(small, 'wa', axis=0, tiled=False)]
    slice x14 -> x2, local copies, waits for them, and re-layouts: 18 us -> 0.08 us  [the longest x1 0.05 us: local(): first = Gathering(qkv_weight[0])]
  transfers between devices with their start and end apart: 64 -> 91, of which waited for: 40 -> 40; matrix products, arithmetic and copies ran while one was open for 5% -> 3% of each run, Pallas kernels for 8% -> 32%
where the time goes in v2:
time: 949 us; the launch traced here: 943 us
  waiting for transfers between devices  391 us (41%)
  Pallas kernels  358 us (38%)
  starting transfers between devices  94.6 us (10%)
  blocking collectives  38.9 us (4%)
  local copies, waits for them, and re-layouts  31.6 us (3%)
  between operations  15.3 us (2%)
  other arithmetic  13.1 us (1%)
    ppermute x87, waiting for transfers between devices, trade(): lax.ppermute(block, axis, [(i, i ^ bits) for i in range(lax.axis_size(axi...  344 us
    pallas_call x4, Pallas kernels, feed_backward(): pl.pallas_call(functools.partial(feed_pull_kernel, bool(final), half, len...  97.6 us
    ppermute x87, starting transfers between devices, trade(): lax.ppermute(block, axis, [(i, i ^ bits) for i in range(lax.axis_size(axi...  94.5 us
    pallas_call x4, Pallas kernels, attend_backward(): pl.pallas_call(functools.partial(attend_pull_kernel, pb, len(far)), grid=...  66.3 us
    pallas_call x4, Pallas kernels, attend_forward(): pl.pallas_call(functools.partial(attend_kernel, pb, len(far)), grid=(pair...  43.7 us
    all_gather x1, blocking collectives, local(): small = lax.all_gather(small, 'wa', axis=0, tiled=False)  38.9 us
    all_gather x1, waiting for transfers between devices, local(): last_array = lax.all_gather(rows_last, both, axis=0, tiled=True)  37.6 us
    pallas_call x2, Pallas kernels, qkv_backward(): pl.pallas_call(functools.partial(qkv_pull_kernel, parts, len(sums[0]), le...  36.4 us
  transfers between devices with their start and end apart: 91, of which 40 were waited for; matrix products, arithmetic and copies ran while one was open for 3% of the time, Pallas kernels for 32%

profile of v2, /device:TPU:0, one launch (start us, length us, event | category | flops | bytes accessed | tf_op | source)
XLA Modules:
  0.0 942.8 jit_solution(13486220660752024459)
XLA Ops:
  16.9 38.9 %all-gather.1 = bf16[8,2,1536]{2,1,0:T(2,128)(2,1)S(1)} all-gather(bf16[1,2,1536]{2,1,0:T(2,128)(2,1)S(1)} %bitcast.213), channel_id=2, replica_groups=mesh['tok'=4,'wa'=8] {'wa'}, dimensions={0}, use_global_device_ids=true | all-gather | bytes 55296 | tf_op jit(solution)/shard_map/all_gather | solution.py:878
  59.8 24.8 %collective-permute-done.4.refs_3_ = bf16[3,32,3072]{2,1,0:T(8,128)(2,1)S(1)} collective-permute-done((bf16[3,32,3072]{2,1,0:T(8,128)(2,1)S(1)}, bf16[3,32,3072]{2,1,0:T(8,128)(2,1)S(1)}, u32[]{:S(2)}, u32[]{:S(2)}) %collective-permute-start.4) | collective-permute-done | bytes 589856 | tf_op jit(solution)/shard_map/ppermute | solution.py:549
  85.1 22.3 %collective-permute-done.6.refs_5_ = bf16[3,32,3072]{2,1,0:T(8,128)(2,1)} collective-permute-done((bf16[3,32,3072]{2,1,0:T(8,128)(2,1)S(1)}, bf16[3,32,3072]{2,1,0:T(8,128)(2,1)}, u32[]{:S(2)}, u32[]{:S(2)}) %collective-permute-start.6) | collective-permute-done | bytes 589856 | tf_op jit(solution)/shard_map/ppermute | solution.py:549
  111.1 5.6 assemble.1
  119.3 9.9 %qkv_forward.2 = (bf16[512,3072]{1,0:T(8,128)(2,1)}, bf16[512,1024]{1,0:T(8,128)(2,1)}) custom-call(f32[512,1024]{1,0:T(8,128)} %maximum_convert_fusion.x_ref.refs_13_, f32[1,13312]{1,0:T(1,128)} %convert_element_type.103.gain_ref.shift_ref.bias_ref.refs_3_.refs_4_.refs_5_.refs_6_.refs_7_.refs_15_, ...), custom_call_target="tpu_custom_call" | custom-call | flops 3221225472 | bytes 16777216 | tf_op jit(solution)/shard_map/qkv_forward/pallas_call | solution.py:81
  140.2 16.4 %collective-permute-done.11.refs_4_ = bf16[2,256,512]{2,1,0:T(8,128)(2,1)S(1)} collective-permute-done((bf16[2,256,512]{2,1,0:T(8,128)(2,1)S(1)}, bf16[2,256,512]{2,1,0:T(8,128)(2,1)S(1)}, u32[]{:S(2)}, u32[]{:S(2)}) %collective-permute-start.11) | collective-permute-done | bytes 524320 | tf_op jit(solution)/shard_map/ppermute | solution.py:549
  157.9 21.1 %collective-permute-done.13.refs_6_ = bf16[2,256,512]{2,1,0:T(8,128)(2,1)S(1)} collective-permute-done((bf16[2,256,512]{2,1,0:T(8,128)(2,1)S(1)}, bf16[2,256,512]{2,1,0:T(8,128)(2,1)S(1)}, u32[]{:S(2)}, u32[]{:S(2)}) %collective-permute-start.13) | collective-permute-done | bytes 524320 | tf_op jit(solution)/shard_map/ppermute | solution.py:549
  179.8 10.9 %attend_forward.4 = (bf16[512,512]{1,0:T(8,128)(2,1)}, f32[8,1,512]{2,1,0:T(1,128)}) custom-call(s32[4]{0:T(128)} %fusion.2.refs_0_, bf16[512,3072]{1,0:T(8,128)(2,1)} %get-tuple-element.206.refs_1_.refs_2_.refs_3_, bf16[512,3072]{1,0:T(8,128)(2,1)} %get-tuple-element.206.refs_1_.refs_2_.refs_3_, ...), custom_call_target="tpu_custom_call" | custom-call | flops 16106127360 | bytes 5242880 | tf_op jit(solution)/shard_map/attend_forward/pallas_call | solution.py:158
  190.6 10.9 %collective-permute-done.14.refs_4_ = bf16[2,256,512]{2,1,0:T(8,128)(2,1)S(1)} collective-permute-done((bf16[2,256,512]{2,1,0:T(8,128)(2,1)S(1)}, bf16[2,256,512]{2,1,0:T(8,128)(2,1)S(1)}, u32[]{:S(2)}, u32[]{:S(2)}) %collective-permute-start.14) | collective-permute-done | bytes 524320 | tf_op jit(solution)/shard_map/ppermute | solution.py:549
  201.5 14.0 %collective-permute-done.16.refs_6_ = bf16[2,256,512]{2,1,0:T(8,128)(2,1)S(1)} collective-permute-done((bf16[2,256,512]{2,1,0:T(8,128)(2,1)S(1)}, bf16[2,256,512]{2,1,0:T(8,128)(2,1)S(1)}, u32[]{:S(2)}, u32[]{:S(2)}) %collective-permute-start.16) | collective-permute-done | bytes 524320 | tf_op jit(solution)/shard_map/ppermute | solution.py:549
  216.4 10.9 %attend_forward.5 = (bf16[512,512]{1,0:T(8,128)(2,1)}, f32[8,1,512]{2,1,0:T(1,128)}) custom-call(s32[4]{0:T(128)} %fusion.2.refs_0_, bf16[512,3072]{1,0:T(8,128)(2,1)} %get-tuple-element.206.refs_1_.refs_2_.refs_3_, bf16[512,3072]{1,0:T(8,128)(2,1)} %get-tuple-element.206.refs_1_.refs_2_.refs_3_, ...), custom_call_target="tpu_custom_call" | custom-call | flops 16106127360 | bytes 5242880 | tf_op jit(solution)/shard_map/attend_forward/pallas_call | solution.py:158
  227.3 8.9 all-gather.5.cloned.1.call-done.refs_2_.refs_8_.w_ref.refs_16_.refs_4_.refs_7_
  236.2 17.7 %feed_forward.2 = (f32[512,1024]{1,0:T(8,128)}, f32[512,1024]{1,0:T(8,128)}, bf16[512,1024]{1,0:T(8,128)(2,1)}, bf16[512,4096]{1,0:T(8,128)(2,1)}) custom-call(f32[512,1024]{1,0:T(8,128)} %maximum_convert_fusion.x_ref.refs_13_, bf16[512,512]{1,0:T(8,128)(2,1)} %get-tuple-element.207.refs_0_.refs_9_, bf16[512,512]{1,0:T(8,128)(2,1)} %get-tuple-element.208.refs_1_.refs_9_, ...), custom_call_target="tpu_custom_call" | custom-call | flops 9663676416 | bytes 31457280 | tf_op jit(solution)/shard_map/feed_forward/pallas_call | solution.py:288
  254.0 9.4 qkv_forward.3
  272.5 15.1 %collective-permute-done.17.refs_4_ = bf16[2,256,512]{2,1,0:T(8,128)(2,1)S(1)} collective-permute-done((bf16[2,256,512]{2,1,0:T(8,128)(2,1)S(1)}, bf16[2,256,512]{2,1,0:T(8,128)(2,1)S(1)}, u32[]{:S(2)}, u32[]{:S(2)}) %collective-permute-start.17) | collective-permute-done | bytes 524320 | tf_op jit(solution)/shard_map/ppermute | solution.py:549
  290.4 19.3 %collective-permute-done.19.refs_6_ = bf16[2,256,512]{2,1,0:T(8,128)(2,1)} collective-permute-done((bf16[2,256,512]{2,1,0:T(8,128)(2,1)S(1)}, bf16[2,256,512]{2,1,0:T(8,128)(2,1)}, u32[]{:S(2)}, u32[]{:S(2)}) %collective-permute-start.19) | collective-permute-done | bytes 524320 | tf_op jit(solution)/shard_map/ppermute | solution.py:549
  309.6 11.1 %attend_forward.6 = (bf16[512,512]{1,0:T(8,128)(2,1)}, f32[8,1,512]{2,1,0:T(1,128)}) custom-call(s32[4]{0:T(128)} %fusion.2.refs_0_, bf16[512,3072]{1,0:T(8,128)(2,1)} %get-tuple-element.211.refs_1_.refs_2_.refs_3_, bf16[512,3072]{1,0:T(8,128)(2,1)} %get-tuple-element.211.refs_1_.refs_2_.refs_3_, ...), custom_call_target="tpu_custom_call" | custom-call | flops 16106127360 | bytes 5242880 | tf_op jit(solution)/shard_map/attend_forward/pallas_call | solution.py:158
  320.7 17.8 %collective-permute-done.22.refs_6_ = bf16[2,256,512]{2,1,0:T(8,128)(2,1)S(1)} collective-permute-done((bf16[2,256,512]{2,1,0:T(8,128)(2,1)S(1)}, bf16[2,256,512]{2,1,0:T(8,128)(2,1)S(1)}, u32[]{:S(2)}, u32[]{:S(2)}) %collective-permute-start.22) | collective-permute-done | bytes 524320 | tf_op jit(solution)/shard_map/ppermute | solution.py:549
  339.3 10.9 %attend_forward.7 = (bf16[512,512]{1,0:T(8,128)(2,1)}, f32[8,1,512]{2,1,0:T(1,128)}) custom-call(s32[4]{0:T(128)} %fusion.2.refs_0_, bf16[512,3072]{1,0:T(8,128)(2,1)} %get-tuple-element.211.refs_1_.refs_2_.refs_3_, bf16[512,3072]{1,0:T(8,128)(2,1)} %get-tuple-element.211.refs_1_.refs_2_.refs_3_, ...), custom_call_target="tpu_custom_call" | custom-call | flops 16106127360 | bytes 5242880 | tf_op jit(solution)/shard_map/attend_forward/pallas_call | solution.py:158
  350.2 37.6 %all-gather.7.cloned.1.call-done.refs_2_.refs_8_.refs_4_.refs_7_ = bf16[1024,9216]{1,0:T(8,128)(2,1)} async-done(((bf16[32,9216]{1,0:T(8,128)(2,1)}), bf16[1024,9216]{1,0:T(8,128)(2,1)}) %all-gather.7.cloned.1.call-update) | async-done | bytes 18874384 | tf_op jit(solution)/shard_map/all_gather | solution.py:901
  387.8 17.6 %feed_forward.3 = (f32[512,1024]{1,0:T(8,128)}, f32[512,1024]{1,0:T(8,128)}, bf16[512,1024]{1,0:T(8,128)(2,1)}, bf16[512,4096]{1,0:T(8,128)(2,1)}) custom-call(f32[512,1024]{1,0:T(8,128)} %get-tuple-element.210.x_ref.refs_13_, bf16[512,512]{1,0:T(8,128)(2,1)} %get-tuple-element.212.refs_0_.refs_9_, bf16[512,512]{1,0:T(8,128)(2,1)} %get-tuple-element.213.refs_1_.refs_9_, ...), custom_call_target="tpu_custom_call" | custom-call | flops 9663676416 | bytes 31457280 | tf_op jit(solution)/shard_map/feed_forward/pallas_call | solution.py:288
  405.4 29.7 %feed_backward.4 = (bf16[1024,6144]{1,0:T(8,128)(2,1)}, f32[1,3072]{1,0:T(1,128)}, f32[512,1024]{1,0:T(8,128)}, f32[1,1024]{1,0:T(1,128)}) custom-call(s32[1]{0:T(128)} %bitcast.45.core_ref, f32[512,1024]{1,0:T(8,128)} %maximum_convert_fusion.1.gs_ref, bf16[512,4096]{1,0:T(8,128)(2,1)} %get-tuple-element.218.refs_0_.refs_2_, ...), custom_call_target="tpu_custom_call" | custom-call | flops 12884901888 | bytes 31457280 | tf_op jit(solution)/shard_map/feed_backward/pallas_call | solution.py:455
  435.1 19.8 %feed_backward.5 = (bf16[4,128,3072]{2,1,0:T(8,128)(2,1)}, bf16[4,128,3072]{2,1,0:T(8,128)(2,1)}, f32[1,1024]{1,0:T(1,128)}, f32[512,1024]{1,0:T(8,128)}, bf16[5...) custom-call(s32[1]{0:T(128)} %bitcast.45.core_ref, ...), custom_call_target="tpu_custom_call" | custom-call | flops 6442450944 | bytes 15728640 | tf_op jit(solution)/shard_map/feed_backward/pallas_call | solution.py:455
  455.2 16.8 %attend_backward.4 = (bf16[512,512]{1,0:T(8,128)(2,1)}, bf16[2,256,512]{2,1,0:T(8,128)(2,1)}, bf16[2,256,512]{2,1,0:T(8,128)(2,1)}, bf16[2,256,512]{2,1,0:T(8,12...) custom-call(s32[4]{0:T(128)} %fusion.2.refs_0_, ...), custom_call_target="tpu_custom_call" | custom-call | flops 26843545600 | bytes 9437184 | tf_op jit(solution)/shard_map/attend_backward/pallas_call | solution.py:237
  475.5 16.4 %attend_backward.5 = (bf16[512,512]{1,0:T(8,128)(2,1)}, bf16[2,256,512]{2,1,0:T(8,128)(2,1)}, bf16[2,256,512]{2,1,0:T(8,128)(2,1)}, bf16[2,256,512]{2,1,0:T(8,12...) custom-call(s32[4]{0:T(128)} %fusion.2.refs_0_, ...), custom_call_target="tpu_custom_call" | custom-call | flops 26843545600 | bytes 9437184 | tf_op jit(solution)/shard_map/attend_backward/pallas_call | solution.py:237
  502.6 7.0 collective-permute-done.27.refs_9_
  509.8 11.2 %collective-permute-done.29.refs_11_ = bf16[2,256,512]{2,1,0:T(8,128)(2,1)} collective-permute-done((bf16[2,256,512]{2,1,0:T(8,128)(2,1)}, bf16[2,256,512]{2,1,0:T(8,128)(2,1)}, u32[]{:S(2)}, u32[]{:S(2)}) %collective-permute-start.29) | collective-permute-done | bytes 524320 | tf_op jit(solution)/shard_map/ppermute | solution.py:549
  521.0 18.3 %qkv_backward.2 = (bf16[4,128,3072]{2,1,0:T(8,128)(2,1)}, bf16[4,128,3072]{2,1,0:T(8,128)(2,1)}, f32[512,1024]{1,0:T(8,128)}, f32[1,3072]{1,0:T(1,128)}, f32[1,1024]{1,0:T(1,128)}, /*index=5*/f32[1,1024]{1,0:T(1,128)}) custom-call(s32[1]{0:T(128)} %bitcast.45.core_ref, bf16[512,512]{1,0:T(8,128)(2,1)} %get-tuple-element.223.refs_0_, ...), custom_call_target="tpu_custom_call" | custom-call | flops 6442450944 | bytes 25165824 | tf_op jit(solution)/shard_map/qkv_backward/pallas_call | solution.py:511
  543.3 29.6 %feed_backward.6 = (bf16[1024,6144]{1,0:T(8,128)(2,1)}, f32[1,3072]{1,0:T(1,128)}, f32[512,1024]{1,0:T(8,128)}, f32[1,1024]{1,0:T(1,128)}) custom-call(s32[1]{0:T(128)} %bitcast.45.core_ref, f32[512,1024]{1,0:T(8,128)} %get-tuple-element.250.gs_ref, bf16[512,4096]{1,0:T(8,128)(2,1)} %get-tuple-element.251.refs_0_.refs_2_, ...), custom_call_target="tpu_custom_call" | custom-call | flops 12884901888 | bytes 31457280 | tf_op jit(solution)/shard_map/feed_backward/pallas_call | solution.py:455
  576.1 9.0 collective-permute-done.32.refs_1_
  603.9 18.6 %feed_backward.7 = (bf16[4,128,3072]{2,1,0:T(8,128)(2,1)}, bf16[4,128,3072]{2,1,0:T(8,128)(2,1)}, f32[1,1024]{1,0:T(1,128)}, f32[512,1024]{1,0:T(8,128)}, bf16[5...) custom-call(s32[1]{0:T(128)} %bitcast.45.core_ref, ...), custom_call_target="tpu_custom_call" | custom-call | flops 6442450944 | bytes 15728640 | tf_op jit(solution)/shard_map/feed_backward/pallas_call | solution.py:455
  623.5 8.0 collective-permute-done.44
  633.1 7.3 collective-permute-done.41
  647.0 16.7 %attend_backward.6 = (bf16[512,512]{1,0:T(8,128)(2,1)}, bf16[2,256,512]{2,1,0:T(8,128)(2,1)}, bf16[2,256,512]{2,1,0:T(8,128)(2,1)}, bf16[2,256,512]{2,1,0:T(8,12...) custom-call(s32[4]{0:T(128)} %fusion.2.refs_0_, ...), custom_call_target="tpu_custom_call" | custom-call | flops 26843545600 | bytes 9437184 | tf_op jit(solution)/shard_map/attend_backward/pallas_call | solution.py:237
  672.8 16.4 %attend_backward.7 = (bf16[512,512]{1,0:T(8,128)(2,1)}, bf16[2,256,512]{2,1,0:T(8,128)(2,1)}, bf16[2,256,512]{2,1,0:T(8,128)(2,1)}, bf16[2,256,512]{2,1,0:T(8,12...) custom-call(s32[4]{0:T(128)} %fusion.2.refs_0_, ...), custom_call_target="tpu_custom_call" | custom-call | flops 26843545600 | bytes 9437184 | tf_op jit(solution)/shard_map/attend_backward/pallas_call | solution.py:237
  690.2 9.2 collective-permute-done.47
  709.5 5.7 collective-permute-done.51.refs_7_
  715.2 10.9 %collective-permute-done.52.refs_9_ = bf16[2,256,512]{2,1,0:T(8,128)(2,1)S(1)} collective-permute-done((bf16[2,256,512]{2,1,0:T(8,128)(2,1)}, bf16[2,256,512]{2,1,0:T(8,128)(2,1)S(1)}, u32[]{:S(2)}, u32[]{:S(2)}) %collective-permute-start.52) | collective-permute-done | bytes 524320 | tf_op jit(solution)/shard_map/ppermute | solution.py:549
  726.4 8.8 collective-permute-done.54.refs_11_
  735.3 18.1 %qkv_backward.3 = (bf16[4,128,3072]{2,1,0:T(8,128)(2,1)}, bf16[4,128,3072]{2,1,0:T(8,128)(2,1)}, f32[512,1024]{1,0:T(8,128)}, f32[1,3072]{1,0:T(1,128)}, f32[1,1024]{1,0:T(1,128)}, /*index=5*/f32[1,1024]{1,0:T(1,128)}) custom-call(s32[1]{0:T(128)} %bitcast.45.core_ref, bf16[512,512]{1,0:T(8,128)(2,1)} %get-tuple-element.277.refs_0_, ...), custom_call_target="tpu_custom_call" | custom-call | flops 6442450944 | bytes 25165824 | tf_op jit(solution)/shard_map/qkv_backward/pallas_call | solution.py:511
  764.0 12.9 %collective-permute-done.63.refs_1_ = bf16[4,2,32,1536]{3,2,1,0:T(8,128)(2,1)} collective-permute-done((bf16[4,2,32,1536]{3,2,1,0:T(8,128)(2,1)}, bf16[4,2,32,1536]{3,2,1,0:T(8,128)(2,1)}, u32[]{:S(2)}, u32[]{:S(2)}) %collective-permute-start.63) | collective-permute-done | bytes 786464 | tf_op jit(solution)/shard_map/ppermute | solution.py:549
  790.9 7.8 collective-permute-done.68
  808.1 5.8 collective-permute-done.69.refs_1_
  818.8 13.7 %collective-permute-done.71.refs_1_ = bf16[4,2,32,1536]{3,2,1,0:T(8,128)(2,1)S(1)} collective-permute-done((bf16[4,2,32,1536]{3,2,1,0:T(8,128)(2,1)}, bf16[4,2,32,1536]{3,2,1,0:T(8,128)(2,1)S(1)}, u32[]{:S(2)}, u32[]{:S(2)}) %collective-permute-start.71) | collective-permute-done | bytes 786464 | tf_op jit(solution)/shard_map/ppermute | solution.py:549
  847.8 6.4 collective-permute-done.74
  856.4 16.4 %collective-permute-done.76.refs_1_ = bf16[4,1,32,1536]{3,2,1,0:T(8,128)(2,1)S(1)} collective-permute-done((bf16[4,1,32,1536]{3,2,1,0:T(8,128)(2,1)}, bf16[4,1,32,1536]{3,2,1,0:T(8,128)(2,1)S(1)}, u32[]{:S(2)}, u32[]{:S(2)}) %collective-permute-start.76) | collective-permute-done | bytes 393248 | tf_op jit(solution)/shard_map/ppermute | solution.py:549
  888.4 10.3 %collective-permute-done.79 = bf16[32,3072]{1,0:T(8,128)(2,1)S(1)} collective-permute-done((bf16[32,3072]{1,0:T(8,128)(2,1)}, bf16[32,3072]{1,0:T(8,128)(2,1)S(1)}, u32[]{:S(2)}, u32[]{:S(2)}) %collective-permute-start.79) | collective-permute-done | bytes 196640 | tf_op jit(solution)/shard_map/ppermute | solution.py:549
  905.0 13.7 %collective-permute-done.81.refs_1_ = bf16[32,3072]{1,0:T(8,128)(2,1)S(1)} collective-permute-done((bf16[32,3072]{1,0:T(8,128)(2,1)S(1)}, bf16[32,3072]{1,0:T(8,128)(2,1)S(1)}, u32[]{:S(2)}, u32[]{:S(2)}) %collective-permute-start.81) | collective-permute-done | bytes 196640 | tf_op jit(solution)/shard_map/ppermute | solution.py:549
  (453 shorter events, 212.1 us)
Async XLA Ops:
  7.2 229.0 %all-gather.5.cloned.1.call-start = ((), (), s32[]{:S(2)}) async-start(), calls=%async_computation.2 | async-start | bytes 25952256 | tf_op jit(solution)/shard_map/all_gather | solution.py:900
  10.0 377.8 %all-gather.7.cloned.1.call-start = ((), (), s32[]{:S(2)}) async-start(), calls=%async_computation.3 | async-start | bytes 19464192 | tf_op jit(solution)/shard_map/all_gather | solution.py:901
  10.7 584.5 %reduce-scatter.3.cloned.1.call-start = ((), (), s32[]{:S(2)}) async-start(), calls=%async_computation.4 | async-start | bytes 14155776 | tf_op jit(solution)/shard_map/reduce_scatter | solution.py:953
  10.8 100.2 %collective-permute-start = (bf16[4,32,3072]{2,1,0:T(8,128)(2,1)S(1)}, bf16[4,32,3072]{2,1,0:T(8,128)(2,1)S(1)}, u32[]{:S(2)}, u32[]{:S(2)}) collective-permute-start(bf16[4,32,3072]{2,1,0:T(8,128)(2,1)S(1)} %bitcast.171), channel_id=1, source_target_pairs={{0,1},{1,0},{2,3},{3,2},{4,5},{5,4},{6,7},{7,6},{8,9},{9,8},{10,11... | collective-permute-start | bytes 2359304 | tf_op jit(solution)/shard_map/ppermute | solution.py:549
  11.4 44.6 %collective-permute-start.3 = (bf16[32,3072]{1,0:T(8,128)(2,1)S(1)}, bf16[32,3072]{1,0:T(8,128)(2,1)S(1)}, u32[]{:S(2)}, u32[]{:S(2)}) collective-permute-start(bf16[32,3072]{1,0:T(8,128)(2,1)S(1)} %dynamic-slice_bitcast_fusion.8), channel_id=1, source_target_pairs={{0,6},{1,7},{2,4},{3,5},{4,2},{5,3},{6,0},{7,1},{8,14},{9,15},{10,... | collective-permute-start | bytes 589832 | tf_op jit(solution)/shard_map/ppermute | solution.py:549
  16.1 39.9 %collective-permute-start.2 = (bf16[32,3072]{1,0:T(8,128)(2,1)S(1)}, bf16[32,3072]{1,0:T(8,128)(2,1)S(1)}, u32[]{:S(2)}, u32[]{:S(2)}) collective-permute-start(bf16[32,3072]{1,0:T(8,128)(2,1)S(1)} %dynamic-slice_bitcast_fusion.8), channel_id=1, source_target_pairs={{0,4},{1,5},{2,6},{3,7},{4,0},{5,1},{6,2},{7,3},{8,12},{9,13},{10,... | collective-permute-start | bytes 589832 | tf_op jit(solution)/shard_map/ppermute | solution.py:549
  16.1 39.9 %collective-permute-start.1 = (bf16[32,3072]{1,0:T(8,128)(2,1)S(1)}, bf16[32,3072]{1,0:T(8,128)(2,1)S(1)}, u32[]{:S(2)}, u32[]{:S(2)}) collective-permute-start(bf16[32,3072]{1,0:T(8,128)(2,1)S(1)} %dynamic-slice_bitcast_fusion.8), channel_id=1, source_target_pairs={{0,2},{1,3},{2,0},{3,1},{4,6},{5,7},{6,4},{7,5},{8,10},{9,11},{10,... | collective-permute-start | bytes 589832 | tf_op jit(solution)/shard_map/ppermute | solution.py:549
  56.1 28.5 %collective-permute-start.4 = (bf16[3,32,3072]{2,1,0:T(8,128)(2,1)S(1)}, bf16[3,32,3072]{2,1,0:T(8,128)(2,1)S(1)}, u32[]{:S(2)}, u32[]{:S(2)}) collective-permute-start(bf16[3,32,3072]{2,1,0:T(8,128)(2,1)S(1)} %pad_maximum_fusion.1.refs_2_), channel_id=1, source_target_pairs={{0,8},{8,0},{16,24},{24,16},{1,9},{9,1},{17,25},{25,17},{2,10},{10... | collective-permute-start | bytes 1769480 | tf_op jit(solution)/shard_map/ppermute | solution.py:549
  57.6 26.9 %collective-permute-start.5 = (bf16[3,32,3072]{2,1,0:T(8,128)(2,1)S(1)}, bf16[3,32,3072]{2,1,0:T(8,128)(2,1)S(1)}, u32[]{:S(2)}, u32[]{:S(2)}) collective-permute-start(bf16[3,32,3072]{2,1,0:T(8,128)(2,1)S(1)} %pad_maximum_fusion.1.refs_2_), channel_id=1, source_target_pairs={{0,16},{8,24},{16,0},{24,8},{1,17},{9,25},{17,1},{25,9},{2,18},{10... | collective-permute-start | bytes 1769480 | tf_op jit(solution)/shard_map/ppermute | solution.py:549
  59.2 48.1 %collective-permute-start.6 = (bf16[3,32,3072]{2,1,0:T(8,128)(2,1)S(1)}, bf16[3,32,3072]{2,1,0:T(8,128)(2,1)}, u32[]{:S(2)}, u32[]{:S(2)}) collective-permute-start(bf16[3,32,3072]{2,1,0:T(8,128)(2,1)S(1)} %pad_maximum_fusion.1.refs_2_), channel_id=1, source_target_pairs={{0,24},{8,16},{16,8},{24,0},{1,25},{9,17},{17,9},{25,1},{2,26},{10... | collective-permute-start | bytes 1769480 | tf_op jit(solution)/shard_map/ppermute | solution.py:549
  59.7 51.3 %collective-permute-start.7 = (bf16[3,32,3072]{2,1,0:T(8,128)(2,1)S(1)}, bf16[3,32,3072]{2,1,0:T(8,128)(2,1)}, u32[]{:S(2)}, u32[]{:S(2)}) collective-permute-start(bf16[3,32,3072]{2,1,0:T(8,128)(2,1)S(1)} %pad_maximum_fusion.1.refs_2_), channel_id=1, source_target_pairs={{0,1},{1,0},{2,3},{3,2},{4,5},{5,4},{6,7},{7,6},{8,9},{9,8},{10,11... | collective-permute-start | bytes 1769480 | tf_op jit(solution)/shard_map/ppermute | solution.py:549
  84.5 26.5 %collective-permute-start.8 = (bf16[3,32,3072]{2,1,0:T(8,128)(2,1)S(1)}, bf16[3,32,3072]{2,1,0:T(8,128)(2,1)}, u32[]{:S(2)}, u32[]{:S(2)}) collective-permute-start(bf16[3,32,3072]{2,1,0:T(8,128)(2,1)S(1)} %collective-permute-done.4.refs_3_), channel_id=1, source_target_pairs={{0,1},{1,0},{2,3},{3,2},{4,5},{5,4},{6,7},{7,6},{8,9},{9,8},{10,11... | collective-permute-start | bytes 1769480 | tf_op jit(solution)/shard_map/ppermute | solution.py:549
  84.5 26.5 %collective-permute-start.9 = (bf16[3,32,3072]{2,1,0:T(8,128)(2,1)S(1)}, bf16[3,32,3072]{2,1,0:T(8,128)(2,1)}, u32[]{:S(2)}, u32[]{:S(2)}) collective-permute-start(bf16[3,32,3072]{2,1,0:T(8,128)(2,1)S(1)} %collective-permute-done.5.refs_4_), channel_id=1, source_target_pairs={{0,1},{1,0},{2,3},{3,2},{4,5},{5,4},{6,7},{7,6},{8,9},{9,8},{10,11... | collective-permute-start | bytes 1769480 | tf_op jit(solution)/shard_map/ppermute | solution.py:549
  131.1 26.8 %collective-permute-start.12 = (bf16[2,256,512]{2,1,0:T(8,128)(2,1)S(1)}, bf16[2,256,512]{2,1,0:T(8,128)(2,1)S(1)}, u32[]{:S(2)}, u32[]{:S(2)}) collective-permute-start(bf16[2,256,512]{2,1,0:T(8,128)(2,1)S(1)} %pad_maximum_fusion.3), channel_id=1, source_target_pairs={{0,16},{8,24},{16,0},{24,8},{1,17},{9,25},{17,1},{25,9},{2,18},{10... | collective-permute-start | bytes 1572872 | tf_op jit(solution)/shard_map/ppermute | solution.py:549
  131.4 47.5 %collective-permute-start.13 = (bf16[2,256,512]{2,1,0:T(8,128)(2,1)S(1)}, bf16[2,256,512]{2,1,0:T(8,128)(2,1)S(1)}, u32[]{:S(2)}, u32[]{:S(2)}) collective-permute-start(bf16[2,256,512]{2,1,0:T(8,128)(2,1)S(1)} %pad_maximum_fusion.3), channel_id=1, source_target_pairs={{0,24},{8,16},{16,8},{24,0},{1,25},{9,17},{17,9},{25,1},{2,26},{10... | collective-permute-start | bytes 1572872 | tf_op jit(solution)/shard_map/ppermute | solution.py:549
  139.3 62.3 %collective-permute-start.14 = (bf16[2,256,512]{2,1,0:T(8,128)(2,1)S(1)}, bf16[2,256,512]{2,1,0:T(8,128)(2,1)S(1)}, u32[]{:S(2)}, u32[]{:S(2)}) collective-permute-start(bf16[2,256,512]{2,1,0:T(8,128)(2,1)S(1)} %pad_maximum_fusion.4), channel_id=1, source_target_pairs={{0,8},{8,0},{16,24},{24,16},{1,9},{9,1},{17,25},{25,17},{2,10},{10... | collective-permute-start | bytes 1572872 | tf_op jit(solution)/shard_map/ppermute | solution.py:549
  139.8 61.7 %collective-permute-start.15 = (bf16[2,256,512]{2,1,0:T(8,128)(2,1)S(1)}, bf16[2,256,512]{2,1,0:T(8,128)(2,1)S(1)}, u32[]{:S(2)}, u32[]{:S(2)}) collective-permute-start(bf16[2,256,512]{2,1,0:T(8,128)(2,1)S(1)} %pad_maximum_fusion.4), channel_id=1, source_target_pairs={{0,16},{8,24},{16,0},{24,8},{1,17},{9,25},{17,1},{25,9},{2,18},{10... | collective-permute-start | bytes 1572872 | tf_op jit(solution)/shard_map/ppermute | solution.py:549
  156.6 59.0 %collective-permute-start.16 = (bf16[2,256,512]{2,1,0:T(8,128)(2,1)S(1)}, bf16[2,256,512]{2,1,0:T(8,128)(2,1)S(1)}, u32[]{:S(2)}, u32[]{:S(2)}) collective-permute-start(bf16[2,256,512]{2,1,0:T(8,128)(2,1)S(1)} %pad_maximum_fusion.4), channel_id=1, source_target_pairs={{0,24},{8,16},{16,8},{24,0},{1,25},{9,17},{17,9},{25,1},{2,26},{10... | collective-permute-start | bytes 1572872 | tf_op jit(solution)/shard_map/ppermute | solution.py:549
  267.3 42.3 %collective-permute-start.19 = (bf16[2,256,512]{2,1,0:T(8,128)(2,1)S(1)}, bf16[2,256,512]{2,1,0:T(8,128)(2,1)}, u32[]{:S(2)}, u32[]{:S(2)}) collective-permute-start(bf16[2,256,512]{2,1,0:T(8,128)(2,1)S(1)} %pad_maximum_fusion.5), channel_id=1, source_target_pairs={{0,24},{8,16},{16,8},{24,0},{1,25},{9,17},{17,9},{25,1},{2,26},{10... | collective-permute-start | bytes 1572872 | tf_op jit(solution)/shard_map/ppermute | solution.py:549
  270.4 50.3 %collective-permute-start.20 = (bf16[2,256,512]{2,1,0:T(8,128)(2,1)S(1)}, bf16[2,256,512]{2,1,0:T(8,128)(2,1)S(1)}, u32[]{:S(2)}, u32[]{:S(2)}) collective-permute-start(bf16[2,256,512]{2,1,0:T(8,128)(2,1)S(1)} %pad_maximum_fusion.6), channel_id=1, source_target_pairs={{0,8},{8,0},{16,24},{24,16},{1,9},{9,1},{17,25},{25,17},{2,10},{10... | collective-permute-start | bytes 1572872 | tf_op jit(solution)/shard_map/ppermute | solution.py:549
  271.5 49.2 %collective-permute-start.21 = (bf16[2,256,512]{2,1,0:T(8,128)(2,1)S(1)}, bf16[2,256,512]{2,1,0:T(8,128)(2,1)S(1)}, u32[]{:S(2)}, u32[]{:S(2)}) collective-permute-start(bf16[2,256,512]{2,1,0:T(8,128)(2,1)S(1)} %pad_maximum_fusion.6), channel_id=1, source_target_pairs={{0,16},{8,24},{16,0},{24,8},{1,17},{9,25},{17,1},{25,9},{2,18},{10... | collective-permute-start | bytes 1572872 | tf_op jit(solution)/shard_map/ppermute | solution.py:549
  287.6 50.9 %collective-permute-start.22 = (bf16[2,256,512]{2,1,0:T(8,128)(2,1)S(1)}, bf16[2,256,512]{2,1,0:T(8,128)(2,1)S(1)}, u32[]{:S(2)}, u32[]{:S(2)}) collective-permute-start(bf16[2,256,512]{2,1,0:T(8,128)(2,1)S(1)} %pad_maximum_fusion.6), channel_id=1, source_target_pairs={{0,24},{8,16},{16,8},{24,0},{1,25},{9,17},{17,9},{25,1},{2,26},{10... | collective-permute-start | bytes 1572872 | tf_op jit(solution)/shard_map/ppermute | solution.py:549
  435.1 327.4 %reduce-scatter.5.cloned.1.call-start = ((), (), s32[]{:S(2)}) async-start(), calls=%async_computation.5 | async-start | bytes 14155776 | tf_op jit(solution)/shard_map/reduce_scatter | solution.py:953
  454.9 37.9 %collective-permute-start.23 = (bf16[4,128,3072]{2,1,0:T(8,128)(2,1)}, bf16[4,128,3072]{2,1,0:T(8,128)(2,1)S(1)}, u32[]{:S(2)}, u32[]{:S(2)}) collective-permute-start(bf16[4,128,3072]{2,1,0:T(8,128)(2,1)} %get-tuple-element.229), channel_id=1, source_target_pairs={{0,1},{1,0},{2,3},{3,2},{4,5},{5,4},{6,7},{7,6},{8,9},{9,8},{10,11... | collective-permute-start | bytes 9437192 | tf_op jit(solution)/shard_map/ppermute | solution.py:549
  472.3 28.2 %collective-permute-start.25 = (bf16[2,256,512]{2,1,0:T(8,128)(2,1)}, bf16[2,256,512]{2,1,0:T(8,128)(2,1)}, u32[]{:S(2)}, u32[]{:S(2)}) collective-permute-start(bf16[2,256,512]{2,1,0:T(8,128)(2,1)} %get-tuple-element.235), channel_id=1, source_target_pairs={{0,16},{8,24},{16,0},{24,8},{1,17},{9,25},{17,1},{25,9},{2,18},{10... | collective-permute-start | bytes 1572872 | tf_op jit(solution)/shard_map/ppermute | solution.py:549
  472.8 28.1 %collective-permute-start.26 = (bf16[2,256,512]{2,1,0:T(8,128)(2,1)}, bf16[2,256,512]{2,1,0:T(8,128)(2,1)}, u32[]{:S(2)}, u32[]{:S(2)}) collective-permute-start(bf16[2,256,512]{2,1,0:T(8,128)(2,1)} %get-tuple-element.236), channel_id=1, source_target_pairs={{0,24},{8,16},{16,8},{24,0},{1,25},{9,17},{17,9},{25,1},{2,26},{10... | collective-permute-start | bytes 1572872 | tf_op jit(solution)/shard_map/ppermute | solution.py:549
  493.1 27.9 %collective-permute-start.29 = (bf16[2,256,512]{2,1,0:T(8,128)(2,1)}, bf16[2,256,512]{2,1,0:T(8,128)(2,1)}, u32[]{:S(2)}, u32[]{:S(2)}) collective-permute-start(bf16[2,256,512]{2,1,0:T(8,128)(2,1)} %get-tuple-element.240), channel_id=1, source_target_pairs={{0,24},{8,16},{16,8},{24,0},{1,25},{9,17},{17,9},{25,1},{2,26},{10... | collective-permute-start | bytes 1572872 | tf_op jit(solution)/shard_map/ppermute | solution.py:549
  500.6 38.8 %collective-permute-start.30 = (bf16[4,2,32,1536]{3,2,1,0:T(8,128)(2,1)}, bf16[4,2,32,1536]{3,2,1,0:T(8,128)(2,1)S(1)}, u32[]{:S(2)}, u32[]{:S(2)}) collective-permute-start(bf16[4,2,32,1536]{3,2,1,0:T(8,128)(2,1)} %get-tuple-element.245), channel_id=1, source_target_pairs={{0,8},{8,0},{16,24},{24,16},{1,9},{9,1},{17,25},{25,17},{2,10},{10... | collective-permute-start | bytes 2359304 | tf_op jit(solution)/shard_map/ppermute | solution.py:549
  500.9 38.5 %collective-permute-start.31 = (bf16[4,2,32,1536]{3,2,1,0:T(8,128)(2,1)}, bf16[4,2,32,1536]{3,2,1,0:T(8,128)(2,1)S(1)}, u32[]{:S(2)}, u32[]{:S(2)}) collective-permute-start(bf16[4,2,32,1536]{3,2,1,0:T(8,128)(2,1)} %get-tuple-element.247), channel_id=1, source_target_pairs={{0,16},{8,24},{16,0},{24,8},{1,17},{9,25},{17,1},{25,9},{2,18},{10... | collective-permute-start | bytes 2359304 | tf_op jit(solution)/shard_map/ppermute | solution.py:549
  597.0 44.1 %collective-permute-start.35 = (bf16[4,2,32,1536]{3,2,1,0:T(8,128)(2,1)S(1)}, bf16[4,2,32,1536]{3,2,1,0:T(8,128)(2,1)S(1)}, u32[]{:S(2)}, u32[]{:S(2)}) collective-permute-start(bf16[4,2,32,1536]{3,2,1,0:T(8,128)(2,1)S(1)} %copy-done.60), channel_id=1, source_target_pairs={{0,8},{8,0},{16,24},{24,16},{1,9},{9,1},{17,25},{25,17},{2,10},{10... | collective-permute-start | bytes 2359304 | tf_op jit(solution)/shard_map/ppermute | solution.py:549
  597.9 43.2 %collective-permute-start.36 = (bf16[4,2,32,1536]{3,2,1,0:T(8,128)(2,1)S(1)}, bf16[4,2,32,1536]{3,2,1,0:T(8,128)(2,1)S(1)}, u32[]{:S(2)}, u32[]{:S(2)}) collective-permute-start(bf16[4,2,32,1536]{3,2,1,0:T(8,128)(2,1)S(1)} %copy-done.59), channel_id=1, source_target_pairs={{0,16},{8,24},{16,0},{24,8},{1,17},{9,25},{17,1},{25,9},{2,18},{10... | collective-permute-start | bytes 2359304 | tf_op jit(solution)/shard_map/ppermute | solution.py:549
  599.7 31.8 %collective-permute-start.44 = (bf16[32,3072]{1,0:T(8,128)(2,1)S(1)}, bf16[32,3072]{1,0:T(8,128)(2,1)S(1)}, u32[]{:S(2)}, u32[]{:S(2)}) collective-permute-start(bf16[32,3072]{1,0:T(8,128)(2,1)S(1)} %copy-done.80), channel_id=1, source_target_pairs={{0,4},{1,5},{2,6},{3,7},{4,0},{5,1},{6,2},{7,3},{8,12},{9,13},{10,... | collective-permute-start | bytes 589832 | tf_op jit(solution)/shard_map/ppermute | solution.py:549
  601.7 30.4 %collective-permute-start.43 = (bf16[32,3072]{1,0:T(8,128)(2,1)S(1)}, bf16[32,3072]{1,0:T(8,128)(2,1)S(1)}, u32[]{:S(2)}, u32[]{:S(2)}) collective-permute-start(bf16[32,3072]{1,0:T(8,128)(2,1)S(1)} %copy-done.79), channel_id=1, source_target_pairs={{0,2},{1,3},{2,0},{3,1},{4,6},{5,7},{6,4},{7,5},{8,10},{9,11},{10,... | collective-permute-start | bytes 589832 | tf_op jit(solution)/shard_map/ppermute | solution.py:549
  633.1 70.0 %collective-permute-start.39 = (bf16[4,128,3072]{2,1,0:T(8,128)(2,1)}, bf16[4,128,3072]{2,1,0:T(8,128)(2,1)S(1)}, u32[]{:S(2)}, u32[]{:S(2)}) collective-permute-start(bf16[4,128,3072]{2,1,0:T(8,128)(2,1)} %get-tuple-element.292), channel_id=1, source_target_pairs={{0,1},{1,0},{2,3},{3,2},{4,5},{5,4},{6,7},{7,6},{8,9},{9,8},{10,11... | collective-permute-start | bytes 9437192 | tf_op jit(solution)/shard_map/ppermute | solution.py:549
  663.7 38.3 %collective-permute-start.49 = (bf16[2,256,512]{2,1,0:T(8,128)(2,1)}, bf16[2,256,512]{2,1,0:T(8,128)(2,1)S(1)}, u32[]{:S(2)}, u32[]{:S(2)}) collective-permute-start(bf16[2,256,512]{2,1,0:T(8,128)(2,1)} %get-tuple-element.310), channel_id=1, source_target_pairs={{0,8},{8,0},{16,24},{24,16},{1,9},{9,1},{17,25},{25,17},{2,10},{10... | collective-permute-start | bytes 1572872 | tf_op jit(solution)/shard_map/ppermute | solution.py:549
  669.8 29.6 %collective-permute-start.47 = (bf16[32,3072]{1,0:T(8,128)(2,1)}, bf16[32,3072]{1,0:T(8,128)(2,1)S(1)}, u32[]{:S(2)}, u32[]{:S(2)}) collective-permute-start(bf16[32,3072]{1,0:T(8,128)(2,1)} %get-tuple-element.306), channel_id=1, source_target_pairs={{0,4},{1,5},{2,6},{3,7},{4,0},{5,1},{6,2},{7,3},{8,12},{9,13},{10,... | collective-permute-start | bytes 589832 | tf_op jit(solution)/shard_map/ppermute | solution.py:549
  669.9 30.8 %collective-permute-start.46 = (bf16[32,3072]{1,0:T(8,128)(2,1)}, bf16[32,3072]{1,0:T(8,128)(2,1)S(1)}, u32[]{:S(2)}, u32[]{:S(2)}) collective-permute-start(bf16[32,3072]{1,0:T(8,128)(2,1)} %get-tuple-element.305), channel_id=1, source_target_pairs={{0,2},{1,3},{2,0},{3,1},{4,6},{5,7},{6,4},{7,5},{8,10},{9,11},{10,... | collective-permute-start | bytes 589832 | tf_op jit(solution)/shard_map/ppermute | solution.py:549
  703.1 32.1 %collective-permute-start.54 = (bf16[2,256,512]{2,1,0:T(8,128)(2,1)}, bf16[2,256,512]{2,1,0:T(8,128)(2,1)}, u32[]{:S(2)}, u32[]{:S(2)}) collective-permute-start(bf16[2,256,512]{2,1,0:T(8,128)(2,1)} %get-tuple-element.316), channel_id=1, source_target_pairs={{0,24},{8,16},{16,8},{24,0},{1,25},{9,17},{17,9},{25,1},{2,26},{10... | collective-permute-start | bytes 1572872 | tf_op jit(solution)/shard_map/ppermute | solution.py:549
  753.4 26.3 %collective-permute-start.65 = (bf16[4,128,3072]{2,1,0:T(8,128)(2,1)}, bf16[4,128,3072]{2,1,0:T(8,128)(2,1)S(1)}, u32[]{:S(2)}, u32[]{:S(2)}) collective-permute-start(bf16[4,128,3072]{2,1,0:T(8,128)(2,1)} %get-tuple-element.347), channel_id=1, source_target_pairs={{0,1},{1,0},{2,3},{3,2},{4,5},{5,4},{6,7},{7,6},{8,9},{9,8},{10,11... | collective-permute-start | bytes 9437192 | tf_op jit(solution)/shard_map/ppermute | solution.py:549
  762.0 27.1 %collective-permute-start.56 = (f32[2,2,1536]{2,1,0:T(2,128)S(1)}, f32[2,2,1536]{2,1,0:T(2,128)S(1)}, u32[]{:S(2)}, u32[]{:S(2)}) collective-permute-start(f32[2,2,1536]{2,1,0:T(2,128)S(1)} %dynamic-slice_bitcast_fusion.9), channel_id=1, source_target_pairs={{0,2},{1,3},{2,0},{3,1},{4,6},{5,7},{6,4},{7,5},{8,10},{9,11},{10,... | collective-permute-start | bytes 73736 | tf_op jit(solution)/shard_map/ppermute | solution.py:549
  789.2 50.1 %collective-permute-start.57 = (f32[2,1536]{1,0:T(2,128)S(1)}, f32[2,1536]{1,0:T(2,128)S(1)}, u32[]{:S(2)}, u32[]{:S(2)}) collective-permute-start(f32[2,1536]{1,0:T(2,128)S(1)} %dynamic-slice_bitcast_fusion.10), channel_id=1, source_target_pairs={{0,1},{1,0},{2,3},{3,2},{4,5},{5,4},{6,7},{7,6},{8,9},{9,8},{10,11... | collective-permute-start | bytes 36872 | tf_op jit(solution)/shard_map/ppermute | solution.py:549
  805.5 27.0 %collective-permute-start.71 = (bf16[4,2,32,1536]{3,2,1,0:T(8,128)(2,1)}, bf16[4,2,32,1536]{3,2,1,0:T(8,128)(2,1)S(1)}, u32[]{:S(2)}, u32[]{:S(2)}) collective-permute-start(bf16[4,2,32,1536]{3,2,1,0:T(8,128)(2,1)} %get-tuple-element.363), channel_id=1, source_target_pairs={{0,8},{8,0},{16,24},{24,16},{1,9},{9,1},{17,25},{25,17},{2,10},{10... | collective-permute-start | bytes 2359304 | tf_op jit(solution)/shard_map/ppermute | solution.py:549
  813.9 63.4 %collective-permute-start.60 = (bf16[32,12288]{1,0:T(8,128)(2,1)S(1)}, bf16[32,12288]{1,0:T(8,128)(2,1)S(1)}, u32[]{:S(2)}, u32[]{:S(2)}) collective-permute-start(bf16[32,12288]{1,0:T(8,128)(2,1)S(1)} %copy-done.5), channel_id=1, source_target_pairs={{0,8},{8,0},{16,24},{24,16},{1,9},{9,1},{17,25},{25,17},{2,10},{10... | collective-permute-start | bytes 2359304 | tf_op jit(solution)/shard_map/ppermute | solution.py:549
  815.6 61.8 %collective-permute-start.61 = (bf16[32,12288]{1,0:T(8,128)(2,1)S(1)}, bf16[32,12288]{1,0:T(8,128)(2,1)S(1)}, u32[]{:S(2)}, u32[]{:S(2)}) collective-permute-start(bf16[32,12288]{1,0:T(8,128)(2,1)S(1)} %copy-done.5), channel_id=1, source_target_pairs={{0,16},{8,24},{16,0},{24,8},{1,17},{9,25},{17,1},{25,9},{2,18},{10... | collective-permute-start | bytes 2359304 | tf_op jit(solution)/shard_map/ppermute | solution.py:549
  846.2 31.2 %collective-permute-start.62 = (bf16[32,12288]{1,0:T(8,128)(2,1)S(1)}, bf16[32,12288]{1,0:T(8,128)(2,1)S(1)}, u32[]{:S(2)}, u32[]{:S(2)}) collective-permute-start(bf16[32,12288]{1,0:T(8,128)(2,1)S(1)} %copy-done.5), channel_id=1, source_target_pairs={{0,24},{8,16},{16,8},{24,0},{1,25},{9,17},{17,9},{25,1},{2,26},{10... | collective-permute-start | bytes 2359304 | tf_op jit(solution)/shard_map/ppermute | solution.py:549
  884.9 45.8 %collective-permute-start.84 = (bf16[32,9216]{1,0:T(8,128)(2,1)S(1)}, bf16[32,9216]{1,0:T(8,128)(2,1)S(1)}, u32[]{:S(2)}, u32[]{:S(2)}) collective-permute-start(bf16[32,9216]{1,0:T(8,128)(2,1)S(1)} %pad_maximum_fusion.2.refs_0_), channel_id=1, source_target_pairs={{0,8},{8,0},{16,24},{24,16},{1,9},{9,1},{17,25},{25,17},{2,10},{10... | collective-permute-start | bytes 1769480 | tf_op jit(solution)/shard_map/ppermute | solution.py:549
  887.4 43.3 %collective-permute-start.85 = (bf16[32,9216]{1,0:T(8,128)(2,1)S(1)}, bf16[32,9216]{1,0:T(8,128)(2,1)S(1)}, u32[]{:S(2)}, u32[]{:S(2)}) collective-permute-start(bf16[32,9216]{1,0:T(8,128)(2,1)S(1)} %pad_maximum_fusion.2.refs_0_), channel_id=1, source_target_pairs={{0,16},{8,24},{16,0},{24,8},{1,17},{9,25},{17,1},{25,9},{2,18},{10... | collective-permute-start | bytes 1769480 | tf_op jit(solution)/shard_map/ppermute | solution.py:549
  898.7 32.1 %collective-permute-start.86 = (bf16[32,9216]{1,0:T(8,128)(2,1)S(1)}, bf16[32,9216]{1,0:T(8,128)(2,1)S(1)}, u32[]{:S(2)}, u32[]{:S(2)}) collective-permute-start(bf16[32,9216]{1,0:T(8,128)(2,1)S(1)} %pad_maximum_fusion.2.refs_0_), channel_id=1, source_target_pairs={{0,24},{8,16},{16,8},{24,0},{1,25},{9,17},{17,9},{25,1},{2,26},{10... | collective-permute-start | bytes 1769480 | tf_op jit(solution)/shard_map/ppermute | solution.py:549
  (134 other events, 1609.4 us)
Sparse Core Ops, SparseCore 0:
  11.5 224.7 all-gather.4
  239.7 148.0 all-gather.6
  435.2 126.0 reduce-scatter.2
  573.1 152.1 reduce-scatter.4

commit v3 on v2

--- a/solution.py
+++ b/solution.py
@@ -367,21 +367,32 @@
             acc_ref[...] = jnp.zeros_like(acc_ref)
             drb_ref[...] = jnp.sum(branch.astype(F32), 0, keepdims=True)
 
+    def hidden_part(columns):
+        grad_active = dot_nt(gb_scr[...], w_ref[columns, width:])
+        v = hidden_ref[:, columns].astype(F32)
+        square = v * v
+        t = jnp.tanh(CURVE * v * (1.0 + CUBIC * square))
+        half = 0.5 + 0.5 * t
+        slope = half + 0.5 * v * (1.0 - t * t) * (CURVE * (1.0 + 3 * CUBIC * square))
+        grad_hidden = (grad_active * slope).astype(BF16)
+        deb_ref[:, columns] = jnp.sum(grad_hidden.astype(F32), 0, keepdims=True)
+        acc_ref[...] += dot_nt(grad_hidden, w_ref[:, columns])
+        return (v * half).astype(BF16), grad_hidden
+
+    cut = width // 2
+    pieces = [slice(start, start + cut) for start in range(0, width, cut)]
+
+    if not final:
+        for columns in pieces:
+            active, grad_hidden = hidden_part(columns)
+            dw_refs[0][columns, width:] = dot_tn(active, gb_scr[...]).astype(BF16)
+            dw_refs[0][:, columns] = dot(sec_scr[...], grad_hidden).astype(BF16)
+        return
+
     @pl.when((step % 2 == 0) & (step < 2 * slabs))
     def _():
-        cut = width // 2
-        for start in range(0, width, cut):
-            columns = slice(start, start + cut)
-            grad_active = dot_nt(gb_scr[...], w_ref[columns, width:])
-            v = hidden_ref[:, columns].astype(F32)
-            square = v * v
-            t = jnp.tanh(CURVE * v * (1.0 + CUBIC * square))
-            half = 0.5 + 0.5 * t
-            slope = half + 0.5 * v * (1.0 - t * t) * (CURVE * (1.0 + 3 * CUBIC * square))
-            grad_hidden = (grad_active * slope).astype(BF16)
-            act_scr[:, columns] = (v * half).astype(BF16)
-            deb_ref[:, columns] = jnp.sum(grad_hidden.astype(F32), 0, keepdims=True)
-            acc_ref[...] += dot_nt(grad_hidden, w_ref[:, columns])
+        for columns in pieces:
+            act_scr[:, columns], grad_hidden = hidden_part(columns)
             put_rows(
                 [ref.at[..., columns] for ref in dw_refs],
                 dot(sec_scr[...], grad_hidden).astype(BF16),
@@ -392,8 +403,6 @@
     def _():
         put_rows(dw_refs, dot_tn(act_scr[...], gb_scr[...]).astype(BF16), core)
 
-    if not final:
-        return
 
     @pl.when(step == 2 * slabs)
     def _():
@@ -418,9 +427,10 @@
     row = whole((1, width))
     small = jax.ShapeDtypeStruct((1, width), F32)
     base = EARLY if final else 0
-    slab = lambda j: base + jnp.minimum(j // 2, half - 1)
+    each = 2 if final else 1
+    slab = lambda j: base + jnp.minimum(j // each, half - 1)
     blocks = 2 * half + 1 if final else 2 * half
-    dw_specs, dw_shapes = grad_outs(holders, width, blocks * width, width, apart)
+    dw_specs, dw_shapes = grad_outs(holders, width, blocks * width, 2 * width // each, apart)
     square = whole((rows, width))
     in_specs = [
         pl.BlockSpec((rows, width), lambda j: (0, slab(j))),
@@ -454,7 +464,7 @@
         out_shape += [total, small]
     return pl.pallas_call(
         functools.partial(feed_pull_kernel, bool(final), half, len(attended), len(dw_specs)),
-        grid=(blocks,),
+        grid=(blocks if final else half,),
         in_specs=[pl.BlockSpec(memory_space=pltpu.SMEM), square]
         + [whole(piece.shape) for piece in attended]
         + in_specs,
@@ -500,14 +510,14 @@
         out_ref[...] = gm_ref[...] + term
 
 
-def qkv_backward(holders, core, dqs, conts, sums, normed, stream, grad_middle, vec, weights):
+def qkv_backward(holders, core, dqs, conts, sums, normed, stream, grad_middle, vec, weights, apart):
     rows, width = stream.shape
     parts = len(dqs)
     block = width // parts
     wq, place = weights
     small = jax.ShapeDtypeStruct((1, width), F32)
     flat = [piece for part in sums for piece in part]
-    dw_specs, dw_shapes = grad_outs(holders, width, 3 * width, block, True)
+    dw_specs, dw_shapes = grad_outs(holders, width, 3 * width, block, apart)
     return pl.pallas_call(
         functools.partial(qkv_pull_kernel, parts, len(sums[0]), len(dw_specs)),
         grid=(3 * parts,),
@@ -972,12 +982,16 @@
         conts[-1] = together(conts[-1], [late[layer]])
         if not layer:
             upper = jnp.concatenate([early[1], late[1].finish(), last[1].finish()], 1)
-            conts[-1], upper = sync((conts[-1], upper))
+            conts[-1], upper, rows_early = sync((conts[-1], upper, spread_rows(early[0])))
+            early[0] = added(*from_each(rows_early))
             upper = to_each(upper)
-        dwq_mine, dwq_other, grad_stream, dqb, dfg, dfs = qkv_backward(
-            n_wa, core, dqs, conts, sums, normed, start, grad_middle, vecs[layer], wq
+        *dwq, grad_stream, dqb, dfg, dfs = qkv_backward(
+            n_wa, core, dqs, conts, sums, normed, start, grad_middle, vecs[layer], wq, bool(layer)
         )
-        last[layer] = Reduction((dwq_mine, dwq_other))
+        if layer:
+            last[layer] = Reduction(dwq)
+        else:
+            last[layer] = lax.psum_scatter(dwq[0], "wa", scatter_dimension=0, tiled=True)
         dqb = jnp.concatenate([dqb[:, :width], dqb[:, 2 * width :]], 1)
         deb = jnp.concatenate([deb_low, deb_high], 1)
         deb = deb.reshape(SLABS, n_wa, span).transpose(1, 0, 2)
@@ -994,15 +1008,14 @@
     for step in [1 << bit for bit in range(n_tok.bit_length() - 1)]:
         small = small + trade(small, "tok", step)
 
-    spread = together(spread_rows(early[0]), [late[0], last[0]])
-    early[0] = added(*from_each(spread))
-    early[0] = together(early[0], [late[0], last[0]])
     lower = jnp.concatenate([early[0], late[0].finish()], 1)
-    upper, lower = together((upper, lower), [last[0]])
+    lower, last[0] = sync((lower, spread_rows(last[0])))
+    last[0] = added(*from_each(last[0]))
+    lower = to_each(lower)
     feeds = feed_out(upper, width, me, 1, [])
     qkvs = qkv_out(upper, 3 * width, me, 1, [])
-    feeds = feed_out(to_each(lower), width, me, 0, feeds)
-    qkvs = qkv_out(to_each(last[0].finish()), 3 * width, me, 0, [qkvs])
+    feeds = feed_out(lower, width, me, 0, feeds)
+    qkvs = qkv_out(to_each(last[0]), 3 * width, me, 0, [qkvs])
     mixes, expands, reduces = [
         block.reshape(LAYERS, -1, width) if place != 1 else block.reshape(LAYERS, span, -1)
         for place, block in enumerate(feeds)

time: 949 us -> 908 us (0.957)
  Pallas kernels: 358 us -> 335 us
  starting transfers between devices: 94.6 us -> 82.4 us
    ppermute x87 -> x82, waiting for transfers between devices: 344 us -> 322 us  [trade(): lax.ppermute(block, axis, [(i, i ^ bits) for i in range(lax.axis_size(axi...]
    reduce_scatter x2, waiting for transfers between devices: 0.02 us -> 15.5 us  [local(): lax.psum_scatter(dw_early, 'wa', scatter_dimension=0, tiled=True)]
    pallas_call x4, Pallas kernels: 97.6 us -> 84.2 us  [feed_backward(): pl.pallas_call(functools.partial(feed_pull_kernel, bool(final), half, len...]
    ppermute x87 -> x82, starting transfers between devices: 94.5 us -> 82.2 us  [trade(): lax.ppermute(block, axis, [(i, i ^ bits) for i in range(lax.axis_size(axi...]
    pallas_call x8 -> x6, Pallas kernels: 28.4 us -> 21.6 us  [split_sum(): pl.pallas_call(functools.partial(split_kernel, len(sides[0]), lows), grid...]
    unnamed x214 -> x200, local copies, waits for them, and re-layouts: 19.4 us -> 16.2 us
  transfers between devices with their start and end apart: 91 -> 87, of which waited for: 40 -> 36; matrix products, arithmetic and copies ran while one was open for 3% -> 3% of each run, Pallas kernels for 32% -> 30%
where the time goes in v3:
time: 908 us; the launch traced here: 903 us
  waiting for transfers between devices  385 us (42%)
  Pallas kernels  335 us (37%)
  starting transfers between devices  82.4 us (9%)
  blocking collectives  38.9 us (4%)
  local copies, waits for them, and re-layouts  32.3 us (4%)
  between operations  15.3 us (2%)
  other arithmetic  14.3 us (2%)
    ppermute x82, waiting for transfers between devices, trade(): lax.ppermute(block, axis, [(i, i ^ bits) for i in range(lax.axis_size(axi...  322 us
    pallas_call x4, Pallas kernels, feed_backward(): pl.pallas_call(functools.partial(feed_pull_kernel, bool(final), half, len...  84.2 us
    ppermute x82, starting transfers between devices, trade(): lax.ppermute(block, axis, [(i, i ^ bits) for i in range(lax.axis_size(axi...  82.2 us
    pallas_call x4, Pallas kernels, attend_backward(): pl.pallas_call(functools.partial(attend_pull_kernel, pb, len(far)), grid=...  66.4 us
    pallas_call x4, Pallas kernels, attend_forward(): pl.pallas_call(functools.partial(attend_kernel, pb, len(far)), grid=(pair...  43.6 us
    all_gather x1, blocking collectives, local(): small = lax.all_gather(small, 'wa', axis=0, tiled=False)  38.9 us
    all_gather x1, waiting for transfers between devices, local(): last_array = lax.all_gather(rows_last, both, axis=0, tiled=True)  37.7 us
    pallas_call x2, Pallas kernels, qkv_backward(): pl.pallas_call(functools.partial(qkv_pull_kernel, parts, len(sums[0]), le...  36.3 us
  transfers between devices with their start and end apart: 87, of which 36 were waited for; matrix products, arithmetic and copies ran while one was open for 3% of the time, Pallas kernels for 30%

profile of v3, /device:TPU:0, one launch (start us, length us, event | category | flops | bytes accessed | tf_op | source)
XLA Modules:
  0.0 903.4 jit_solution(6419685206660092708)
XLA Ops:
  11.4 4.7 collective-permute-start.3
  16.9 38.9 %all-gather.1 = bf16[8,2,1536]{2,1,0:T(2,128)(2,1)S(1)} all-gather(bf16[1,2,1536]{2,1,0:T(2,128)(2,1)S(1)} %bitcast.217), channel_id=2, replica_groups=mesh['tok'=4,'wa'=8] {'wa'}, dimensions={0}, use_global_device_ids=true | all-gather | bytes 55296 | tf_op jit(solution)/shard_map/all_gather | solution.py:888
  59.8 24.8 %collective-permute-done.4.refs_3_ = bf16[3,32,3072]{2,1,0:T(8,128)(2,1)S(1)} collective-permute-done((bf16[3,32,3072]{2,1,0:T(8,128)(2,1)S(1)}, bf16[3,32,3072]{2,1,0:T(8,128)(2,1)S(1)}, u32[]{:S(2)}, u32[]{:S(2)}) %collective-permute-start.4) | collective-permute-done | bytes 589856 | tf_op jit(solution)/shard_map/ppermute | solution.py:559
  85.1 22.3 %collective-permute-done.6.refs_5_ = bf16[3,32,3072]{2,1,0:T(8,128)(2,1)} collective-permute-done((bf16[3,32,3072]{2,1,0:T(8,128)(2,1)S(1)}, bf16[3,32,3072]{2,1,0:T(8,128)(2,1)}, u32[]{:S(2)}, u32[]{:S(2)}) %collective-permute-start.6) | collective-permute-done | bytes 589856 | tf_op jit(solution)/shard_map/ppermute | solution.py:559
  111.0 5.6 assemble.1
  119.2 9.9 %qkv_forward.2 = (bf16[512,3072]{1,0:T(8,128)(2,1)}, bf16[512,1024]{1,0:T(8,128)(2,1)}) custom-call(f32[512,1024]{1,0:T(8,128)} %maximum_convert_fusion.x_ref.refs_13_, f32[1,13312]{1,0:T(1,128)} %convert_element_type.103.gain_ref.shift_ref.bias_ref.refs_3_.refs_4_.refs_5_.refs_6_.refs_7_.refs_15_, ...), custom_call_target="tpu_custom_call" | custom-call | flops 3221225472 | bytes 16777216 | tf_op jit(solution)/shard_map/qkv_forward/pallas_call | solution.py:81
  140.1 16.4 %collective-permute-done.11.refs_4_ = bf16[2,256,512]{2,1,0:T(8,128)(2,1)S(1)} collective-permute-done((bf16[2,256,512]{2,1,0:T(8,128)(2,1)S(1)}, bf16[2,256,512]{2,1,0:T(8,128)(2,1)S(1)}, u32[]{:S(2)}, u32[]{:S(2)}) %collective-permute-start.11) | collective-permute-done | bytes 524320 | tf_op jit(solution)/shard_map/ppermute | solution.py:559
  157.8 21.1 %collective-permute-done.13.refs_6_ = bf16[2,256,512]{2,1,0:T(8,128)(2,1)S(1)} collective-permute-done((bf16[2,256,512]{2,1,0:T(8,128)(2,1)S(1)}, bf16[2,256,512]{2,1,0:T(8,128)(2,1)S(1)}, u32[]{:S(2)}, u32[]{:S(2)}) %collective-permute-start.13) | collective-permute-done | bytes 524320 | tf_op jit(solution)/shard_map/ppermute | solution.py:559
  179.7 10.8 %attend_forward.4 = (bf16[512,512]{1,0:T(8,128)(2,1)}, f32[8,1,512]{2,1,0:T(1,128)}) custom-call(s32[4]{0:T(128)} %fusion.2.refs_0_, bf16[512,3072]{1,0:T(8,128)(2,1)} %get-tuple-element.178.refs_1_.refs_2_.refs_3_, bf16[512,3072]{1,0:T(8,128)(2,1)} %get-tuple-element.178.refs_1_.refs_2_.refs_3_, ...), custom_call_target="tpu_custom_call" | custom-call | flops 16106127360 | bytes 5242880 | tf_op jit(solution)/shard_map/attend_forward/pallas_call | solution.py:158
  190.6 10.9 %collective-permute-done.14.refs_4_ = bf16[2,256,512]{2,1,0:T(8,128)(2,1)S(1)} collective-permute-done((bf16[2,256,512]{2,1,0:T(8,128)(2,1)S(1)}, bf16[2,256,512]{2,1,0:T(8,128)(2,1)S(1)}, u32[]{:S(2)}, u32[]{:S(2)}) %collective-permute-start.14) | collective-permute-done | bytes 524320 | tf_op jit(solution)/shard_map/ppermute | solution.py:559
  201.5 14.1 %collective-permute-done.16.refs_6_ = bf16[2,256,512]{2,1,0:T(8,128)(2,1)S(1)} collective-permute-done((bf16[2,256,512]{2,1,0:T(8,128)(2,1)S(1)}, bf16[2,256,512]{2,1,0:T(8,128)(2,1)S(1)}, u32[]{:S(2)}, u32[]{:S(2)}) %collective-permute-start.16) | collective-permute-done | bytes 524320 | tf_op jit(solution)/shard_map/ppermute | solution.py:559
  216.4 10.9 %attend_forward.5 = (bf16[512,512]{1,0:T(8,128)(2,1)}, f32[8,1,512]{2,1,0:T(1,128)}) custom-call(s32[4]{0:T(128)} %fusion.2.refs_0_, bf16[512,3072]{1,0:T(8,128)(2,1)} %get-tuple-element.178.refs_1_.refs_2_.refs_3_, bf16[512,3072]{1,0:T(8,128)(2,1)} %get-tuple-element.178.refs_1_.refs_2_.refs_3_, ...), custom_call_target="tpu_custom_call" | custom-call | flops 16106127360 | bytes 5242880 | tf_op jit(solution)/shard_map/attend_forward/pallas_call | solution.py:158
  227.2 9.0 all-gather.5.cloned.1.call-done.refs_2_.refs_8_.w_ref.refs_16_.refs_4_.refs_7_
  236.3 17.6 %feed_forward.2 = (f32[512,1024]{1,0:T(8,128)}, f32[512,1024]{1,0:T(8,128)}, bf16[512,1024]{1,0:T(8,128)(2,1)}, bf16[512,4096]{1,0:T(8,128)(2,1)}) custom-call(f32[512,1024]{1,0:T(8,128)} %maximum_convert_fusion.x_ref.refs_13_, bf16[512,512]{1,0:T(8,128)(2,1)} %get-tuple-element.179.refs_0_.refs_9_, bf16[512,512]{1,0:T(8,128)(2,1)} %get-tuple-element.180.refs_1_.refs_9_, ...), custom_call_target="tpu_custom_call" | custom-call | flops 9663676416 | bytes 31457280 | tf_op jit(solution)/shard_map/feed_forward/pallas_call | solution.py:288
  253.9 9.4 %qkv_forward.3 = (bf16[512,3072]{1,0:T(8,128)(2,1)}, bf16[512,1024]{1,0:T(8,128)(2,1)}) custom-call(f32[512,1024]{1,0:T(8,128)} %get-tuple-element.182.x_ref.refs_13_, f32[1,13312]{1,0:T(1,128)} %convert_element_type.104.gain_ref.shift_ref.bias_ref.refs_3_.refs_4_.refs_5_.refs_6_.refs_7_.refs_15_, ...), custom_call_target="tpu_custom_call" | custom-call | flops 3221225472 | bytes 16777216 | tf_op jit(solution)/shard_map/qkv_forward/pallas_call | solution.py:81
  272.4 15.0 %collective-permute-done.17.refs_4_ = bf16[2,256,512]{2,1,0:T(8,128)(2,1)S(1)} collective-permute-done((bf16[2,256,512]{2,1,0:T(8,128)(2,1)S(1)}, bf16[2,256,512]{2,1,0:T(8,128)(2,1)S(1)}, u32[]{:S(2)}, u32[]{:S(2)}) %collective-permute-start.17) | collective-permute-done | bytes 524320 | tf_op jit(solution)/shard_map/ppermute | solution.py:559
  290.4 19.1 %collective-permute-done.19.refs_6_ = bf16[2,256,512]{2,1,0:T(8,128)(2,1)} collective-permute-done((bf16[2,256,512]{2,1,0:T(8,128)(2,1)S(1)}, bf16[2,256,512]{2,1,0:T(8,128)(2,1)}, u32[]{:S(2)}, u32[]{:S(2)}) %collective-permute-start.19) | collective-permute-done | bytes 524320 | tf_op jit(solution)/shard_map/ppermute | solution.py:559
  309.5 11.0 %attend_forward.6 = (bf16[512,512]{1,0:T(8,128)(2,1)}, f32[8,1,512]{2,1,0:T(1,128)}) custom-call(s32[4]{0:T(128)} %fusion.2.refs_0_, bf16[512,3072]{1,0:T(8,128)(2,1)} %get-tuple-element.183.refs_1_.refs_2_.refs_3_, bf16[512,3072]{1,0:T(8,128)(2,1)} %get-tuple-element.183.refs_1_.refs_2_.refs_3_, ...), custom_call_target="tpu_custom_call" | custom-call | flops 16106127360 | bytes 5242880 | tf_op jit(solution)/shard_map/attend_forward/pallas_call | solution.py:158
  320.6 17.7 %collective-permute-done.22.refs_6_ = bf16[2,256,512]{2,1,0:T(8,128)(2,1)S(1)} collective-permute-done((bf16[2,256,512]{2,1,0:T(8,128)(2,1)S(1)}, bf16[2,256,512]{2,1,0:T(8,128)(2,1)S(1)}, u32[]{:S(2)}, u32[]{:S(2)}) %collective-permute-start.22) | collective-permute-done | bytes 524320 | tf_op jit(solution)/shard_map/ppermute | solution.py:559
  339.1 10.9 %attend_forward.7 = (bf16[512,512]{1,0:T(8,128)(2,1)}, f32[8,1,512]{2,1,0:T(1,128)}) custom-call(s32[4]{0:T(128)} %fusion.2.refs_0_, bf16[512,3072]{1,0:T(8,128)(2,1)} %get-tuple-element.183.refs_1_.refs_2_.refs_3_, bf16[512,3072]{1,0:T(8,128)(2,1)} %get-tuple-element.183.refs_1_.refs_2_.refs_3_, ...), custom_call_target="tpu_custom_call" | custom-call | flops 16106127360 | bytes 5242880 | tf_op jit(solution)/shard_map/attend_forward/pallas_call | solution.py:158
  350.0 37.7 %all-gather.7.cloned.1.call-done.refs_2_.refs_8_.refs_4_.refs_7_ = bf16[1024,9216]{1,0:T(8,128)(2,1)} async-done(((bf16[32,9216]{1,0:T(8,128)(2,1)}), bf16[1024,9216]{1,0:T(8,128)(2,1)}) %all-gather.7.cloned.1.call-update) | async-done | bytes 18874384 | tf_op jit(solution)/shard_map/all_gather | solution.py:911
  387.7 17.6 %feed_forward.3 = (f32[512,1024]{1,0:T(8,128)}, f32[512,1024]{1,0:T(8,128)}, bf16[512,1024]{1,0:T(8,128)(2,1)}, bf16[512,4096]{1,0:T(8,128)(2,1)}) custom-call(f32[512,1024]{1,0:T(8,128)} %get-tuple-element.182.x_ref.refs_13_, bf16[512,512]{1,0:T(8,128)(2,1)} %get-tuple-element.184.refs_0_.refs_9_, bf16[512,512]{1,0:T(8,128)(2,1)} %get-tuple-element.185.refs_1_.refs_9_, ...), custom_call_target="tpu_custom_call" | custom-call | flops 9663676416 | bytes 31457280 | tf_op jit(solution)/shard_map/feed_forward/pallas_call | solution.py:288
  405.3 23.0 %feed_backward.4 = (bf16[1024,6144]{1,0:T(8,128)(2,1)}, f32[1,3072]{1,0:T(1,128)}, f32[512,1024]{1,0:T(8,128)}, f32[1,1024]{1,0:T(1,128)}) custom-call(s32[1]{0:T(128)} %bitcast.45.core_ref, f32[512,1024]{1,0:T(8,128)} %maximum_convert_fusion.1.gs_ref, bf16[512,4096]{1,0:T(8,128)(2,1)} %get-tuple-element.190.refs_0_.refs_2_, ...), custom_call_target="tpu_custom_call" | custom-call | flops 12884901888 | bytes 31457280 | tf_op jit(solution)/shard_map/feed_backward/pallas_call | solution.py:465
  428.4 19.7 %feed_backward.5 = (bf16[4,128,3072]{2,1,0:T(8,128)(2,1)}, bf16[4,128,3072]{2,1,0:T(8,128)(2,1)}, f32[1,1024]{1,0:T(1,128)}, f32[512,1024]{1,0:T(8,128)}, bf16[5...) custom-call(s32[1]{0:T(128)} %bitcast.45.core_ref, ...), custom_call_target="tpu_custom_call" | custom-call | flops 6442450944 | bytes 15728640 | tf_op jit(solution)/shard_map/feed_backward/pallas_call | solution.py:465
  448.4 16.7 %attend_backward.4 = (bf16[512,512]{1,0:T(8,128)(2,1)}, bf16[2,256,512]{2,1,0:T(8,128)(2,1)}, bf16[2,256,512]{2,1,0:T(8,128)(2,1)}, bf16[2,256,512]{2,1,0:T(8,12...) custom-call(s32[4]{0:T(128)} %fusion.2.refs_0_, ...), custom_call_target="tpu_custom_call" | custom-call | flops 26843545600 | bytes 9437184 | tf_op jit(solution)/shard_map/attend_backward/pallas_call | solution.py:237
  468.7 16.4 %attend_backward.5 = (bf16[512,512]{1,0:T(8,128)(2,1)}, bf16[2,256,512]{2,1,0:T(8,128)(2,1)}, bf16[2,256,512]{2,1,0:T(8,128)(2,1)}, bf16[2,256,512]{2,1,0:T(8,12...) custom-call(s32[4]{0:T(128)} %fusion.2.refs_0_, ...), custom_call_target="tpu_custom_call" | custom-call | flops 26843545600 | bytes 9437184 | tf_op jit(solution)/shard_map/attend_backward/pallas_call | solution.py:237
  495.9 6.9 collective-permute-done.27.refs_9_
  503.0 11.2 %collective-permute-done.29.refs_11_ = bf16[2,256,512]{2,1,0:T(8,128)(2,1)} collective-permute-done((bf16[2,256,512]{2,1,0:T(8,128)(2,1)}, bf16[2,256,512]{2,1,0:T(8,128)(2,1)}, u32[]{:S(2)}, u32[]{:S(2)}) %collective-permute-start.29) | collective-permute-done | bytes 524320 | tf_op jit(solution)/shard_map/ppermute | solution.py:559
  514.2 18.2 %qkv_backward.2 = (bf16[4,128,3072]{2,1,0:T(8,128)(2,1)}, bf16[4,128,3072]{2,1,0:T(8,128)(2,1)}, f32[512,1024]{1,0:T(8,128)}, f32[1,3072]{1,0:T(1,128)}, f32[1,1024]{1,0:T(1,128)}, /*index=5*/f32[1,1024]{1,0:T(1,128)}) custom-call(s32[1]{0:T(128)} %bitcast.45.core_ref, bf16[512,512]{1,0:T(8,128)(2,1)} %get-tuple-element.195.refs_0_, ...), custom_call_target="tpu_custom_call" | custom-call | flops 6442450944 | bytes 25165824 | tf_op jit(solution)/shard_map/qkv_backward/pallas_call | solution.py:521
  536.4 23.0 %feed_backward.6 = (bf16[1024,6144]{1,0:T(8,128)(2,1)}, f32[1,3072]{1,0:T(1,128)}, f32[512,1024]{1,0:T(8,128)}, f32[1,1024]{1,0:T(1,128)}) custom-call(s32[1]{0:T(128)} %bitcast.45.core_ref, f32[512,1024]{1,0:T(8,128)} %get-tuple-element.222.gs_ref, bf16[512,4096]{1,0:T(8,128)(2,1)} %get-tuple-element.223.refs_0_.refs_2_, ...), custom_call_target="tpu_custom_call" | custom-call | flops 12884901888 | bytes 31457280 | tf_op jit(solution)/shard_map/feed_backward/pallas_call | solution.py:465
  561.7 9.6 %collective-permute-done.32.refs_1_ = bf16[4,1,32,1536]{3,2,1,0:T(8,128)(2,1)S(1)} collective-permute-done((bf16[4,1,32,1536]{3,2,1,0:T(8,128)(2,1)}, bf16[4,1,32,1536]{3,2,1,0:T(8,128)(2,1)S(1)}, u32[]{:S(2)}, u32[]{:S(2)}) %collective-permute-start.32) | collective-permute-done | bytes 393248 | tf_op jit(solution)/shard_map/ppermute | solution.py:559
  589.9 18.4 %feed_backward.7 = (bf16[4,128,3072]{2,1,0:T(8,128)(2,1)}, bf16[4,128,3072]{2,1,0:T(8,128)(2,1)}, f32[1,1024]{1,0:T(1,128)}, f32[512,1024]{1,0:T(8,128)}, bf16[5...) custom-call(s32[1]{0:T(128)} %bitcast.45.core_ref, ...), custom_call_target="tpu_custom_call" | custom-call | flops 6442450944 | bytes 15728640 | tf_op jit(solution)/shard_map/feed_backward/pallas_call | solution.py:465
  609.1 8.4 collective-permute-done.44
  619.3 7.5 collective-permute-done.41
  633.6 16.7 %attend_backward.6 = (bf16[512,512]{1,0:T(8,128)(2,1)}, bf16[2,256,512]{2,1,0:T(8,128)(2,1)}, bf16[2,256,512]{2,1,0:T(8,128)(2,1)}, bf16[2,256,512]{2,1,0:T(8,12...) custom-call(s32[4]{0:T(128)} %fusion.2.refs_0_, ...), custom_call_target="tpu_custom_call" | custom-call | flops 26843545600 | bytes 9437184 | tf_op jit(solution)/shard_map/attend_backward/pallas_call | solution.py:237
  659.2 16.5 %attend_backward.7 = (bf16[512,512]{1,0:T(8,128)(2,1)}, bf16[2,256,512]{2,1,0:T(8,128)(2,1)}, bf16[2,256,512]{2,1,0:T(8,128)(2,1)}, bf16[2,256,512]{2,1,0:T(8,12...) custom-call(s32[4]{0:T(128)} %fusion.2.refs_0_, ...), custom_call_target="tpu_custom_call" | custom-call | flops 26843545600 | bytes 9437184 | tf_op jit(solution)/shard_map/attend_backward/pallas_call | solution.py:237
  677.1 9.3 %collective-permute-done.47 = bf16[32,3072]{1,0:T(8,128)(2,1)S(1)} collective-permute-done((bf16[32,3072]{1,0:T(8,128)(2,1)}, bf16[32,3072]{1,0:T(8,128)(2,1)S(1)}, u32[]{:S(2)}, u32[]{:S(2)}) %collective-permute-start.47) | collective-permute-done | bytes 196640 | tf_op jit(solution)/shard_map/ppermute | solution.py:559
  696.3 15.5 %reduce-scatter.6.cloned.1.call-done = bf16[128,6144]{1,0:T(8,128)(2,1)} async-done(((bf16[1024,6144]{1,0:T(8,128)(2,1)}), bf16[128,6144]{1,0:T(8,128)(2,1)}) %reduce-scatter.6.cloned.1.call-update) | async-done | bytes 1572880 | tf_op jit(solution)/shard_map/reduce_scatter | solution.py:963
  714.0 8.6 collective-permute-done.54.refs_11_
  722.6 18.1 %qkv_backward.3 = (bf16[1024,3072]{1,0:T(8,128)(2,1)}, f32[512,1024]{1,0:T(8,128)}, f32[1,3072]{1,0:T(1,128)}, f32[1,1024]{1,0:T(1,128)}, f32[1,1024]{1,0:T(1,128)}) custom-call(s32[1]{0:T(128)} %bitcast.45.core_ref, bf16[512,512]{1,0:T(8,128)(2,1)} %get-tuple-element.249.refs_0_, bf16[512,512]{1,0:T(8,128)(2,1)} %get-tuple-element.260.refs_1_, ...), custom_call_target="tpu_custom_call" | custom-call | flops 6442450944 | bytes 25165824 | tf_op jit(solution)/shard_map/qkv_backward/pallas_call | solution.py:521
  743.1 4.6 collective-permute-done.55
  758.0 9.2 %collective-permute-done.63.refs_1_ = bf16[4,2,32,1536]{3,2,1,0:T(8,128)(2,1)S(1)} collective-permute-done((bf16[4,2,32,1536]{3,2,1,0:T(8,128)(2,1)}, bf16[4,2,32,1536]{3,2,1,0:T(8,128)(2,1)S(1)}, u32[]{:S(2)}, u32[]{:S(2)}) %collective-permute-start.63) | collective-permute-done | bytes 786464 | tf_op jit(solution)/shard_map/ppermute | solution.py:559
  777.9 13.5 %collective-permute-done.65.refs_1_ = bf16[4,1,32,1536]{3,2,1,0:T(8,128)(2,1)S(1)} collective-permute-done((bf16[4,1,32,1536]{3,2,1,0:T(8,128)(2,1)}, bf16[4,1,32,1536]{3,2,1,0:T(8,128)(2,1)S(1)}, u32[]{:S(2)}, u32[]{:S(2)}) %collective-permute-start.65) | collective-permute-done | bytes 393248 | tf_op jit(solution)/shard_map/ppermute | solution.py:559
  796.0 5.3 collective-permute-done.61
  803.3 6.9 collective-permute-done.69
  810.9 10.7 %collective-permute-done.68 = bf16[32,3072]{1,0:T(8,128)(2,1)S(1)} collective-permute-done((bf16[32,3072]{1,0:T(8,128)(2,1)}, bf16[32,3072]{1,0:T(8,128)(2,1)S(1)}, u32[]{:S(2)}, u32[]{:S(2)}) %collective-permute-start.68) | collective-permute-done | bytes 196640 | tf_op jit(solution)/shard_map/ppermute | solution.py:559
  832.9 17.0 %collective-permute-done.71 = bf16[32,3072]{1,0:T(8,128)(2,1)S(1)} collective-permute-done((bf16[32,3072]{1,0:T(8,128)(2,1)S(1)}, bf16[32,3072]{1,0:T(8,128)(2,1)S(1)}, u32[]{:S(2)}, u32[]{:S(2)}) %collective-permute-start.71) | collective-permute-done | bytes 196640 | tf_op jit(solution)/shard_map/ppermute | solution.py:559
  857.2 21.0 %collective-permute-done.73.refs_1_ = bf16[32,3072]{1,0:T(8,128)(2,1)S(1)} collective-permute-done((bf16[32,3072]{1,0:T(8,128)(2,1)S(1)}, bf16[32,3072]{1,0:T(8,128)(2,1)S(1)}, u32[]{:S(2)}, u32[]{:S(2)}) %collective-permute-start.73) | collective-permute-done | bytes 196640 | tf_op jit(solution)/shard_map/ppermute | solution.py:559
  (430 shorter events, 180.6 us)
Async XLA Ops:
  7.2 229.1 %all-gather.5.cloned.1.call-start = ((), (), s32[]{:S(2)}) async-start(), calls=%async_computation.3 | async-start | bytes 25952256 | tf_op jit(solution)/shard_map/all_gather | solution.py:910
  10.0 377.7 %all-gather.7.cloned.1.call-start = ((), (), s32[]{:S(2)}) async-start(), calls=%async_computation.4 | async-start | bytes 19464192 | tf_op jit(solution)/shard_map/all_gather | solution.py:911
  10.7 570.4 %reduce-scatter.4.cloned.1.call-start = ((), (), s32[]{:S(2)}) async-start(), calls=%async_computation.5 | async-start | bytes 14155776 | tf_op jit(solution)/shard_map/reduce_scatter | solution.py:963
  10.8 100.1 %collective-permute-start = (bf16[4,32,3072]{2,1,0:T(8,128)(2,1)S(1)}, bf16[4,32,3072]{2,1,0:T(8,128)(2,1)S(1)}, u32[]{:S(2)}, u32[]{:S(2)}) collective-permute-start(bf16[4,32,3072]{2,1,0:T(8,128)(2,1)S(1)} %bitcast.178), channel_id=1, source_target_pairs={{0,1},{1,0},{2,3},{3,2},{4,5},{5,4},{6,7},{7,6},{8,9},{9,8},{10,11... | collective-permute-start | bytes 2359304 | tf_op jit(solution)/shard_map/ppermute | solution.py:559
  11.4 44.6 %collective-permute-start.3 = (bf16[32,3072]{1,0:T(8,128)(2,1)S(1)}, bf16[32,3072]{1,0:T(8,128)(2,1)S(1)}, u32[]{:S(2)}, u32[]{:S(2)}) collective-permute-start(bf16[32,3072]{1,0:T(8,128)(2,1)S(1)} %dynamic-slice_bitcast_fusion.12), channel_id=1, source_target_pairs={{0,6},{1,7},{2,4},{3,5},{4,2},{5,3},{6,0},{7,1},{8,14},{9,15},{10,... | collective-permute-start | bytes 589832 | tf_op jit(solution)/shard_map/ppermute | solution.py:559
  16.1 39.9 %collective-permute-start.2 = (bf16[32,3072]{1,0:T(8,128)(2,1)S(1)}, bf16[32,3072]{1,0:T(8,128)(2,1)S(1)}, u32[]{:S(2)}, u32[]{:S(2)}) collective-permute-start(bf16[32,3072]{1,0:T(8,128)(2,1)S(1)} %dynamic-slice_bitcast_fusion.12), channel_id=1, source_target_pairs={{0,4},{1,5},{2,6},{3,7},{4,0},{5,1},{6,2},{7,3},{8,12},{9,13},{10,... | collective-permute-start | bytes 589832 | tf_op jit(solution)/shard_map/ppermute | solution.py:559
  16.1 39.9 %collective-permute-start.1 = (bf16[32,3072]{1,0:T(8,128)(2,1)S(1)}, bf16[32,3072]{1,0:T(8,128)(2,1)S(1)}, u32[]{:S(2)}, u32[]{:S(2)}) collective-permute-start(bf16[32,3072]{1,0:T(8,128)(2,1)S(1)} %dynamic-slice_bitcast_fusion.12), channel_id=1, source_target_pairs={{0,2},{1,3},{2,0},{3,1},{4,6},{5,7},{6,4},{7,5},{8,10},{9,11},{10,... | collective-permute-start | bytes 589832 | tf_op jit(solution)/shard_map/ppermute | solution.py:559
  56.1 28.5 %collective-permute-start.4 = (bf16[3,32,3072]{2,1,0:T(8,128)(2,1)S(1)}, bf16[3,32,3072]{2,1,0:T(8,128)(2,1)S(1)}, u32[]{:S(2)}, u32[]{:S(2)}) collective-permute-start(bf16[3,32,3072]{2,1,0:T(8,128)(2,1)S(1)} %pad_maximum_fusion.1.refs_2_), channel_id=1, source_target_pairs={{0,8},{8,0},{16,24},{24,16},{1,9},{9,1},{17,25},{25,17},{2,10},{10... | collective-permute-start | bytes 1769480 | tf_op jit(solution)/shard_map/ppermute | solution.py:559
  57.6 26.9 %collective-permute-start.5 = (bf16[3,32,3072]{2,1,0:T(8,128)(2,1)S(1)}, bf16[3,32,3072]{2,1,0:T(8,128)(2,1)S(1)}, u32[]{:S(2)}, u32[]{:S(2)}) collective-permute-start(bf16[3,32,3072]{2,1,0:T(8,128)(2,1)S(1)} %pad_maximum_fusion.1.refs_2_), channel_id=1, source_target_pairs={{0,16},{8,24},{16,0},{24,8},{1,17},{9,25},{17,1},{25,9},{2,18},{10... | collective-permute-start | bytes 1769480 | tf_op jit(solution)/shard_map/ppermute | solution.py:559
  59.2 48.1 %collective-permute-start.6 = (bf16[3,32,3072]{2,1,0:T(8,128)(2,1)S(1)}, bf16[3,32,3072]{2,1,0:T(8,128)(2,1)}, u32[]{:S(2)}, u32[]{:S(2)}) collective-permute-start(bf16[3,32,3072]{2,1,0:T(8,128)(2,1)S(1)} %pad_maximum_fusion.1.refs_2_), channel_id=1, source_target_pairs={{0,24},{8,16},{16,8},{24,0},{1,25},{9,17},{17,9},{25,1},{2,26},{10... | collective-permute-start | bytes 1769480 | tf_op jit(solution)/shard_map/ppermute | solution.py:559
  59.7 51.3 %collective-permute-start.7 = (bf16[3,32,3072]{2,1,0:T(8,128)(2,1)S(1)}, bf16[3,32,3072]{2,1,0:T(8,128)(2,1)}, u32[]{:S(2)}, u32[]{:S(2)}) collective-permute-start(bf16[3,32,3072]{2,1,0:T(8,128)(2,1)S(1)} %pad_maximum_fusion.1.refs_2_), channel_id=1, source_target_pairs={{0,1},{1,0},{2,3},{3,2},{4,5},{5,4},{6,7},{7,6},{8,9},{9,8},{10,11... | collective-permute-start | bytes 1769480 | tf_op jit(solution)/shard_map/ppermute | solution.py:559
  84.5 26.4 %collective-permute-start.8 = (bf16[3,32,3072]{2,1,0:T(8,128)(2,1)S(1)}, bf16[3,32,3072]{2,1,0:T(8,128)(2,1)}, u32[]{:S(2)}, u32[]{:S(2)}) collective-permute-start(bf16[3,32,3072]{2,1,0:T(8,128)(2,1)S(1)} %collective-permute-done.4.refs_3_), channel_id=1, source_target_pairs={{0,1},{1,0},{2,3},{3,2},{4,5},{5,4},{6,7},{7,6},{8,9},{9,8},{10,11... | collective-permute-start | bytes 1769480 | tf_op jit(solution)/shard_map/ppermute | solution.py:559
  131.0 26.8 %collective-permute-start.12 = (bf16[2,256,512]{2,1,0:T(8,128)(2,1)S(1)}, bf16[2,256,512]{2,1,0:T(8,128)(2,1)S(1)}, u32[]{:S(2)}, u32[]{:S(2)}) collective-permute-start(bf16[2,256,512]{2,1,0:T(8,128)(2,1)S(1)} %pad_maximum_fusion.3), channel_id=1, source_target_pairs={{0,16},{8,24},{16,0},{24,8},{1,17},{9,25},{17,1},{25,9},{2,18},{10... | collective-permute-start | bytes 1572872 | tf_op jit(solution)/shard_map/ppermute | solution.py:559
  131.4 47.5 %collective-permute-start.13 = (bf16[2,256,512]{2,1,0:T(8,128)(2,1)S(1)}, bf16[2,256,512]{2,1,0:T(8,128)(2,1)S(1)}, u32[]{:S(2)}, u32[]{:S(2)}) collective-permute-start(bf16[2,256,512]{2,1,0:T(8,128)(2,1)S(1)} %pad_maximum_fusion.3), channel_id=1, source_target_pairs={{0,24},{8,16},{16,8},{24,0},{1,25},{9,17},{17,9},{25,1},{2,26},{10... | collective-permute-start | bytes 1572872 | tf_op jit(solution)/shard_map/ppermute | solution.py:559
  139.2 62.3 %collective-permute-start.14 = (bf16[2,256,512]{2,1,0:T(8,128)(2,1)S(1)}, bf16[2,256,512]{2,1,0:T(8,128)(2,1)S(1)}, u32[]{:S(2)}, u32[]{:S(2)}) collective-permute-start(bf16[2,256,512]{2,1,0:T(8,128)(2,1)S(1)} %pad_maximum_fusion.4), channel_id=1, source_target_pairs={{0,8},{8,0},{16,24},{24,16},{1,9},{9,1},{17,25},{25,17},{2,10},{10... | collective-permute-start | bytes 1572872 | tf_op jit(solution)/shard_map/ppermute | solution.py:559
  139.7 61.7 %collective-permute-start.15 = (bf16[2,256,512]{2,1,0:T(8,128)(2,1)S(1)}, bf16[2,256,512]{2,1,0:T(8,128)(2,1)S(1)}, u32[]{:S(2)}, u32[]{:S(2)}) collective-permute-start(bf16[2,256,512]{2,1,0:T(8,128)(2,1)S(1)} %pad_maximum_fusion.4), channel_id=1, source_target_pairs={{0,16},{8,24},{16,0},{24,8},{1,17},{9,25},{17,1},{25,9},{2,18},{10... | collective-permute-start | bytes 1572872 | tf_op jit(solution)/shard_map/ppermute | solution.py:559
  156.5 59.0 %collective-permute-start.16 = (bf16[2,256,512]{2,1,0:T(8,128)(2,1)S(1)}, bf16[2,256,512]{2,1,0:T(8,128)(2,1)S(1)}, u32[]{:S(2)}, u32[]{:S(2)}) collective-permute-start(bf16[2,256,512]{2,1,0:T(8,128)(2,1)S(1)} %pad_maximum_fusion.4), channel_id=1, source_target_pairs={{0,24},{8,16},{16,8},{24,0},{1,25},{9,17},{17,9},{25,1},{2,26},{10... | collective-permute-start | bytes 1572872 | tf_op jit(solution)/shard_map/ppermute | solution.py:559
  267.2 42.3 %collective-permute-start.19 = (bf16[2,256,512]{2,1,0:T(8,128)(2,1)S(1)}, bf16[2,256,512]{2,1,0:T(8,128)(2,1)}, u32[]{:S(2)}, u32[]{:S(2)}) collective-permute-start(bf16[2,256,512]{2,1,0:T(8,128)(2,1)S(1)} %pad_maximum_fusion.5), channel_id=1, source_target_pairs={{0,24},{8,16},{16,8},{24,0},{1,25},{9,17},{17,9},{25,1},{2,26},{10... | collective-permute-start | bytes 1572872 | tf_op jit(solution)/shard_map/ppermute | solution.py:559
  270.2 50.3 %collective-permute-start.20 = (bf16[2,256,512]{2,1,0:T(8,128)(2,1)S(1)}, bf16[2,256,512]{2,1,0:T(8,128)(2,1)S(1)}, u32[]{:S(2)}, u32[]{:S(2)}) collective-permute-start(bf16[2,256,512]{2,1,0:T(8,128)(2,1)S(1)} %pad_maximum_fusion.6), channel_id=1, source_target_pairs={{0,8},{8,0},{16,24},{24,16},{1,9},{9,1},{17,25},{25,17},{2,10},{10... | collective-permute-start | bytes 1572872 | tf_op jit(solution)/shard_map/ppermute | solution.py:559
  271.4 49.2 %collective-permute-start.21 = (bf16[2,256,512]{2,1,0:T(8,128)(2,1)S(1)}, bf16[2,256,512]{2,1,0:T(8,128)(2,1)S(1)}, u32[]{:S(2)}, u32[]{:S(2)}) collective-permute-start(bf16[2,256,512]{2,1,0:T(8,128)(2,1)S(1)} %pad_maximum_fusion.6), channel_id=1, source_target_pairs={{0,16},{8,24},{16,0},{24,8},{1,17},{9,25},{17,1},{25,9},{2,18},{10... | collective-permute-start | bytes 1572872 | tf_op jit(solution)/shard_map/ppermute | solution.py:559
  287.4 50.9 %collective-permute-start.22 = (bf16[2,256,512]{2,1,0:T(8,128)(2,1)S(1)}, bf16[2,256,512]{2,1,0:T(8,128)(2,1)S(1)}, u32[]{:S(2)}, u32[]{:S(2)}) collective-permute-start(bf16[2,256,512]{2,1,0:T(8,128)(2,1)S(1)} %pad_maximum_fusion.6), channel_id=1, source_target_pairs={{0,24},{8,16},{16,8},{24,0},{1,25},{9,17},{17,9},{25,1},{2,26},{10... | collective-permute-start | bytes 1572872 | tf_op jit(solution)/shard_map/ppermute | solution.py:559
  428.3 283.5 %reduce-scatter.6.cloned.1.call-start = ((), (), s32[]{:S(2)}) async-start(), calls=%async_computation.6 | async-start | bytes 14155776 | tf_op jit(solution)/shard_map/reduce_scatter | solution.py:963
  448.1 37.9 %collective-permute-start.23 = (bf16[4,128,3072]{2,1,0:T(8,128)(2,1)}, bf16[4,128,3072]{2,1,0:T(8,128)(2,1)S(1)}, u32[]{:S(2)}, u32[]{:S(2)}) collective-permute-start(bf16[4,128,3072]{2,1,0:T(8,128)(2,1)} %get-tuple-element.201), channel_id=1, source_target_pairs={{0,1},{1,0},{2,3},{3,2},{4,5},{5,4},{6,7},{7,6},{8,9},{9,8},{10,11... | collective-permute-start | bytes 9437192 | tf_op jit(solution)/shard_map/ppermute | solution.py:559
  465.5 28.3 %collective-permute-start.25 = (bf16[2,256,512]{2,1,0:T(8,128)(2,1)}, bf16[2,256,512]{2,1,0:T(8,128)(2,1)}, u32[]{:S(2)}, u32[]{:S(2)}) collective-permute-start(bf16[2,256,512]{2,1,0:T(8,128)(2,1)} %get-tuple-element.207), channel_id=1, source_target_pairs={{0,16},{8,24},{16,0},{24,8},{1,17},{9,25},{17,1},{25,9},{2,18},{10... | collective-permute-start | bytes 1572872 | tf_op jit(solution)/shard_map/ppermute | solution.py:559
  466.0 28.1 %collective-permute-start.26 = (bf16[2,256,512]{2,1,0:T(8,128)(2,1)}, bf16[2,256,512]{2,1,0:T(8,128)(2,1)}, u32[]{:S(2)}, u32[]{:S(2)}) collective-permute-start(bf16[2,256,512]{2,1,0:T(8,128)(2,1)} %get-tuple-element.208), channel_id=1, source_target_pairs={{0,24},{8,16},{16,8},{24,0},{1,25},{9,17},{17,9},{25,1},{2,26},{10... | collective-permute-start | bytes 1572872 | tf_op jit(solution)/shard_map/ppermute | solution.py:559
  486.3 27.9 %collective-permute-start.29 = (bf16[2,256,512]{2,1,0:T(8,128)(2,1)}, bf16[2,256,512]{2,1,0:T(8,128)(2,1)}, u32[]{:S(2)}, u32[]{:S(2)}) collective-permute-start(bf16[2,256,512]{2,1,0:T(8,128)(2,1)} %get-tuple-element.212), channel_id=1, source_target_pairs={{0,24},{8,16},{16,8},{24,0},{1,25},{9,17},{17,9},{25,1},{2,26},{10... | collective-permute-start | bytes 1572872 | tf_op jit(solution)/shard_map/ppermute | solution.py:559
  493.8 38.6 %collective-permute-start.30 = (bf16[4,2,32,1536]{3,2,1,0:T(8,128)(2,1)}, bf16[4,2,32,1536]{3,2,1,0:T(8,128)(2,1)S(1)}, u32[]{:S(2)}, u32[]{:S(2)}) collective-permute-start(bf16[4,2,32,1536]{3,2,1,0:T(8,128)(2,1)} %get-tuple-element.217), channel_id=1, source_target_pairs={{0,8},{8,0},{16,24},{24,16},{1,9},{9,1},{17,25},{25,17},{2,10},{10... | collective-permute-start | bytes 2359304 | tf_op jit(solution)/shard_map/ppermute | solution.py:559
  494.1 38.4 %collective-permute-start.31 = (bf16[4,2,32,1536]{3,2,1,0:T(8,128)(2,1)}, bf16[4,2,32,1536]{3,2,1,0:T(8,128)(2,1)S(1)}, u32[]{:S(2)}, u32[]{:S(2)}) collective-permute-start(bf16[4,2,32,1536]{3,2,1,0:T(8,128)(2,1)} %get-tuple-element.219), channel_id=1, source_target_pairs={{0,16},{8,24},{16,0},{24,8},{1,17},{9,25},{17,1},{25,9},{2,18},{10... | collective-permute-start | bytes 2359304 | tf_op jit(solution)/shard_map/ppermute | solution.py:559
  559.4 262.3 %reduce-scatter.8.cloned.1.call-start = ((), (), s32[]{:S(2)}) async-start(), calls=%async_computation.7 | async-start | bytes 7077888 | tf_op jit(solution)/shard_map/reduce_scatter | solution.py:994
  582.8 45.2 %collective-permute-start.35 = (bf16[4,2,32,1536]{3,2,1,0:T(8,128)(2,1)S(1)}, bf16[4,2,32,1536]{3,2,1,0:T(8,128)(2,1)S(1)}, u32[]{:S(2)}, u32[]{:S(2)}) collective-permute-start(bf16[4,2,32,1536]{3,2,1,0:T(8,128)(2,1)S(1)} %copy-done.60), channel_id=1, source_target_pairs={{0,8},{8,0},{16,24},{24,16},{1,9},{9,1},{17,25},{25,17},{2,10},{10... | collective-permute-start | bytes 2359304 | tf_op jit(solution)/shard_map/ppermute | solution.py:559
  584.3 43.7 %collective-permute-start.36 = (bf16[4,2,32,1536]{3,2,1,0:T(8,128)(2,1)S(1)}, bf16[4,2,32,1536]{3,2,1,0:T(8,128)(2,1)S(1)}, u32[]{:S(2)}, u32[]{:S(2)}) collective-permute-start(bf16[4,2,32,1536]{3,2,1,0:T(8,128)(2,1)S(1)} %copy-done.59), channel_id=1, source_target_pairs={{0,16},{8,24},{16,0},{24,8},{1,17},{9,25},{17,1},{25,9},{2,18},{10... | collective-permute-start | bytes 2359304 | tf_op jit(solution)/shard_map/ppermute | solution.py:559
  585.5 32.0 %collective-permute-start.44 = (bf16[32,3072]{1,0:T(8,128)(2,1)S(1)}, bf16[32,3072]{1,0:T(8,128)(2,1)S(1)}, u32[]{:S(2)}, u32[]{:S(2)}) collective-permute-start(bf16[32,3072]{1,0:T(8,128)(2,1)S(1)} %copy-done.76), channel_id=1, source_target_pairs={{0,4},{1,5},{2,6},{3,7},{4,0},{5,1},{6,2},{7,3},{8,12},{9,13},{10,... | collective-permute-start | bytes 589832 | tf_op jit(solution)/shard_map/ppermute | solution.py:559
  587.3 31.3 %collective-permute-start.43 = (bf16[32,3072]{1,0:T(8,128)(2,1)S(1)}, bf16[32,3072]{1,0:T(8,128)(2,1)S(1)}, u32[]{:S(2)}, u32[]{:S(2)}) collective-permute-start(bf16[32,3072]{1,0:T(8,128)(2,1)S(1)} %copy-done.75), channel_id=1, source_target_pairs={{0,2},{1,3},{2,0},{3,1},{4,6},{5,7},{6,4},{7,5},{8,10},{9,11},{10,... | collective-permute-start | bytes 589832 | tf_op jit(solution)/shard_map/ppermute | solution.py:559
  619.2 69.6 %collective-permute-start.39 = (bf16[4,128,3072]{2,1,0:T(8,128)(2,1)}, bf16[4,128,3072]{2,1,0:T(8,128)(2,1)S(1)}, u32[]{:S(2)}, u32[]{:S(2)}) collective-permute-start(bf16[4,128,3072]{2,1,0:T(8,128)(2,1)} %get-tuple-element.264), channel_id=1, source_target_pairs={{0,1},{1,0},{2,3},{3,2},{4,5},{5,4},{6,7},{7,6},{8,9},{9,8},{10,11... | collective-permute-start | bytes 9437192 | tf_op jit(solution)/shard_map/ppermute | solution.py:559
  650.3 44.5 %collective-permute-start.49 = (bf16[2,256,512]{2,1,0:T(8,128)(2,1)}, bf16[2,256,512]{2,1,0:T(8,128)(2,1)S(1)}, u32[]{:S(2)}, u32[]{:S(2)}) collective-permute-start(bf16[2,256,512]{2,1,0:T(8,128)(2,1)} %get-tuple-element.283), channel_id=1, source_target_pairs={{0,8},{8,0},{16,24},{24,16},{1,9},{9,1},{17,25},{25,17},{2,10},{10... | collective-permute-start | bytes 1572872 | tf_op jit(solution)/shard_map/ppermute | solution.py:559
  656.1 30.3 %collective-permute-start.47 = (bf16[32,3072]{1,0:T(8,128)(2,1)}, bf16[32,3072]{1,0:T(8,128)(2,1)S(1)}, u32[]{:S(2)}, u32[]{:S(2)}) collective-permute-start(bf16[32,3072]{1,0:T(8,128)(2,1)} %get-tuple-element.278), channel_id=1, source_target_pairs={{0,4},{1,5},{2,6},{3,7},{4,0},{5,1},{6,2},{7,3},{8,12},{9,13},{10,... | collective-permute-start | bytes 589832 | tf_op jit(solution)/shard_map/ppermute | solution.py:559
  656.6 30.8 %collective-permute-start.46 = (bf16[32,3072]{1,0:T(8,128)(2,1)}, bf16[32,3072]{1,0:T(8,128)(2,1)S(1)}, u32[]{:S(2)}, u32[]{:S(2)}) collective-permute-start(bf16[32,3072]{1,0:T(8,128)(2,1)} %get-tuple-element.277), channel_id=1, source_target_pairs={{0,2},{1,3},{2,0},{3,1},{4,6},{5,7},{6,4},{7,5},{8,10},{9,11},{10,... | collective-permute-start | bytes 589832 | tf_op jit(solution)/shard_map/ppermute | solution.py:559
  675.7 38.3 %collective-permute-start.50 = (bf16[2,256,512]{2,1,0:T(8,128)(2,1)S(1)}, bf16[2,256,512]{2,1,0:T(8,128)(2,1)}, u32[]{:S(2)}, u32[]{:S(2)}) collective-permute-start(bf16[2,256,512]{2,1,0:T(8,128)(2,1)S(1)} %copy-done.69), channel_id=1, source_target_pairs={{0,16},{8,24},{16,0},{24,8},{1,17},{9,25},{17,1},{25,9},{2,18},{10... | collective-permute-start | bytes 1572872 | tf_op jit(solution)/shard_map/ppermute | solution.py:559
  686.4 27.7 %collective-permute-start.51 = (bf16[2,256,512]{2,1,0:T(8,128)(2,1)S(1)}, bf16[2,256,512]{2,1,0:T(8,128)(2,1)}, u32[]{:S(2)}, u32[]{:S(2)}) collective-permute-start(bf16[2,256,512]{2,1,0:T(8,128)(2,1)S(1)} %copy-done.68), channel_id=1, source_target_pairs={{0,24},{8,16},{16,8},{24,0},{1,25},{9,17},{17,9},{25,1},{2,26},{10... | collective-permute-start | bytes 1572872 | tf_op jit(solution)/shard_map/ppermute | solution.py:559
  687.5 26.6 %collective-permute-start.52 = (bf16[2,256,512]{2,1,0:T(8,128)(2,1)}, bf16[2,256,512]{2,1,0:T(8,128)(2,1)}, u32[]{:S(2)}, u32[]{:S(2)}) collective-permute-start(bf16[2,256,512]{2,1,0:T(8,128)(2,1)} %get-tuple-element.287), channel_id=1, source_target_pairs={{0,8},{8,0},{16,24},{24,16},{1,9},{9,1},{17,25},{25,17},{2,10},{10... | collective-permute-start | bytes 1572872 | tf_op jit(solution)/shard_map/ppermute | solution.py:559
  694.8 27.8 %collective-permute-start.54 = (bf16[2,256,512]{2,1,0:T(8,128)(2,1)}, bf16[2,256,512]{2,1,0:T(8,128)(2,1)}, u32[]{:S(2)}, u32[]{:S(2)}) collective-permute-start(bf16[2,256,512]{2,1,0:T(8,128)(2,1)} %get-tuple-element.289), channel_id=1, source_target_pairs={{0,24},{8,16},{16,8},{24,0},{1,25},{9,17},{17,9},{25,1},{2,26},{10... | collective-permute-start | bytes 1572872 | tf_op jit(solution)/shard_map/ppermute | solution.py:559
  791.4 38.7 %collective-permute-start.76 = (bf16[32,12288]{1,0:T(8,128)(2,1)S(1)}, bf16[32,12288]{1,0:T(8,128)(2,1)S(1)}, u32[]{:S(2)}, u32[]{:S(2)}) collective-permute-start(bf16[32,12288]{1,0:T(8,128)(2,1)S(1)} %pad_maximum_fusion.refs_0_), channel_id=1, source_target_pairs={{0,8},{8,0},{16,24},{24,16},{1,9},{9,1},{17,25},{25,17},{2,10},{10... | collective-permute-start | bytes 2359304 | tf_op jit(solution)/shard_map/ppermute | solution.py:559
  792.1 60.3 %collective-permute-start.77 = (bf16[32,12288]{1,0:T(8,128)(2,1)S(1)}, bf16[32,12288]{1,0:T(8,128)(2,1)S(1)}, u32[]{:S(2)}, u32[]{:S(2)}) collective-permute-start(bf16[32,12288]{1,0:T(8,128)(2,1)S(1)} %pad_maximum_fusion.refs_0_), channel_id=1, source_target_pairs={{0,16},{8,24},{16,0},{24,8},{1,17},{9,25},{17,1},{25,9},{2,18},{10... | collective-permute-start | bytes 2359304 | tf_op jit(solution)/shard_map/ppermute | solution.py:559
  830.1 26.5 %collective-permute-start.78 = (bf16[32,12288]{1,0:T(8,128)(2,1)S(1)}, bf16[32,12288]{1,0:T(8,128)(2,1)S(1)}, u32[]{:S(2)}, u32[]{:S(2)}) collective-permute-start(bf16[32,12288]{1,0:T(8,128)(2,1)S(1)} %pad_maximum_fusion.refs_0_), channel_id=1, source_target_pairs={{0,24},{8,16},{16,8},{24,0},{1,25},{9,17},{17,9},{25,1},{2,26},{10... | collective-permute-start | bytes 2359304 | tf_op jit(solution)/shard_map/ppermute | solution.py:559
  832.2 59.2 %collective-permute-start.79 = (bf16[32,9216]{1,0:T(8,128)(2,1)S(1)}, bf16[32,9216]{1,0:T(8,128)(2,1)S(1)}, u32[]{:S(2)}, u32[]{:S(2)}) collective-permute-start(bf16[32,9216]{1,0:T(8,128)(2,1)S(1)} %pad_maximum_fusion.2.refs_0_), channel_id=1, source_target_pairs={{0,8},{8,0},{16,24},{24,16},{1,9},{9,1},{17,25},{25,17},{2,10},{10... | collective-permute-start | bytes 1769480 | tf_op jit(solution)/shard_map/ppermute | solution.py:559
  850.0 41.4 %collective-permute-start.80 = (bf16[32,9216]{1,0:T(8,128)(2,1)S(1)}, bf16[32,9216]{1,0:T(8,128)(2,1)S(1)}, u32[]{:S(2)}, u32[]{:S(2)}) collective-permute-start(bf16[32,9216]{1,0:T(8,128)(2,1)S(1)} %pad_maximum_fusion.2.refs_0_), channel_id=1, source_target_pairs={{0,16},{8,24},{16,0},{24,8},{1,17},{9,25},{17,1},{25,9},{2,18},{10... | collective-permute-start | bytes 1769480 | tf_op jit(solution)/shard_map/ppermute | solution.py:559
  850.7 40.7 %collective-permute-start.81 = (bf16[32,9216]{1,0:T(8,128)(2,1)S(1)}, bf16[32,9216]{1,0:T(8,128)(2,1)S(1)}, u32[]{:S(2)}, u32[]{:S(2)}) collective-permute-start(bf16[32,9216]{1,0:T(8,128)(2,1)S(1)} %pad_maximum_fusion.2.refs_0_), channel_id=1, source_target_pairs={{0,24},{8,16},{16,8},{24,0},{1,25},{9,17},{17,9},{25,1},{2,26},{10... | collective-permute-start | bytes 1769480 | tf_op jit(solution)/shard_map/ppermute | solution.py:559
  856.5 31.0 %collective-permute-start.74 = (bf16[32,3072]{1,0:T(8,128)(2,1)S(1)}, bf16[32,3072]{1,0:T(8,128)(2,1)S(1)}, u32[]{:S(2)}, u32[]{:S(2)}) collective-permute-start(bf16[32,3072]{1,0:T(8,128)(2,1)S(1)} %add_convert_fusion.2.refs_0_), channel_id=1, source_target_pairs={{0,16},{8,24},{16,0},{24,8},{1,17},{9,25},{17,1},{25,9},{2,18},{10... | collective-permute-start | bytes 589832 | tf_op jit(solution)/shard_map/ppermute | solution.py:559
  (123 other events, 1420.4 us)
Sparse Core Ops, SparseCore 0:
  11.5 224.7 all-gather.4
  239.7 147.8 all-gather.6
  428.4 126.0 reduce-scatter.3
  559.6 152.1 reduce-scatter.5
  741.0 78.4 reduce-scatter.7

commit v4 on v3

--- a/solution.py
+++ b/solution.py
@@ -559,6 +559,15 @@
     return lax.ppermute(block, axis, [(i, i ^ bits) for i in range(lax.axis_size(axis))])
 
 
+def from_others(block, n_tok):
+    if n_tok != 4:
+        return [trade(block, "tok", step) for step in range(1, n_tok)]
+    first, second = trade(block, "tok", 1), trade(block, "tok", 2)
+    half = block.shape[1] // 2
+    third = [trade(first[:, :half], "tok", 2), trade(second[:, half:], "tok", 1)]
+    return [first, second, jnp.concatenate(third, 1)]
+
+
 def pick(block, place, axis):
     return lax.dynamic_index_in_dim(block, place, axis, keepdims=False)
 
@@ -806,38 +815,41 @@
 def feed_out_kernel(pieces, me_ref, *refs):
     mix_ref, expand_ref, reduce_ref = refs[-3:]
     span, width = mix_ref.shape[1] * mix_ref.shape[2], mix_ref.shape[3]
-    for step, ref in enumerate(refs[:pieces]):
+    for step in range(pieces):
         place = jnp.bitwise_xor(me_ref[0], step)
+        early_ref, late_ref = refs[step], refs[pieces + step]
         for a in range(SLABS):
+            ref, start = (early_ref, 2 * a) if a < EARLY else (late_ref, 2 * (a - EARLY))
+            start *= width
             for w in range(width // span):
-                there = 2 * a * width + w * span
-                value = ref[:, there : there + span].astype(F32)
+                value = ref[:, start + w * span : start + (w + 1) * span].astype(F32)
                 expand_ref[0, place, :, (w * SLABS + a) * span : (w * SLABS + a + 1) * span] = value
-            there = (2 * a + 1) * width
-            reduce_ref[0, a, place] = ref[:, there : there + width].astype(F32)
-        mix_ref[0, place] = ref[:, 2 * SLABS * width :].astype(F32)
-
-
-def feed_out(pieces, width, me, layer, held):
-    n_tok = len(pieces)
-    share = pieces[0].shape[0]
+            reduce_ref[0, a, place] = ref[:, start + width : start + 2 * width].astype(F32)
+        mix_ref[0, place] = late_ref[:, 2 * (SLABS - EARLY) * width :].astype(F32)
+
+
+def feed_out(early, late, width, me, layer, held):
+    n_tok, share = len(early), early[0].shape[0]
+    early_size, late_size = 2 * EARLY * width, (2 * (SLABS - EARLY) + 1) * width
+    late_at = early_size // late_size if late[0].shape[1] > late_size else 0
     shapes = [(n_tok, share, width), (n_tok, share, SLABS * width), (SLABS, n_tok, share, width)]
     return pl.pallas_call(
         functools.partial(feed_out_kernel, n_tok),
         grid=(1,),
         in_specs=[pl.BlockSpec(memory_space=pltpu.SMEM)]
-        + [whole((share, (2 * SLABS + 1) * width)) for _ in pieces]
+        + [whole((share, early_size)) for _ in early]
+        + [pl.BlockSpec((share, late_size), lambda i: (0, late_at)) for _ in late]
         + [pl.BlockSpec(memory_space=pl.ANY) for _ in held],
         out_specs=[
             pl.BlockSpec((1,) + shape, lambda i, rank=len(shape): (layer,) + (0,) * rank)
             for shape in shapes
         ],
         out_shape=[jax.ShapeDtypeStruct((LAYERS,) + shape, F32) for shape in shapes],
-        input_output_aliases={1 + n_tok + k: k for k in range(len(held))},
+        input_output_aliases={1 + 2 * n_tok + k: k for k in range(len(held))},
         compiler_params=params(),
         cost_estimate=cost(9 * share * n_tok * width, 6 * 9 * share * n_tok * width),
         name="feed_out",
-    )(me.reshape(1), *pieces, *held)
+    )(me.reshape(1), *early, *late, *held)
 
 
 def qkv_out_kernel(pieces, me_ref, *refs):
@@ -929,7 +941,7 @@
                     for kind in (1, 2)
                 ]
             )
-            fars.append([trade(block, "tok", step) for step in steps])
+            fars.append(from_others(block, n_tok))
         for part in range(parts):
             one, lse = attend_forward(thr, qkv, fars[part], part, parts)
             attended.append(one)
@@ -982,8 +994,7 @@
         conts[-1] = together(conts[-1], [late[layer]])
         if not layer:
             upper = jnp.concatenate([early[1], late[1].finish(), last[1].finish()], 1)
-            conts[-1], upper, rows_early = sync((conts[-1], upper, spread_rows(early[0])))
-            early[0] = added(*from_each(rows_early))
+            conts[-1], upper = sync((conts[-1], upper))
             upper = to_each(upper)
         *dwq, grad_stream, dqb, dfg, dfs = qkv_backward(
             n_wa, core, dqs, conts, sums, normed, start, grad_middle, vecs[layer], wq, bool(layer)
@@ -1008,13 +1019,14 @@
     for step in [1 << bit for bit in range(n_tok.bit_length() - 1)]:
         small = small + trade(small, "tok", step)
 
-    lower = jnp.concatenate([early[0], late[0].finish()], 1)
-    lower, last[0] = sync((lower, spread_rows(last[0])))
+    rows_early = together(spread_rows(early[0]), [late[0]])
+    early[0] = to_each(added(*from_each(rows_early)))
+    rows_late, last[0] = sync((late[0].finish(), spread_rows(last[0])))
     last[0] = added(*from_each(last[0]))
-    lower = to_each(lower)
-    feeds = feed_out(upper, width, me, 1, [])
+    feeds = feed_out(upper, upper, width, me, 1, [])
     qkvs = qkv_out(upper, 3 * width, me, 1, [])
-    feeds = feed_out(lower, width, me, 0, feeds)
+    rows_late, early[0], feeds, qkvs = sync((to_each(rows_late), early[0], feeds, qkvs))
+    feeds = feed_out(early[0], rows_late, width, me, 0, feeds)
     qkvs = qkv_out(to_each(last[0]), 3 * width, me, 0, [qkvs])
     mixes, expands, reduces = [
         block.reshape(LAYERS, -1, width) if place != 1 else block.reshape(LAYERS, span, -1)

time: 908 us -> 893 us (0.983)
  waiting for transfers between devices: 385 us -> 356 us
  starting transfers between devices: 82.4 us -> 99.7 us
    ppermute x82 -> x89, waiting for transfers between devices: 322 us -> 300 us  [trade(): lax.ppermute(block, axis, [(i, i ^ bits) for i in range(lax.axis_size(axi...]
    ppermute x82 -> x89, starting transfers between devices: 82.2 us -> 99.5 us  [trade(): lax.ppermute(block, axis, [(i, i ^ bits) for i in range(lax.axis_size(axi...]
    reduce_scatter x2, waiting for transfers between devices: 15.5 us -> 0.04 us  [local(): lax.psum_scatter(dw_early, 'wa', scatter_dimension=0, tiled=True)]
  transfers between devices with their start and end apart: 87 -> 94, of which waited for: 36 -> 38; matrix products, arithmetic and copies ran while one was open for 3% -> 3% of each run, Pallas kernels for 30% -> 33%
where the time goes in v4:
time: 893 us; the launch traced here: 889 us
  waiting for transfers between devices  356 us (40%)
  Pallas kernels  336 us (38%)
  starting transfers between devices  99.7 us (11%)
  blocking collectives  38.9 us (4%)
  local copies, waits for them, and re-layouts  29.3 us (3%)
  between operations  15.6 us (2%)
  other arithmetic  13.4 us (2%)
    ppermute x89, waiting for transfers between devices, trade(): lax.ppermute(block, axis, [(i, i ^ bits) for i in range(lax.axis_size(axi...  300 us
    ppermute x89, starting transfers between devices, trade(): lax.ppermute(block, axis, [(i, i ^ bits) for i in range(lax.axis_size(axi...  99.5 us
    pallas_call x4, Pallas kernels, feed_backward(): pl.pallas_call(functools.partial(feed_pull_kernel, bool(final), half, len...  84.2 us
    pallas_call x4, Pallas kernels, attend_backward(): pl.pallas_call(functools.partial(attend_pull_kernel, pb, len(far)), grid=...  66.4 us
    pallas_call x4, Pallas kernels, attend_forward(): pl.pallas_call(functools.partial(attend_kernel, pb, len(far)), grid=(pair...  44.2 us
    all_gather x1, waiting for transfers between devices, local(): last_array = lax.all_gather(rows_last, both, axis=0, tiled=True)  39.5 us
    all_gather x1, blocking collectives, local(): small = lax.all_gather(small, 'wa', axis=0, tiled=False)  38.9 us
    pallas_call x2, Pallas kernels, qkv_backward(): pl.pallas_call(functools.partial(qkv_pull_kernel, parts, len(sums[0]), le...  36.3 us
  transfers between devices with their start and end apart: 94, of which 38 were waited for; matrix products, arithmetic and copies ran while one was open for 3% of the time, Pallas kernels for 33%

profile of v4, /device:TPU:0, one launch (start us, length us, event | category | flops | bytes accessed | tf_op | source)
XLA Modules:
  0.0 888.8 jit_solution(8160758515076392722)
XLA Ops:
  11.4 4.7 collective-permute-start.3
  16.9 38.9 %all-gather.1 = bf16[8,2,1536]{2,1,0:T(2,128)(2,1)S(1)} all-gather(bf16[1,2,1536]{2,1,0:T(2,128)(2,1)S(1)} %bitcast.217), channel_id=2, replica_groups=mesh['tok'=4,'wa'=8] {'wa'}, dimensions={0}, use_global_device_ids=true | all-gather | bytes 55296 | tf_op jit(solution)/shard_map/all_gather | solution.py:900
  59.8 24.8 %collective-permute-done.4.refs_3_ = bf16[3,32,3072]{2,1,0:T(8,128)(2,1)S(1)} collective-permute-done((bf16[3,32,3072]{2,1,0:T(8,128)(2,1)S(1)}, bf16[3,32,3072]{2,1,0:T(8,128)(2,1)S(1)}, u32[]{:S(2)}, u32[]{:S(2)}) %collective-permute-start.4) | collective-permute-done | bytes 589856 | tf_op jit(solution)/shard_map/ppermute | solution.py:559
  85.1 22.3 %collective-permute-done.6.refs_5_ = bf16[3,32,3072]{2,1,0:T(8,128)(2,1)} collective-permute-done((bf16[3,32,3072]{2,1,0:T(8,128)(2,1)S(1)}, bf16[3,32,3072]{2,1,0:T(8,128)(2,1)}, u32[]{:S(2)}, u32[]{:S(2)}) %collective-permute-start.6) | collective-permute-done | bytes 589856 | tf_op jit(solution)/shard_map/ppermute | solution.py:559
  111.0 5.6 assemble.1
  119.3 9.9 %qkv_forward.2 = (bf16[512,3072]{1,0:T(8,128)(2,1)}, bf16[512,1024]{1,0:T(8,128)(2,1)}) custom-call(f32[512,1024]{1,0:T(8,128)} %maximum_convert_fusion.x_ref.refs_13_, f32[1,13312]{1,0:T(1,128)} %convert_element_type.103.gain_ref.shift_ref.bias_ref.refs_3_.refs_4_.refs_5_.refs_6_.refs_7_.refs_15_, ...), custom_call_target="tpu_custom_call" | custom-call | flops 3221225472 | bytes 16777216 | tf_op jit(solution)/shard_map/qkv_forward/pallas_call | solution.py:81
  134.8 21.8 %collective-permute-done.11.refs_4_ = bf16[2,256,512]{2,1,0:T(8,128)(2,1)S(1)} collective-permute-done((bf16[2,256,512]{2,1,0:T(8,128)(2,1)S(1)}, bf16[2,256,512]{2,1,0:T(8,128)(2,1)S(1)}, u32[]{:S(2)}, u32[]{:S(2)}) %collective-permute-start.11) | collective-permute-done | bytes 524320 | tf_op jit(solution)/shard_map/ppermute | solution.py:559
  157.4 21.5 %collective-permute-done.15.refs_4_ = bf16[2,256,512]{2,1,0:T(8,128)(2,1)S(1)} collective-permute-done((bf16[2,256,512]{2,1,0:T(8,128)(2,1)S(1)}, bf16[2,256,512]{2,1,0:T(8,128)(2,1)S(1)}, u32[]{:S(2)}, u32[]{:S(2)}) %collective-permute-start.15) | collective-permute-done | bytes 524320 | tf_op jit(solution)/shard_map/ppermute | solution.py:559
  187.8 4.6 collective-permute-done.13
  192.4 10.8 %collective-permute-done.17 = bf16[2,128,512]{2,1,0:T(8,128)(2,1)S(1)} collective-permute-done((bf16[2,128,512]{2,1,0:T(8,128)(2,1)S(1)}, bf16[2,128,512]{2,1,0:T(8,128)(2,1)S(1)}, u32[]{:S(2)}, u32[]{:S(2)}) %collective-permute-start.17) | collective-permute-done | bytes 262176 | tf_op jit(solution)/shard_map/ppermute | solution.py:559
  204.1 11.3 %attend_forward.4 = (bf16[512,512]{1,0:T(8,128)(2,1)}, f32[8,1,512]{2,1,0:T(1,128)}) custom-call(s32[4]{0:T(128)} %fusion.2.refs_0_, bf16[512,3072]{1,0:T(8,128)(2,1)} %get-tuple-element.192.refs_1_.refs_2_.refs_3_, bf16[512,3072]{1,0:T(8,128)(2,1)} %get-tuple-element.192.refs_1_.refs_2_.refs_3_, ...), custom_call_target="tpu_custom_call" | custom-call | flops 16106127360 | bytes 5242880 | tf_op jit(solution)/shard_map/attend_forward/pallas_call | solution.py:158
  215.5 10.9 %attend_forward.5 = (bf16[512,512]{1,0:T(8,128)(2,1)}, f32[8,1,512]{2,1,0:T(1,128)}) custom-call(s32[4]{0:T(128)} %fusion.2.refs_0_, bf16[512,3072]{1,0:T(8,128)(2,1)} %get-tuple-element.192.refs_1_.refs_2_.refs_3_, bf16[512,3072]{1,0:T(8,128)(2,1)} %get-tuple-element.192.refs_1_.refs_2_.refs_3_, ...), custom_call_target="tpu_custom_call" | custom-call | flops 16106127360 | bytes 5242880 | tf_op jit(solution)/shard_map/attend_forward/pallas_call | solution.py:158
  226.4 6.5 all-gather.5.cloned.1.call-done.refs_2_.refs_8_.w_ref.refs_16_.refs_4_.refs_7_
  232.9 17.6 %feed_forward.2 = (f32[512,1024]{1,0:T(8,128)}, f32[512,1024]{1,0:T(8,128)}, bf16[512,1024]{1,0:T(8,128)(2,1)}, bf16[512,4096]{1,0:T(8,128)(2,1)}) custom-call(f32[512,1024]{1,0:T(8,128)} %maximum_convert_fusion.x_ref.refs_13_, bf16[512,512]{1,0:T(8,128)(2,1)} %get-tuple-element.193.refs_0_.refs_9_, bf16[512,512]{1,0:T(8,128)(2,1)} %get-tuple-element.194.refs_1_.refs_9_, ...), custom_call_target="tpu_custom_call" | custom-call | flops 9663676416 | bytes 31457280 | tf_op jit(solution)/shard_map/feed_forward/pallas_call | solution.py:288
  250.5 9.6 %qkv_forward.3 = (bf16[512,3072]{1,0:T(8,128)(2,1)}, bf16[512,1024]{1,0:T(8,128)(2,1)}) custom-call(f32[512,1024]{1,0:T(8,128)} %get-tuple-element.196.x_ref.refs_13_, f32[1,13312]{1,0:T(1,128)} %convert_element_type.104.gain_ref.shift_ref.bias_ref.refs_3_.refs_4_.refs_5_.refs_6_.refs_7_.refs_15_, ...), custom_call_target="tpu_custom_call" | custom-call | flops 3221225472 | bytes 16777216 | tf_op jit(solution)/shard_map/qkv_forward/pallas_call | solution.py:81
  265.6 19.8 %collective-permute-done.19.refs_4_ = bf16[2,256,512]{2,1,0:T(8,128)(2,1)S(1)} collective-permute-done((bf16[2,256,512]{2,1,0:T(8,128)(2,1)S(1)}, bf16[2,256,512]{2,1,0:T(8,128)(2,1)S(1)}, u32[]{:S(2)}, u32[]{:S(2)}) %collective-permute-start.19) | collective-permute-done | bytes 524320 | tf_op jit(solution)/shard_map/ppermute | solution.py:559
  288.2 16.2 %collective-permute-done.23.refs_4_ = bf16[2,256,512]{2,1,0:T(8,128)(2,1)S(1)} collective-permute-done((bf16[2,256,512]{2,1,0:T(8,128)(2,1)S(1)}, bf16[2,256,512]{2,1,0:T(8,128)(2,1)S(1)}, u32[]{:S(2)}, u32[]{:S(2)}) %collective-permute-start.23) | collective-permute-done | bytes 524320 | tf_op jit(solution)/shard_map/ppermute | solution.py:559
  314.9 11.1 %attend_forward.6 = (bf16[512,512]{1,0:T(8,128)(2,1)}, f32[8,1,512]{2,1,0:T(1,128)}) custom-call(s32[4]{0:T(128)} %fusion.2.refs_0_, bf16[512,3072]{1,0:T(8,128)(2,1)} %get-tuple-element.197.refs_1_.refs_2_.refs_3_, bf16[512,3072]{1,0:T(8,128)(2,1)} %get-tuple-element.197.refs_1_.refs_2_.refs_3_, ...), custom_call_target="tpu_custom_call" | custom-call | flops 16106127360 | bytes 5242880 | tf_op jit(solution)/shard_map/attend_forward/pallas_call | solution.py:158
  326.0 10.9 %attend_forward.7 = (bf16[512,512]{1,0:T(8,128)(2,1)}, f32[8,1,512]{2,1,0:T(1,128)}) custom-call(s32[4]{0:T(128)} %fusion.2.refs_0_, bf16[512,3072]{1,0:T(8,128)(2,1)} %get-tuple-element.197.refs_1_.refs_2_.refs_3_, bf16[512,3072]{1,0:T(8,128)(2,1)} %get-tuple-element.197.refs_1_.refs_2_.refs_3_, ...), custom_call_target="tpu_custom_call" | custom-call | flops 16106127360 | bytes 5242880 | tf_op jit(solution)/shard_map/attend_forward/pallas_call | solution.py:158
  336.9 39.5 %all-gather.7.cloned.1.call-done.refs_2_.refs_8_.refs_4_.refs_7_ = bf16[1024,9216]{1,0:T(8,128)(2,1)} async-done(((bf16[32,9216]{1,0:T(8,128)(2,1)}), bf16[1024,9216]{1,0:T(8,128)(2,1)}) %all-gather.7.cloned.1.call-update) | async-done | bytes 18874384 | tf_op jit(solution)/shard_map/all_gather | solution.py:923
  376.4 17.6 %feed_forward.3 = (f32[512,1024]{1,0:T(8,128)}, f32[512,1024]{1,0:T(8,128)}, bf16[512,1024]{1,0:T(8,128)(2,1)}, bf16[512,4096]{1,0:T(8,128)(2,1)}) custom-call(f32[512,1024]{1,0:T(8,128)} %get-tuple-element.196.x_ref.refs_13_, bf16[512,512]{1,0:T(8,128)(2,1)} %get-tuple-element.198.refs_0_.refs_9_, bf16[512,512]{1,0:T(8,128)(2,1)} %get-tuple-element.199.refs_1_.refs_9_, ...), custom_call_target="tpu_custom_call" | custom-call | flops 9663676416 | bytes 31457280 | tf_op jit(solution)/shard_map/feed_forward/pallas_call | solution.py:288
  394.0 23.0 %feed_backward.4 = (bf16[1024,6144]{1,0:T(8,128)(2,1)}, f32[1,3072]{1,0:T(1,128)}, f32[512,1024]{1,0:T(8,128)}, f32[1,1024]{1,0:T(1,128)}) custom-call(s32[1]{0:T(128)} %bitcast.45.core_ref, f32[512,1024]{1,0:T(8,128)} %maximum_convert_fusion.1.gs_ref, bf16[512,4096]{1,0:T(8,128)(2,1)} %get-tuple-element.204.refs_0_.refs_2_, ...), custom_call_target="tpu_custom_call" | custom-call | flops 12884901888 | bytes 31457280 | tf_op jit(solution)/shard_map/feed_backward/pallas_call | solution.py:465
  417.1 19.8 %feed_backward.5 = (bf16[4,128,3072]{2,1,0:T(8,128)(2,1)}, bf16[4,128,3072]{2,1,0:T(8,128)(2,1)}, f32[1,1024]{1,0:T(1,128)}, f32[512,1024]{1,0:T(8,128)}, bf16[5...) custom-call(s32[1]{0:T(128)} %bitcast.45.core_ref, ...), custom_call_target="tpu_custom_call" | custom-call | flops 6442450944 | bytes 15728640 | tf_op jit(solution)/shard_map/feed_backward/pallas_call | solution.py:465
  437.2 16.7 %attend_backward.4 = (bf16[512,512]{1,0:T(8,128)(2,1)}, bf16[2,256,512]{2,1,0:T(8,128)(2,1)}, bf16[2,256,512]{2,1,0:T(8,128)(2,1)}, bf16[2,256,512]{2,1,0:T(8,12...) custom-call(s32[4]{0:T(128)} %fusion.2.refs_0_, ...), custom_call_target="tpu_custom_call" | custom-call | flops 26843545600 | bytes 9437184 | tf_op jit(solution)/shard_map/attend_backward/pallas_call | solution.py:237
  457.5 16.4 %attend_backward.5 = (bf16[512,512]{1,0:T(8,128)(2,1)}, bf16[2,256,512]{2,1,0:T(8,128)(2,1)}, bf16[2,256,512]{2,1,0:T(8,128)(2,1)}, bf16[2,256,512]{2,1,0:T(8,12...) custom-call(s32[4]{0:T(128)} %fusion.2.refs_0_, ...), custom_call_target="tpu_custom_call" | custom-call | flops 26843545600 | bytes 9437184 | tf_op jit(solution)/shard_map/attend_backward/pallas_call | solution.py:237
  485.2 6.3 collective-permute-done.31.refs_9_
  491.6 11.4 %collective-permute-done.32.refs_10_ = bf16[2,256,512]{2,1,0:T(8,128)(2,1)} collective-permute-done((bf16[2,256,512]{2,1,0:T(8,128)(2,1)}, bf16[2,256,512]{2,1,0:T(8,128)(2,1)}, u32[]{:S(2)}, u32[]{:S(2)}) %collective-permute-start.32) | collective-permute-done | bytes 524320 | tf_op jit(solution)/shard_map/ppermute | solution.py:559
  503.7 18.2 %qkv_backward.2 = (bf16[4,128,3072]{2,1,0:T(8,128)(2,1)}, bf16[4,128,3072]{2,1,0:T(8,128)(2,1)}, f32[512,1024]{1,0:T(8,128)}, f32[1,3072]{1,0:T(1,128)}, f32[1,1024]{1,0:T(1,128)}, /*index=5*/f32[1,1024]{1,0:T(1,128)}) custom-call(s32[1]{0:T(128)} %bitcast.45.core_ref, bf16[512,512]{1,0:T(8,128)(2,1)} %get-tuple-element.209.refs_0_, ...), custom_call_target="tpu_custom_call" | custom-call | flops 6442450944 | bytes 25165824 | tf_op jit(solution)/shard_map/qkv_backward/pallas_call | solution.py:521
  526.0 23.0 %feed_backward.6 = (bf16[1024,6144]{1,0:T(8,128)(2,1)}, f32[1,3072]{1,0:T(1,128)}, f32[512,1024]{1,0:T(8,128)}, f32[1,1024]{1,0:T(1,128)}) custom-call(s32[1]{0:T(128)} %bitcast.45.core_ref, f32[512,1024]{1,0:T(8,128)} %get-tuple-element.236.gs_ref, bf16[512,4096]{1,0:T(8,128)(2,1)} %get-tuple-element.237.refs_0_.refs_2_, ...), custom_call_target="tpu_custom_call" | custom-call | flops 12884901888 | bytes 31457280 | tf_op jit(solution)/shard_map/feed_backward/pallas_call | solution.py:465
  551.2 9.6 %collective-permute-done.36.refs_1_ = bf16[4,1,32,1536]{3,2,1,0:T(8,128)(2,1)S(1)} collective-permute-done((bf16[4,1,32,1536]{3,2,1,0:T(8,128)(2,1)}, bf16[4,1,32,1536]{3,2,1,0:T(8,128)(2,1)S(1)}, u32[]{:S(2)}, u32[]{:S(2)}) %collective-permute-start.36) | collective-permute-done | bytes 393248 | tf_op jit(solution)/shard_map/ppermute | solution.py:559
  578.6 18.4 %feed_backward.7 = (bf16[4,128,3072]{2,1,0:T(8,128)(2,1)}, bf16[4,128,3072]{2,1,0:T(8,128)(2,1)}, f32[1,1024]{1,0:T(1,128)}, f32[512,1024]{1,0:T(8,128)}, bf16[5...) custom-call(s32[1]{0:T(128)} %bitcast.45.core_ref, ...), custom_call_target="tpu_custom_call" | custom-call | flops 6442450944 | bytes 15728640 | tf_op jit(solution)/shard_map/feed_backward/pallas_call | solution.py:465
  598.3 6.9 collective-permute-done.48
  607.4 8.1 collective-permute-done.45
  621.9 16.7 %attend_backward.6 = (bf16[512,512]{1,0:T(8,128)(2,1)}, bf16[2,256,512]{2,1,0:T(8,128)(2,1)}, bf16[2,256,512]{2,1,0:T(8,128)(2,1)}, bf16[2,256,512]{2,1,0:T(8,12...) custom-call(s32[4]{0:T(128)} %fusion.2.refs_0_, ...), custom_call_target="tpu_custom_call" | custom-call | flops 26843545600 | bytes 9437184 | tf_op jit(solution)/shard_map/attend_backward/pallas_call | solution.py:237
  647.8 16.6 %attend_backward.7 = (bf16[512,512]{1,0:T(8,128)(2,1)}, bf16[2,256,512]{2,1,0:T(8,128)(2,1)}, bf16[2,256,512]{2,1,0:T(8,128)(2,1)}, bf16[2,256,512]{2,1,0:T(8,12...) custom-call(s32[4]{0:T(128)} %fusion.2.refs_0_, ...), custom_call_target="tpu_custom_call" | custom-call | flops 26843545600 | bytes 9437184 | tf_op jit(solution)/shard_map/attend_backward/pallas_call | solution.py:237
  665.0 9.6 %collective-permute-done.51 = bf16[32,3072]{1,0:T(8,128)(2,1)S(1)} collective-permute-done((bf16[32,3072]{1,0:T(8,128)(2,1)}, bf16[32,3072]{1,0:T(8,128)(2,1)S(1)}, u32[]{:S(2)}, u32[]{:S(2)}) %collective-permute-start.51) | collective-permute-done | bytes 196640 | tf_op jit(solution)/shard_map/ppermute | solution.py:559
  680.0 4.5 split_sum.10
  684.5 5.9 collective-permute-done.55.refs_7_
  690.4 11.3 %collective-permute-done.56.refs_9_ = bf16[2,256,512]{2,1,0:T(8,128)(2,1)} collective-permute-done((bf16[2,256,512]{2,1,0:T(8,128)(2,1)}, bf16[2,256,512]{2,1,0:T(8,128)(2,1)}, u32[]{:S(2)}, u32[]{:S(2)}) %collective-permute-start.56) | collective-permute-done | bytes 524320 | tf_op jit(solution)/shard_map/ppermute | solution.py:559
  701.7 8.7 collective-permute-done.58.refs_11_
  710.4 18.1 %qkv_backward.3 = (bf16[1024,3072]{1,0:T(8,128)(2,1)}, f32[512,1024]{1,0:T(8,128)}, f32[1,3072]{1,0:T(1,128)}, f32[1,1024]{1,0:T(1,128)}, f32[1,1024]{1,0:T(1,128)}) custom-call(s32[1]{0:T(128)} %bitcast.45.core_ref, bf16[512,512]{1,0:T(8,128)(2,1)} %get-tuple-element.263.refs_0_, bf16[512,512]{1,0:T(8,128)(2,1)} %get-tuple-element.274.refs_1_, ...), custom_call_target="tpu_custom_call" | custom-call | flops 6442450944 | bytes 25165824 | tf_op jit(solution)/shard_map/qkv_backward/pallas_call | solution.py:521
  742.1 11.2 %collective-permute-done.64.refs_1_ = bf16[4,2,32,1536]{3,2,1,0:T(8,128)(2,1)S(1)} collective-permute-done((bf16[4,2,32,1536]{3,2,1,0:T(8,128)(2,1)}, bf16[4,2,32,1536]{3,2,1,0:T(8,128)(2,1)S(1)}, u32[]{:S(2)}, u32[]{:S(2)}) %collective-permute-start.64) | collective-permute-done | bytes 786464 | tf_op jit(solution)/shard_map/ppermute | solution.py:559
  780.4 5.7 collective-permute-done.70
  787.5 13.6 %collective-permute-done.69 = bf16[32,3072]{1,0:T(8,128)(2,1)S(1)} collective-permute-done((bf16[32,3072]{1,0:T(8,128)(2,1)}, bf16[32,3072]{1,0:T(8,128)(2,1)S(1)}, u32[]{:S(2)}, u32[]{:S(2)}) %collective-permute-start.69) | collective-permute-done | bytes 196640 | tf_op jit(solution)/shard_map/ppermute | solution.py:559
  803.2 8.5 reduce-scatter.8.cloned.1.call-done
  821.0 17.6 %collective-permute-done.73 = bf16[32,3072]{1,0:T(8,128)(2,1)S(1)} collective-permute-done((bf16[32,3072]{1,0:T(8,128)(2,1)S(1)}, bf16[32,3072]{1,0:T(8,128)(2,1)S(1)}, u32[]{:S(2)}, u32[]{:S(2)}) %collective-permute-start.73) | collective-permute-done | bytes 196640 | tf_op jit(solution)/shard_map/ppermute | solution.py:559
  845.1 6.2 collective-permute-done.83.refs_1_
  852.8 8.0 collective-permute-done.84.refs_2_
  (469 shorter events, 197.2 us)
Async XLA Ops:
  7.2 225.7 %all-gather.5.cloned.1.call-start = ((), (), s32[]{:S(2)}) async-start(), calls=%async_computation.3 | async-start | bytes 25952256 | tf_op jit(solution)/shard_map/all_gather | solution.py:922
  10.0 366.4 %all-gather.7.cloned.1.call-start = ((), (), s32[]{:S(2)}) async-start(), calls=%async_computation.4 | async-start | bytes 19464192 | tf_op jit(solution)/shard_map/all_gather | solution.py:923
  10.7 559.5 %reduce-scatter.4.cloned.1.call-start = ((), (), s32[]{:S(2)}) async-start(), calls=%async_computation.5 | async-start | bytes 14155776 | tf_op jit(solution)/shard_map/reduce_scatter | solution.py:975
  10.8 100.2 %collective-permute-start = (bf16[4,32,3072]{2,1,0:T(8,128)(2,1)S(1)}, bf16[4,32,3072]{2,1,0:T(8,128)(2,1)S(1)}, u32[]{:S(2)}, u32[]{:S(2)}) collective-permute-start(bf16[4,32,3072]{2,1,0:T(8,128)(2,1)S(1)} %bitcast.178), channel_id=1, source_target_pairs={{0,1},{1,0},{2,3},{3,2},{4,5},{5,4},{6,7},{7,6},{8,9},{9,8},{10,11... | collective-permute-start | bytes 2359304 | tf_op jit(solution)/shard_map/ppermute | solution.py:559
  11.4 44.6 %collective-permute-start.3 = (bf16[32,3072]{1,0:T(8,128)(2,1)S(1)}, bf16[32,3072]{1,0:T(8,128)(2,1)S(1)}, u32[]{:S(2)}, u32[]{:S(2)}) collective-permute-start(bf16[32,3072]{1,0:T(8,128)(2,1)S(1)} %dynamic-slice_bitcast_fusion.12), channel_id=1, source_target_pairs={{0,6},{1,7},{2,4},{3,5},{4,2},{5,3},{6,0},{7,1},{8,14},{9,15},{10,... | collective-permute-start | bytes 589832 | tf_op jit(solution)/shard_map/ppermute | solution.py:559
  16.1 39.9 %collective-permute-start.2 = (bf16[32,3072]{1,0:T(8,128)(2,1)S(1)}, bf16[32,3072]{1,0:T(8,128)(2,1)S(1)}, u32[]{:S(2)}, u32[]{:S(2)}) collective-permute-start(bf16[32,3072]{1,0:T(8,128)(2,1)S(1)} %dynamic-slice_bitcast_fusion.12), channel_id=1, source_target_pairs={{0,4},{1,5},{2,6},{3,7},{4,0},{5,1},{6,2},{7,3},{8,12},{9,13},{10,... | collective-permute-start | bytes 589832 | tf_op jit(solution)/shard_map/ppermute | solution.py:559
  16.1 39.9 %collective-permute-start.1 = (bf16[32,3072]{1,0:T(8,128)(2,1)S(1)}, bf16[32,3072]{1,0:T(8,128)(2,1)S(1)}, u32[]{:S(2)}, u32[]{:S(2)}) collective-permute-start(bf16[32,3072]{1,0:T(8,128)(2,1)S(1)} %dynamic-slice_bitcast_fusion.12), channel_id=1, source_target_pairs={{0,2},{1,3},{2,0},{3,1},{4,6},{5,7},{6,4},{7,5},{8,10},{9,11},{10,... | collective-permute-start | bytes 589832 | tf_op jit(solution)/shard_map/ppermute | solution.py:559
  56.1 28.5 %collective-permute-start.4 = (bf16[3,32,3072]{2,1,0:T(8,128)(2,1)S(1)}, bf16[3,32,3072]{2,1,0:T(8,128)(2,1)S(1)}, u32[]{:S(2)}, u32[]{:S(2)}) collective-permute-start(bf16[3,32,3072]{2,1,0:T(8,128)(2,1)S(1)} %pad_maximum_fusion.1.refs_2_), channel_id=1, source_target_pairs={{0,8},{8,0},{16,24},{24,16},{1,9},{9,1},{17,25},{25,17},{2,10},{10... | collective-permute-start | bytes 1769480 | tf_op jit(solution)/shard_map/ppermute | solution.py:559
  57.6 26.9 %collective-permute-start.5 = (bf16[3,32,3072]{2,1,0:T(8,128)(2,1)S(1)}, bf16[3,32,3072]{2,1,0:T(8,128)(2,1)S(1)}, u32[]{:S(2)}, u32[]{:S(2)}) collective-permute-start(bf16[3,32,3072]{2,1,0:T(8,128)(2,1)S(1)} %pad_maximum_fusion.1.refs_2_), channel_id=1, source_target_pairs={{0,16},{8,24},{16,0},{24,8},{1,17},{9,25},{17,1},{25,9},{2,18},{10... | collective-permute-start | bytes 1769480 | tf_op jit(solution)/shard_map/ppermute | solution.py:559
  59.2 48.1 %collective-permute-start.6 = (bf16[3,32,3072]{2,1,0:T(8,128)(2,1)S(1)}, bf16[3,32,3072]{2,1,0:T(8,128)(2,1)}, u32[]{:S(2)}, u32[]{:S(2)}) collective-permute-start(bf16[3,32,3072]{2,1,0:T(8,128)(2,1)S(1)} %pad_maximum_fusion.1.refs_2_), channel_id=1, source_target_pairs={{0,24},{8,16},{16,8},{24,0},{1,25},{9,17},{17,9},{25,1},{2,26},{10... | collective-permute-start | bytes 1769480 | tf_op jit(solution)/shard_map/ppermute | solution.py:559
  59.7 51.3 %collective-permute-start.7 = (bf16[3,32,3072]{2,1,0:T(8,128)(2,1)S(1)}, bf16[3,32,3072]{2,1,0:T(8,128)(2,1)}, u32[]{:S(2)}, u32[]{:S(2)}) collective-permute-start(bf16[3,32,3072]{2,1,0:T(8,128)(2,1)S(1)} %pad_maximum_fusion.1.refs_2_), channel_id=1, source_target_pairs={{0,1},{1,0},{2,3},{3,2},{4,5},{5,4},{6,7},{7,6},{8,9},{9,8},{10,11... | collective-permute-start | bytes 1769480 | tf_op jit(solution)/shard_map/ppermute | solution.py:559
  84.5 26.5 %collective-permute-start.8 = (bf16[3,32,3072]{2,1,0:T(8,128)(2,1)S(1)}, bf16[3,32,3072]{2,1,0:T(8,128)(2,1)}, u32[]{:S(2)}, u32[]{:S(2)}) collective-permute-start(bf16[3,32,3072]{2,1,0:T(8,128)(2,1)S(1)} %collective-permute-done.4.refs_3_), channel_id=1, source_target_pairs={{0,1},{1,0},{2,3},{3,2},{4,5},{5,4},{6,7},{7,6},{8,9},{9,8},{10,11... | collective-permute-start | bytes 1769480 | tf_op jit(solution)/shard_map/ppermute | solution.py:559
  84.5 26.5 %collective-permute-start.9 = (bf16[3,32,3072]{2,1,0:T(8,128)(2,1)S(1)}, bf16[3,32,3072]{2,1,0:T(8,128)(2,1)}, u32[]{:S(2)}, u32[]{:S(2)}) collective-permute-start(bf16[3,32,3072]{2,1,0:T(8,128)(2,1)S(1)} %collective-permute-done.5.refs_4_), channel_id=1, source_target_pairs={{0,1},{1,0},{2,3},{3,2},{4,5},{5,4},{6,7},{7,6},{8,9},{9,8},{10,11... | collective-permute-start | bytes 1769480 | tf_op jit(solution)/shard_map/ppermute | solution.py:559
  130.5 26.1 %collective-permute-start.11 = (bf16[2,256,512]{2,1,0:T(8,128)(2,1)S(1)}, bf16[2,256,512]{2,1,0:T(8,128)(2,1)S(1)}, u32[]{:S(2)}, u32[]{:S(2)}) collective-permute-start(bf16[2,256,512]{2,1,0:T(8,128)(2,1)S(1)} %pad_maximum_fusion.2), channel_id=1, source_target_pairs={{0,8},{8,0},{16,24},{24,16},{1,9},{9,1},{17,25},{25,17},{2,10},{10... | collective-permute-start | bytes 1572872 | tf_op jit(solution)/shard_map/ppermute | solution.py:559
  131.1 47.8 %collective-permute-start.15 = (bf16[2,256,512]{2,1,0:T(8,128)(2,1)S(1)}, bf16[2,256,512]{2,1,0:T(8,128)(2,1)S(1)}, u32[]{:S(2)}, u32[]{:S(2)}) collective-permute-start(bf16[2,256,512]{2,1,0:T(8,128)(2,1)S(1)} %pad_maximum_fusion.3), channel_id=1, source_target_pairs={{0,8},{8,0},{16,24},{24,16},{1,9},{9,1},{17,25},{25,17},{2,10},{10... | collective-permute-start | bytes 1572872 | tf_op jit(solution)/shard_map/ppermute | solution.py:559
  132.7 47.4 %collective-permute-start.12 = (bf16[2,256,512]{2,1,0:T(8,128)(2,1)S(1)}, bf16[2,256,512]{2,1,0:T(8,128)(2,1)}, u32[]{:S(2)}, u32[]{:S(2)}) collective-permute-start(bf16[2,256,512]{2,1,0:T(8,128)(2,1)S(1)} %pad_maximum_fusion.2), channel_id=1, source_target_pairs={{0,16},{8,24},{16,0},{24,8},{1,17},{9,25},{17,1},{25,9},{2,18},{10... | collective-permute-start | bytes 1572872 | tf_op jit(solution)/shard_map/ppermute | solution.py:559
  133.2 52.8 %collective-permute-start.16 = (bf16[2,256,512]{2,1,0:T(8,128)(2,1)S(1)}, bf16[2,256,512]{2,1,0:T(8,128)(2,1)S(1)}, u32[]{:S(2)}, u32[]{:S(2)}) collective-permute-start(bf16[2,256,512]{2,1,0:T(8,128)(2,1)S(1)} %pad_maximum_fusion.3), channel_id=1, source_target_pairs={{0,16},{8,24},{16,0},{24,8},{1,17},{9,25},{17,1},{25,9},{2,18},{10... | collective-permute-start | bytes 1572872 | tf_op jit(solution)/shard_map/ppermute | solution.py:559
  156.6 35.8 %collective-permute-start.13 = (bf16[2,128,512]{2,1,0:T(8,128)(2,1)S(1)}, bf16[2,128,512]{2,1,0:T(8,128)(2,1)S(1)}, u32[]{:S(2)}, u32[]{:S(2)}) collective-permute-start(bf16[2,128,512]{2,1,0:T(8,128)(2,1)S(1)} %slice.222), channel_id=1, source_target_pairs={{0,16},{8,24},{16,0},{24,8},{1,17},{9,25},{17,1},{25,9},{2,18},{10... | collective-permute-start | bytes 786440 | tf_op jit(solution)/shard_map/ppermute | solution.py:559
  263.5 40.8 %collective-permute-start.23 = (bf16[2,256,512]{2,1,0:T(8,128)(2,1)S(1)}, bf16[2,256,512]{2,1,0:T(8,128)(2,1)S(1)}, u32[]{:S(2)}, u32[]{:S(2)}) collective-permute-start(bf16[2,256,512]{2,1,0:T(8,128)(2,1)S(1)} %pad_maximum_fusion.5), channel_id=1, source_target_pairs={{0,8},{8,0},{16,24},{24,16},{1,9},{9,1},{17,25},{25,17},{2,10},{10... | collective-permute-start | bytes 1572872 | tf_op jit(solution)/shard_map/ppermute | solution.py:559
  264.2 42.4 %collective-permute-start.24 = (bf16[2,256,512]{2,1,0:T(8,128)(2,1)S(1)}, bf16[2,256,512]{2,1,0:T(8,128)(2,1)S(1)}, u32[]{:S(2)}, u32[]{:S(2)}) collective-permute-start(bf16[2,256,512]{2,1,0:T(8,128)(2,1)S(1)} %pad_maximum_fusion.5), channel_id=1, source_target_pairs={{0,16},{8,24},{16,0},{24,8},{1,17},{9,25},{17,1},{25,9},{2,18},{10... | collective-permute-start | bytes 1572872 | tf_op jit(solution)/shard_map/ppermute | solution.py:559
  417.1 322.7 %reduce-scatter.6.cloned.1.call-start = ((), (), s32[]{:S(2)}) async-start(), calls=%async_computation.6 | async-start | bytes 14155776 | tf_op jit(solution)/shard_map/reduce_scatter | solution.py:975
  436.9 38.6 %collective-permute-start.27 = (bf16[4,128,3072]{2,1,0:T(8,128)(2,1)}, bf16[4,128,3072]{2,1,0:T(8,128)(2,1)S(1)}, u32[]{:S(2)}, u32[]{:S(2)}) collective-permute-start(bf16[4,128,3072]{2,1,0:T(8,128)(2,1)} %get-tuple-element.215), channel_id=1, source_target_pairs={{0,1},{1,0},{2,3},{3,2},{4,5},{5,4},{6,7},{7,6},{8,9},{9,8},{10,11... | collective-permute-start | bytes 9437192 | tf_op jit(solution)/shard_map/ppermute | solution.py:559
  455.4 27.1 %collective-permute-start.29 = (bf16[2,256,512]{2,1,0:T(8,128)(2,1)}, bf16[2,256,512]{2,1,0:T(8,128)(2,1)}, u32[]{:S(2)}, u32[]{:S(2)}) collective-permute-start(bf16[2,256,512]{2,1,0:T(8,128)(2,1)} %get-tuple-element.221), channel_id=1, source_target_pairs={{0,16},{8,24},{16,0},{24,8},{1,17},{9,25},{17,1},{25,9},{2,18},{10... | collective-permute-start | bytes 1572872 | tf_op jit(solution)/shard_map/ppermute | solution.py:559
  455.5 28.4 %collective-permute-start.30 = (bf16[2,256,512]{2,1,0:T(8,128)(2,1)}, bf16[2,256,512]{2,1,0:T(8,128)(2,1)}, u32[]{:S(2)}, u32[]{:S(2)}) collective-permute-start(bf16[2,256,512]{2,1,0:T(8,128)(2,1)} %get-tuple-element.222), channel_id=1, source_target_pairs={{0,24},{8,16},{16,8},{24,0},{1,25},{9,17},{17,9},{25,1},{2,26},{10... | collective-permute-start | bytes 1572872 | tf_op jit(solution)/shard_map/ppermute | solution.py:559
  475.4 27.6 %collective-permute-start.32 = (bf16[2,256,512]{2,1,0:T(8,128)(2,1)}, bf16[2,256,512]{2,1,0:T(8,128)(2,1)}, u32[]{:S(2)}, u32[]{:S(2)}) collective-permute-start(bf16[2,256,512]{2,1,0:T(8,128)(2,1)} %get-tuple-element.225), channel_id=1, source_target_pairs={{0,16},{8,24},{16,0},{24,8},{1,17},{9,25},{17,1},{25,9},{2,18},{10... | collective-permute-start | bytes 1572872 | tf_op jit(solution)/shard_map/ppermute | solution.py:559
  476.2 27.5 %collective-permute-start.33 = (bf16[2,256,512]{2,1,0:T(8,128)(2,1)}, bf16[2,256,512]{2,1,0:T(8,128)(2,1)}, u32[]{:S(2)}, u32[]{:S(2)}) collective-permute-start(bf16[2,256,512]{2,1,0:T(8,128)(2,1)} %get-tuple-element.226), channel_id=1, source_target_pairs={{0,24},{8,16},{16,8},{24,0},{1,25},{9,17},{17,9},{25,1},{2,26},{10... | collective-permute-start | bytes 1572872 | tf_op jit(solution)/shard_map/ppermute | solution.py:559
  482.5 39.4 %collective-permute-start.34 = (bf16[4,2,32,1536]{3,2,1,0:T(8,128)(2,1)}, bf16[4,2,32,1536]{3,2,1,0:T(8,128)(2,1)S(1)}, u32[]{:S(2)}, u32[]{:S(2)}) collective-permute-start(bf16[4,2,32,1536]{3,2,1,0:T(8,128)(2,1)} %get-tuple-element.231), channel_id=1, source_target_pairs={{0,8},{8,0},{16,24},{24,16},{1,9},{9,1},{17,25},{25,17},{2,10},{10... | collective-permute-start | bytes 2359304 | tf_op jit(solution)/shard_map/ppermute | solution.py:559
  483.9 38.1 %collective-permute-start.35 = (bf16[4,2,32,1536]{3,2,1,0:T(8,128)(2,1)}, bf16[4,2,32,1536]{3,2,1,0:T(8,128)(2,1)S(1)}, u32[]{:S(2)}, u32[]{:S(2)}) collective-permute-start(bf16[4,2,32,1536]{3,2,1,0:T(8,128)(2,1)} %get-tuple-element.233), channel_id=1, source_target_pairs={{0,16},{8,24},{16,0},{24,8},{1,17},{9,25},{17,1},{25,9},{2,18},{10... | collective-permute-start | bytes 2359304 | tf_op jit(solution)/shard_map/ppermute | solution.py:559
  549.0 262.7 %reduce-scatter.8.cloned.1.call-start = ((), (), s32[]{:S(2)}) async-start(), calls=%async_computation.7 | async-start | bytes 7077888 | tf_op jit(solution)/shard_map/reduce_scatter | solution.py:1005
  571.9 43.9 %collective-permute-start.39 = (bf16[4,2,32,1536]{3,2,1,0:T(8,128)(2,1)S(1)}, bf16[4,2,32,1536]{3,2,1,0:T(8,128)(2,1)S(1)}, u32[]{:S(2)}, u32[]{:S(2)}) collective-permute-start(bf16[4,2,32,1536]{3,2,1,0:T(8,128)(2,1)S(1)} %copy-done.73), channel_id=1, source_target_pairs={{0,8},{8,0},{16,24},{24,16},{1,9},{9,1},{17,25},{25,17},{2,10},{10... | collective-permute-start | bytes 2359304 | tf_op jit(solution)/shard_map/ppermute | solution.py:559
  573.2 42.6 %collective-permute-start.40 = (bf16[4,2,32,1536]{3,2,1,0:T(8,128)(2,1)S(1)}, bf16[4,2,32,1536]{3,2,1,0:T(8,128)(2,1)S(1)}, u32[]{:S(2)}, u32[]{:S(2)}) collective-permute-start(bf16[4,2,32,1536]{3,2,1,0:T(8,128)(2,1)S(1)} %copy-done.72), channel_id=1, source_target_pairs={{0,16},{8,24},{16,0},{24,8},{1,17},{9,25},{17,1},{25,9},{2,18},{10... | collective-permute-start | bytes 2359304 | tf_op jit(solution)/shard_map/ppermute | solution.py:559
  574.6 30.5 %collective-permute-start.48 = (bf16[32,3072]{1,0:T(8,128)(2,1)S(1)}, bf16[32,3072]{1,0:T(8,128)(2,1)S(1)}, u32[]{:S(2)}, u32[]{:S(2)}) collective-permute-start(bf16[32,3072]{1,0:T(8,128)(2,1)S(1)} %copy-done.81), channel_id=1, source_target_pairs={{0,4},{1,5},{2,6},{3,7},{4,0},{5,1},{6,2},{7,3},{8,12},{9,13},{10,... | collective-permute-start | bytes 589832 | tf_op jit(solution)/shard_map/ppermute | solution.py:559
  574.8 31.4 %collective-permute-start.47 = (bf16[32,3072]{1,0:T(8,128)(2,1)S(1)}, bf16[32,3072]{1,0:T(8,128)(2,1)S(1)}, u32[]{:S(2)}, u32[]{:S(2)}) collective-permute-start(bf16[32,3072]{1,0:T(8,128)(2,1)S(1)} %copy-done.80), channel_id=1, source_target_pairs={{0,2},{1,3},{2,0},{3,1},{4,6},{5,7},{6,4},{7,5},{8,10},{9,11},{10,... | collective-permute-start | bytes 589832 | tf_op jit(solution)/shard_map/ppermute | solution.py:559
  607.3 71.0 %collective-permute-start.43 = (bf16[4,128,3072]{2,1,0:T(8,128)(2,1)}, bf16[4,128,3072]{2,1,0:T(8,128)(2,1)S(1)}, u32[]{:S(2)}, u32[]{:S(2)}) collective-permute-start(bf16[4,128,3072]{2,1,0:T(8,128)(2,1)} %get-tuple-element.278), channel_id=1, source_target_pairs={{0,1},{1,0},{2,3},{3,2},{4,5},{5,4},{6,7},{7,6},{8,9},{9,8},{10,11... | collective-permute-start | bytes 9437192 | tf_op jit(solution)/shard_map/ppermute | solution.py:559
  638.6 39.0 %collective-permute-start.53 = (bf16[2,256,512]{2,1,0:T(8,128)(2,1)}, bf16[2,256,512]{2,1,0:T(8,128)(2,1)S(1)}, u32[]{:S(2)}, u32[]{:S(2)}) collective-permute-start(bf16[2,256,512]{2,1,0:T(8,128)(2,1)} %get-tuple-element.296), channel_id=1, source_target_pairs={{0,8},{8,0},{16,24},{24,16},{1,9},{9,1},{17,25},{25,17},{2,10},{10... | collective-permute-start | bytes 1572872 | tf_op jit(solution)/shard_map/ppermute | solution.py:559
  645.9 28.7 %collective-permute-start.51 = (bf16[32,3072]{1,0:T(8,128)(2,1)}, bf16[32,3072]{1,0:T(8,128)(2,1)S(1)}, u32[]{:S(2)}, u32[]{:S(2)}) collective-permute-start(bf16[32,3072]{1,0:T(8,128)(2,1)} %get-tuple-element.292), channel_id=1, source_target_pairs={{0,4},{1,5},{2,6},{3,7},{4,0},{5,1},{6,2},{7,3},{8,12},{9,13},{10,... | collective-permute-start | bytes 589832 | tf_op jit(solution)/shard_map/ppermute | solution.py:559
  645.9 30.3 %collective-permute-start.50 = (bf16[32,3072]{1,0:T(8,128)(2,1)}, bf16[32,3072]{1,0:T(8,128)(2,1)S(1)}, u32[]{:S(2)}, u32[]{:S(2)}) collective-permute-start(bf16[32,3072]{1,0:T(8,128)(2,1)} %get-tuple-element.291), channel_id=1, source_target_pairs={{0,2},{1,3},{2,0},{3,1},{4,6},{5,7},{6,4},{7,5},{8,10},{9,11},{10,... | collective-permute-start | bytes 589832 | tf_op jit(solution)/shard_map/ppermute | solution.py:559
  676.2 25.5 %collective-permute-start.56 = (bf16[2,256,512]{2,1,0:T(8,128)(2,1)}, bf16[2,256,512]{2,1,0:T(8,128)(2,1)}, u32[]{:S(2)}, u32[]{:S(2)}) collective-permute-start(bf16[2,256,512]{2,1,0:T(8,128)(2,1)} %get-tuple-element.300), channel_id=1, source_target_pairs={{0,8},{8,0},{16,24},{24,16},{1,9},{9,1},{17,25},{25,17},{2,10},{10... | collective-permute-start | bytes 1572872 | tf_op jit(solution)/shard_map/ppermute | solution.py:559
  678.3 32.1 %collective-permute-start.58 = (bf16[2,256,512]{2,1,0:T(8,128)(2,1)}, bf16[2,256,512]{2,1,0:T(8,128)(2,1)}, u32[]{:S(2)}, u32[]{:S(2)}) collective-permute-start(bf16[2,256,512]{2,1,0:T(8,128)(2,1)} %get-tuple-element.302), channel_id=1, source_target_pairs={{0,24},{8,16},{16,8},{24,0},{1,25},{9,17},{17,9},{25,1},{2,26},{10... | collective-permute-start | bytes 1572872 | tf_op jit(solution)/shard_map/ppermute | solution.py:559
  774.2 26.9 %collective-permute-start.69 = (bf16[32,3072]{1,0:T(8,128)(2,1)}, bf16[32,3072]{1,0:T(8,128)(2,1)S(1)}, u32[]{:S(2)}, u32[]{:S(2)}) collective-permute-start(bf16[32,3072]{1,0:T(8,128)(2,1)} %get-tuple-element.337), channel_id=1, source_target_pairs={{0,4},{1,5},{2,6},{3,7},{4,0},{5,1},{6,2},{7,3},{8,12},{9,13},{10,... | collective-permute-start | bytes 589832 | tf_op jit(solution)/shard_map/ppermute | solution.py:559
  774.2 27.6 %collective-permute-start.68 = (bf16[32,3072]{1,0:T(8,128)(2,1)}, bf16[32,3072]{1,0:T(8,128)(2,1)S(1)}, u32[]{:S(2)}, u32[]{:S(2)}) collective-permute-start(bf16[32,3072]{1,0:T(8,128)(2,1)} %get-tuple-element.336), channel_id=1, source_target_pairs={{0,2},{1,3},{2,0},{3,1},{4,6},{5,7},{6,4},{7,5},{8,10},{9,11},{10,... | collective-permute-start | bytes 589832 | tf_op jit(solution)/shard_map/ppermute | solution.py:559
  777.9 35.0 %collective-permute-start.86 = (bf16[32,12288]{1,0:T(8,128)(2,1)S(1)}, bf16[32,12288]{1,0:T(8,128)(2,1)S(1)}, u32[]{:S(2)}, u32[]{:S(2)}) collective-permute-start(bf16[32,12288]{1,0:T(8,128)(2,1)S(1)} %pad_maximum_fusion.refs_0_.refs_4_), channel_id=1, source_target_pairs={{0,8},{8,0},{16,24},{24,16},{1,9},{9,1},{17,25},{25,17},{2,10},{10... | collective-permute-start | bytes 2359304 | tf_op jit(solution)/shard_map/ppermute | solution.py:559
  778.5 41.9 %collective-permute-start.87 = (bf16[32,12288]{1,0:T(8,128)(2,1)S(1)}, bf16[32,12288]{1,0:T(8,128)(2,1)S(1)}, u32[]{:S(2)}, u32[]{:S(2)}) collective-permute-start(bf16[32,12288]{1,0:T(8,128)(2,1)S(1)} %pad_maximum_fusion.refs_0_.refs_4_), channel_id=1, source_target_pairs={{0,16},{8,24},{16,0},{24,8},{1,17},{9,25},{17,1},{25,9},{2,18},{10... | collective-permute-start | bytes 2359304 | tf_op jit(solution)/shard_map/ppermute | solution.py:559
  786.1 29.3 %collective-permute-start.82 = (bf16[32,6144]{1,0:T(8,128)(2,1)}, bf16[32,6144]{1,0:T(8,128)(2,1)}, u32[]{:S(2)}, u32[]{:S(2)}) collective-permute-start(bf16[32,6144]{1,0:T(8,128)(2,1)} %get-tuple-element.348), channel_id=1, source_target_pairs={{0,24},{8,16},{16,8},{24,0},{1,25},{9,17},{17,9},{25,1},{2,26},{10... | collective-permute-start | bytes 1179656 | tf_op jit(solution)/shard_map/ppermute | solution.py:559
  813.0 31.5 %collective-permute-start.88 = (bf16[32,12288]{1,0:T(8,128)(2,1)S(1)}, bf16[32,12288]{1,0:T(8,128)(2,1)S(1)}, u32[]{:S(2)}, u32[]{:S(2)}) collective-permute-start(bf16[32,12288]{1,0:T(8,128)(2,1)S(1)} %pad_maximum_fusion.refs_0_.refs_4_), channel_id=1, source_target_pairs={{0,24},{8,16},{16,8},{24,0},{1,25},{9,17},{17,9},{25,1},{2,26},{10... | collective-permute-start | bytes 2359304 | tf_op jit(solution)/shard_map/ppermute | solution.py:559
  817.5 25.4 %collective-permute-start.71 = (bf16[32,3072]{1,0:T(8,128)(2,1)S(1)}, bf16[32,3072]{1,0:T(8,128)(2,1)S(1)}, u32[]{:S(2)}, u32[]{:S(2)}) collective-permute-start(bf16[32,3072]{1,0:T(8,128)(2,1)S(1)} %get-tuple-element.341), channel_id=1, source_target_pairs={{0,8},{8,0},{16,24},{24,16},{1,9},{9,1},{17,25},{25,17},{2,10},{10... | collective-permute-start | bytes 589832 | tf_op jit(solution)/shard_map/ppermute | solution.py:559
  820.4 30.9 %collective-permute-start.83 = (bf16[32,6144]{1,0:T(8,128)(2,1)S(1)}, bf16[32,6144]{1,0:T(8,128)(2,1)S(1)}, u32[]{:S(2)}, u32[]{:S(2)}) collective-permute-start(bf16[32,6144]{1,0:T(8,128)(2,1)S(1)} %add_convert_fusion.refs_0_), channel_id=1, source_target_pairs={{0,8},{8,0},{16,24},{24,16},{1,9},{9,1},{17,25},{25,17},{2,10},{10... | collective-permute-start | bytes 1179656 | tf_op jit(solution)/shard_map/ppermute | solution.py:559
  844.5 28.8 %collective-permute-start.78 = (bf16[32,3072]{1,0:T(8,128)(2,1)S(1)}, bf16[32,3072]{1,0:T(8,128)(2,1)S(1)}, u32[]{:S(2)}, u32[]{:S(2)}) collective-permute-start(bf16[32,3072]{1,0:T(8,128)(2,1)S(1)} %add_convert_fusion.3.refs_4_), channel_id=1, source_target_pairs={{0,16},{8,24},{16,0},{24,8},{1,17},{9,25},{17,1},{25,9},{2,18},{10... | collective-permute-start | bytes 589832 | tf_op jit(solution)/shard_map/ppermute | solution.py:559
  (135 other events, 1791.9 us)
Sparse Core Ops, SparseCore 0:
  11.5 221.3 all-gather.4
  236.3 140.0 all-gather.6
  417.2 127.3 reduce-scatter.3
  549.1 151.9 reduce-scatter.5
  728.8 82.8 reduce-scatter.7
